TPU v7x, 32 devices: a whole 2x2x4 slice. The times are simulated.
32 devices in a mesh: ctx: 8 (over z, x), head: 4 (over y, core).
Axes of the slice: x: 2, y: 2, z: 4, core: 2. Of those that a mesh axis runs over, the one named last changes fastest.
Arguments:
- queries: bfloat16 [4096, 8192], P('ctx', 'head'), may hold values from -6 to 6
- key_rows: bfloat16 [4096, 8192], P('ctx', 'head'), may hold values from -8 to 8
- value_rows: bfloat16 [4096, 8192], P('ctx', 'head'), may hold values from -6 to 6
- log_decay: float32 [4096, 64], P('ctx', 'head'), may hold values from -3 to 0, as said below
- write_rate: float32 [4096, 64], P('ctx', 'head'), may hold values from 0 to 1, as said below
- level_weights: float32 [4096, 320], P('ctx', 'head'), may hold values from 0.25 to 2.5
- block_levels: int32 [64], P('ctx'), may hold values from 1 to 5
Outputs:
- mixed: bfloat16 [4096, 8192], P(('ctx', 'head'))
Inputs may be any that keep to these rules, and one draw needn't show every extreme that they name: `log_decay`: strictly negative. `write_rate`: strictly positive.
All inputs are finite; a program needn't handle non-finite values.
Results may differ from a plain program's by a relative error of at most 0.0087.
Values may be sent and summed in bfloat16 or wider, within the bound.
No kernel may reach another device: no remote copies, remote signals or barrier semaphores. Data moves between devices by JAX's collectives and lax.ppermute only.
A program may use at most 128 MiB of HBM per device.

v0:
```python
import jax
import jax.numpy as jnp
from jax import lax
from jax.sharding import PartitionSpec as P

BLOCK = 64
LEVELS = 5


precise = lax.Precision.HIGHEST


def partner(array, axis, bit):
    return lax.ppermute(array, axis, [(i, i ^ 1 << bit) for i in range(lax.axis_size(axis))])


def matmul_hi(left_mat, right_mat):
    return jnp.matmul(left_mat, right_mat, precision=precise)


def low_product(form, left_op, right_op):
    return jnp.einsum(form, left_op, right_op, preferred_element_type=jnp.float32)


def to_blocks(tensor):
    block_count = tensor.shape[0] // BLOCK
    shaped = tensor.reshape((block_count, BLOCK) + tensor.shape[1:])
    return jnp.moveaxis(shaped, 2, 0)


def prepare(query_in, key_in, value_in, head_count):
    length = query_in.shape[0]
    query_low = query_in.reshape(length, head_count, -1)
    key_f = key_in.astype(jnp.float32).reshape(length, head_count, -1)
    key_low = (key_f * lax.rsqrt(jnp.sum(key_f * key_f, axis=-1, keepdims=True) + 1e-06)).astype(
        jnp.bfloat16
    )
    value_f = value_in.astype(jnp.float32).reshape(length, head_count, -1)
    return (query_low, key_low, value_f)


def local_pass(query_low, key_low, value_f, log_decay, write_rate):
    head_count = key_low.shape[1]
    head_width = key_low.shape[2]
    query_b = to_blocks(query_low)
    key_lb = to_blocks(key_low)
    key_b = key_lb.astype(jnp.float32)
    value_b = to_blocks(value_f)
    cum_log = jnp.cumsum(to_blocks(log_decay), axis=-1)
    rate_b = to_blocks(write_rate)
    places = jnp.arange(BLOCK)
    lower_tri = places[:, None] >= places[None, :]
    strict_tri = places[:, None] > places[None, :]
    log_gaps = cum_log[..., :, None] - cum_log[..., None, :]
    decay_incl = jnp.exp(jnp.where(lower_tri, log_gaps, -1e30))
    decay_strict = jnp.where(strict_tri, decay_incl, 0.0)
    gram_keys = jnp.einsum("hbik,hbjk->hbij", key_b, key_b, precision=precise)
    strict_part = rate_b[..., :, None] * decay_strict * gram_keys
    right_side = jnp.concatenate(
        [rate_b[..., None] * value_b, (rate_b * jnp.exp(cum_log))[..., None] * key_b], axis=-1
    )
    solved = jax.scipy.linalg.solve_triangular(
        strict_part, right_side, lower=True, unit_diagonal=True
    )
    wy_values = solved[..., :head_width]
    wy_keys = solved[..., head_width:]
    inputs = jnp.concatenate([wy_values, jnp.zeros_like(wy_keys)], axis=-1)
    key_tail = jnp.exp(cum_log[..., -1:] - cum_log)[..., None] * key_b
    block_fall = jnp.exp(cum_log[..., -1])
    scores_low = (low_product("hbik,hbjk->hbij", query_b, key_lb) * decay_incl).astype(jnp.bfloat16)
    initial = jnp.concatenate(
        [
            jnp.zeros((head_count, head_width, head_width), key_b.dtype),
            jnp.broadcast_to(
                jnp.eye(head_width, dtype=key_b.dtype), (head_count, head_width, head_width)
            ),
        ],
        axis=-1,
    )

    def advance(carry_state, slices):
        wy_part, given_vals, tail_keys, fall_now = slices
        errors = given_vals - jnp.einsum("hcd,hde->hce", wy_part, carry_state, precision=precise)
        updated = fall_now[:, None, None] * carry_state + jnp.einsum(
            "hcd,hce->hde", tail_keys, errors, precision=precise
        )
        return (updated, (carry_state, errors))

    end_state, (starts, errors) = lax.scan(
        advance,
        initial,
        (
            jnp.moveaxis(wy_keys, 1, 0),
            jnp.moveaxis(inputs, 1, 0),
            jnp.moveaxis(key_tail, 1, 0),
            jnp.moveaxis(block_fall, 1, 0),
        ),
    )
    mixed = jnp.exp(cum_log)[..., None] * low_product(
        "hbcd,bhde->hbce", query_b, starts.astype(jnp.bfloat16)
    )
    mixed = mixed + low_product("hbij,bhje->hbie", scores_low, errors.astype(jnp.bfloat16))
    mixed = jnp.moveaxis(mixed, 0, 2).reshape(-1, head_count, 2 * head_width)
    return (mixed, end_state)


def join_runs(left_run, right_run):
    head_width = left_run.shape[-2]
    return matmul_hi(right_run[..., head_width:], left_run) + jnp.concatenate(
        [right_run[..., :head_width], jnp.zeros_like(right_run[..., :head_width])], axis=-1
    )


def finish(mixed, carried, weights, levels_in):
    length, head_count, twice = mixed.shape
    head_width = twice // 2
    near_part = mixed[..., :head_width]
    row_part = mixed[..., head_width:].astype(jnp.bfloat16)
    far_part = low_product("thd,lhde->thle", row_part, carried.astype(jnp.bfloat16))
    terms = jnp.concatenate([near_part[:, :, None], far_part], axis=2)
    level_ids = jnp.arange(LEVELS)
    keep_mask = (level_ids[None, :] < levels_in[:, None]).astype(weights.dtype)
    scaled = (
        weights.reshape(length // BLOCK, BLOCK, head_count, LEVELS) * keep_mask[:, None, None, :]
    )
    scaled = scaled.reshape(length, head_count, LEVELS)
    total = jnp.sum(scaled[..., None] * terms, axis=2)
    return total.astype(jnp.bfloat16).reshape(length, head_count * head_width)


def per_device(queries, key_rows, value_rows, log_decay, write_rate, level_weights, block_levels):
    head_count = log_decay.shape[1]
    query_low, key_low, value_f = prepare(queries, key_rows, value_rows, head_count)
    mixed, own_run = local_pass(query_low, key_low, value_f, log_decay, write_rate)
    head_width = key_low.shape[2]
    bits_total = lax.axis_size("ctx").bit_length() - 1
    position = lax.axis_index("ctx")
    prefix = jnp.broadcast_to(
        jnp.eye(head_width, dtype=own_run.dtype), (head_count, head_width, head_width)
    )
    carried = []
    for section in range(bits_total):
        upper = position >> section & 1 == 1
        other_run = partner(own_run, "ctx", section)
        carried.append(jnp.where(upper, matmul_hi(prefix, other_run[..., :head_width]), 0.0))
        prefix = jnp.where(upper, matmul_hi(prefix, other_run[..., head_width:]), prefix)
        if section + 1 < bits_total:
            left_run = jnp.where(upper, other_run, own_run)
            right_run = jnp.where(upper, own_run, other_run)
            own_run = join_runs(left_run, right_run)
    for section in range(bits_total, LEVELS - 1):
        carried.append(jnp.zeros_like(prefix))
    stacked = jnp.stack(carried, axis=0)
    outputs = finish(mixed, stacked, level_weights, block_levels)
    return lax.all_to_all(outputs, "head", split_axis=0, concat_axis=1, tiled=True)


def solution(mesh):
    in_specs = (
        P("ctx", "head"),
        P("ctx", "head"),
        P("ctx", "head"),
        P("ctx", "head"),
        P("ctx", "head"),
        P("ctx", "head"),
        P("ctx"),
    )
    out_specs = P(("ctx", "head"), None)
    return jax.shard_map(
        per_device, mesh=mesh, in_specs=in_specs, out_specs=out_specs, check_vma=False
    )
```

profile of v0, /device:TPU:24, one launch (start us, length us, event | category | flops | bytes accessed | tf_op | source)
XLA Modules:
  0.0 1005.9 jit_solution(16081232928709878852)
XLA Ops:
  0.0 4.3 fusion.14
  4.3 2.5 convert_bitcast_fusion
  6.9 3.5 reduce_window_sum.13
  10.9 5.0 copy.78
  15.9 3.4 reduce_sum.18
  19.5 3.1 copy.77
  22.7 3.9 convert_multiply_fusion.1
  26.6 3.9 add_bitcast_fusion
  30.5 630.6 %custom-call.4 = f32[16,8,1,64,64]{3,4,2,1,0:T(8,128)} custom-call(f32[16,8,1,64,64]{4,3,2,1,0:T(8,128)} %add_bitcast_fusion), custom_call_target="InvertDiagBlocksLowerTriangular" | custom-call | tf_op jit(solution)/shard_map/jit(_solve_triangular)/vmap(vmap())/triangular_solve | solution.py:62
  665.7 11.1 %fusion.8 = f32[16,8,64,256]{3,2,1,0:T(8,128)S(1)} fusion(f32[16,8,64,128]{3,2,1,0:T(8,128)} %get-tuple-element.100, f32[16,8,64,128]{3,2,1,0:T(8,128)S(1)} %bitcast_multiply_fusion.2, f32[16,8,1,64,64]{3,4,2,1,0:T(8,128)} %custom-call.4), kind=kOutput, calls=%fused_computation.15 | convolution fusion | flops 1612709888 | bytes 18874368 | tf_op jit(solution)/shard_map/jit(_solve_triangular)/vmap(vmap())/triangular_solve | solution.py:62
  676.9 2.4 slice_bitcast_fusion.1
  679.3 4.2 select_bitcast_fusion
  683.6 2.6 bitcast_multiply_fusion.3
  686.5 65.8 %while.14 = (s32[]{:T(128)}, f32[16,128,256]{2,1,0:T(8,128)S(1)}, bf16[8,16,128,256]{3,2,1,0:T(8,128)(2,1)}, bf16[8,16,64,256]{3,2,1,0:T(8,128)(2,1)}, f32[8,16]...) while((s32[]{:T(128)}, f32[16,128,256]{2,1,0:T(8,128)S(1)}, ...), condition=%wide.region_3.4_spmd, body=%wide.region_2.3_spmd.sunk | while | flops 806617088 | bytes 15730977 | solution.py:89
  686.5 3.6 bitcast_dynamic-update-slice_fusion.4
  691.3 3.5 multiply_add_fusion.2
  694.8 3.6 bitcast_dynamic-update-slice_fusion.4
  699.5 3.5 multiply_add_fusion.2
  703.0 3.5 bitcast_dynamic-update-slice_fusion.4
  707.6 3.5 multiply_add_fusion.2
  711.2 3.5 bitcast_dynamic-update-slice_fusion.4
  715.8 3.5 multiply_add_fusion.2
  719.3 3.5 bitcast_dynamic-update-slice_fusion.4
  724.0 3.5 multiply_add_fusion.2
  727.6 3.5 bitcast_dynamic-update-slice_fusion.4
  732.2 3.5 multiply_add_fusion.2
  735.8 3.5 bitcast_dynamic-update-slice_fusion.4
  740.4 3.5 multiply_add_fusion.2
  743.9 3.5 bitcast_dynamic-update-slice_fusion.4
  748.6 3.5 multiply_add_fusion.2
  753.9 46.0 %collective-permute-done = f32[16,128,256]{2,1,0:T(8,128)} collective-permute-done((f32[16,128,256]{2,1,0:T(8,128)S(1)}, f32[16,128,256]{2,1,0:T(8,128)}, u32[]{:S(2)}, u32[]{:S(2)}) %collective-permute-start) | collective-permute-done | bytes 2097184 | tf_op jit(solution)/shard_map/ppermute | solution.py:14
  801.7 3.5 select_add_fusion.1
  807.9 8.1 fusion.12
  815.9 36.1 %collective-permute-done.1 = f32[16,128,256]{2,1,0:T(8,128)} collective-permute-done((f32[16,128,256]{2,1,0:T(8,128)}, f32[16,128,256]{2,1,0:T(8,128)}, u32[]{:S(2)}, u32[]{:S(2)}) %collective-permute-start.1) | collective-permute-done | bytes 2097184 | tf_op jit(solution)/shard_map/ppermute | solution.py:14
  853.9 5.0 select_add_fusion
  859.3 8.6 bitcast_add_fusion
  867.9 4.5 slice_bitcast_fusion
  872.4 5.6 copy.62
  882.9 2.4 fusion.47
  885.3 2.4 convolution_select_fusion
  887.7 62.9 %collective-permute-done.2 = f32[16,128,256]{2,1,0:T(8,128)} collective-permute-done((f32[16,128,256]{2,1,0:T(8,128)}, f32[16,128,256]{2,1,0:T(8,128)}, u32[]{:S(2)}, u32[]{:S(2)}) %collective-permute-start.2) | collective-permute-done | bytes 2097184 | tf_op jit(solution)/shard_map/ppermute | solution.py:14
  950.5 2.4 fusion.46
  952.9 4.6 convolution_bitcast_fusion
  957.6 8.1 fusion.7
  967.6 3.0 copy.72
  970.6 28.9 %all_to_all.16 = bf16[4,128,2048]{2,1,0:T(8,128)(2,1)} all-to-all(bf16[4,128,2048]{2,1,0:T(8,128)(2,1)S(1)} %copy.72), channel_id=1, replica_groups=mesh['ctx'=8,'head'=4] {'head'}, dimensions={0} | all-to-all | bytes 4194304 | tf_op jit(solution)/shard_map/all_to_all | solution.py:155
  999.6 3.0 copy.64
  1002.6 2.9 copy.65
  (68 shorter events, 29.9 us)
Async XLA Ops:
  0.0 4.3 copy-start.2
  4.3 2.5 copy-start.4
  4.3 6.5 copy-start.5
  26.6 657.0 %copy-start = (bf16[8,64,16,128]{3,1,0,2:T(8,128)(2,1)}, bf16[8,64,16,128]{3,1,0,2:T(8,128)(2,1)S(1)}, u32[]{:S(2)}) copy-start(bf16[8,64,16,128]{3,1,0,2:T(8,128)(2,1)S(1)} %get-tuple-element.101) | copy-start | bytes 6291460
  676.8 2.4 copy-start.6
  752.3 47.5 %collective-permute-start = (f32[16,128,256]{2,1,0:T(8,128)S(1)}, f32[16,128,256]{2,1,0:T(8,128)}, u32[]{:S(2)}, u32[]{:S(2)}) collective-permute-start(f32[16,128,256]{2,1,0:T(8,128)S(1)} %get-tuple-element.51), channel_id=1, source_target_pairs={{0,4},{4,0},{8,12},{12,8},{16,20},{20,16},{24,28},{28,24},{1,5},{5... | collective-permute-start | bytes 6291464 | tf_op jit(solution)/shard_map/ppermute | solution.py:14
  805.2 46.8 %collective-permute-start.1 = (f32[16,128,256]{2,1,0:T(8,128)}, f32[16,128,256]{2,1,0:T(8,128)}, u32[]{:S(2)}, u32[]{:S(2)}) collective-permute-start(f32[16,128,256]{2,1,0:T(8,128)} %select_add_fusion.1), channel_id=1, source_target_pairs={{0,8},{4,12},{8,0},{12,4},{16,24},{20,28},{24,16},{28,20},{1,9},{5... | collective-permute-start | bytes 6291464 | tf_op jit(solution)/shard_map/ppermute | solution.py:14
  858.9 91.6 %collective-permute-start.2 = (f32[16,128,256]{2,1,0:T(8,128)}, f32[16,128,256]{2,1,0:T(8,128)}, u32[]{:S(2)}, u32[]{:S(2)}) collective-permute-start(f32[16,128,256]{2,1,0:T(8,128)} %select_add_fusion), channel_id=1, source_target_pairs={{0,16},{4,20},{8,24},{12,28},{16,0},{20,4},{24,8},{28,12},{1,17},{... | collective-permute-start | bytes 6291464 | tf_op jit(solution)/shard_map/ppermute | solution.py:14
  872.4 5.6 copy-start.3
  872.4 5.7 copy-start.7
  952.9 4.6 copy-start.1
where the time goes:
time: 1020 us; the launch traced here: 1010 us
  other arithmetic  671 us (66%)
  waiting for transfers between devices  145 us (14%)
  matrix products  113 us (11%)
  local copies, waits for them, and re-layouts  45 us (4%)
  blocking collectives  28.9 us (3%)
    another operation x3, other arithmetic, local_pass(): jax.scipy.linalg.solve_triangular(strict_part, right_side, lower=True, un...  631 us
    ppermute x3, waiting for transfers between devices, partner(): lax.ppermute(array, axis, [(i, i ^ 1 << bit) for i in range(lax.axis_size...  145 us
    all_to_all x1, blocking collectives, per_device(): lax.all_to_all(outputs, 'head', split_axis=0, concat_axis=1, tiled=True)  28.9 us
    dot_general x8, matrix products, advance(): jnp.einsum('hcd,hde->hce', wy_part, carry_state, precision=precise)  28.3 us
    dot_general x8, matrix products, advance(): jnp.einsum('hcd,hce->hde', tail_keys, errors, precision=precise)  28.1 us
    dot_general x3, matrix products, low_product(): jnp.einsum(form, left_op, right_op, preferred_element_type=jnp.float32)  21.3 us
  transfers between devices with their start and end apart: 3, of which 3 were waited for; matrix products, arithmetic and copies ran while one was open for 4% of the time, Pallas kernels for 0%

commit v1 on v0

v1 whole, which is shorter than its diff:
```python
import jax
import jax.numpy as jnp
from jax import lax
from jax.sharding import PartitionSpec as P
from jax.experimental import pallas as pl
from jax.experimental.pallas import tpu as pltpu

BLOCK = 64
WIDE = 128
LEVELS = 5
f32 = jnp.float32
bf16 = jnp.bfloat16


def mxu(a, b):
    return lax.dot_general(a, b, (((1,), (0,)), ((), ())), preferred_element_type=f32)


def mxu_t(a, b):
    return lax.dot_general(a, b, (((1,), (1,)), ((), ())), preferred_element_type=f32)


def halves(x):
    hi = x.astype(bf16)
    return hi, (x - hi.astype(f32)).astype(bf16)


def local_kernel(
    q_ref, k_ref, v_ref, ld_ref, wr_ref,
    run_ref, near_ref, rows_ref,
    kn_s, gram_s, low_s, inv_s, row_s, colg_s, colb_s, m_s, s_s, qt_s, near_s, p_s,
):
    heads = k_ref.shape[1] // WIDE
    tokens = k_ref.shape[0]
    pairs = tokens // WIDE
    units = heads * pairs
    blocks = tokens // BLOCK

    lane = lax.broadcasted_iota(jnp.int32, (BLOCK, WIDE), 1)
    left = lane < BLOCK
    ri = lax.broadcasted_iota(jnp.int32, (WIDE, WIDE), 0)
    ci = lax.broadcasted_iota(jnp.int32, (WIDE, WIDE), 1)
    tri = jnp.where((ri <= ci) & ((ri >= BLOCK) == (ci >= BLOCK)), 1.0, 0.0)
    grow = lax.dot_general(
        ld_ref[...], tri, (((1,), (0,)), ((), ())),
        precision=lax.Precision.HIGHEST, preferred_element_type=f32,
    )
    row_s[0] = grow
    row_s[1] = jnp.exp(grow)
    gcol = grow.T
    bcol = wr_ref[...].T
    colg_s[...] = jnp.concatenate([gcol[:BLOCK], gcol[BLOCK:]], axis=1)
    colb_s[...] = jnp.concatenate([bcol[:BLOCK], bcol[BLOCK:]], axis=1)

    def keys(h, _):
        cols = pl.ds(pl.multiple_of(h * WIDE, WIDE), WIDE)
        kf = k_ref[:, cols].astype(f32)
        kn = (kf * lax.rsqrt(jnp.sum(kf * kf, axis=1, keepdims=True) + 1e-6)).astype(bf16)
        kn_s[h] = kn
        for p in range(pairs):
            kp = kn[p * WIDE:(p + 1) * WIDE]
            g = mxu_t(kp, kp)
            u = h * pairs + p
            gram_s[pl.ds(pl.multiple_of(u * BLOCK, BLOCK), BLOCK), :] = jnp.where(
                left, g[:BLOCK], g[BLOCK:]
            )
        return 0

    lax.fori_loop(0, heads, keys, 0)

    def to_lanes(i, _):
        a = gram_s[pl.ds(i, units, stride=BLOCK), :].T
        g = jnp.concatenate([a[:BLOCK], a[BLOCK:]], axis=1)
        gi = colg_s[pl.ds(i, 1), :]
        bi = colb_s[pl.ds(i, 1), :]
        low_s[i] = g * (bi * jnp.exp(gi - colg_s[...]))
        inv_s[i] = jnp.zeros_like(g)
        return 0

    lax.fori_loop(0, BLOCK, to_lanes, 0)

    lanes = 2 * units
    sub = lax.broadcasted_iota(jnp.int32, (8, lanes), 0)

    def solve(bi, _):
        i0 = bi * 8

        def column(cb, _):
            c0 = pl.multiple_of(cb * 8, 8)

            def step(jb, acc):
                acc = list(acc)
                for jj in range(8):
                    j = jb * 8 + jj
                    t = inv_s[j, pl.ds(c0, 8), :]
                    for r in range(8):
                        acc[r] = acc[r] - low_s[i0 + r, pl.ds(j, 1), :] * t
                return tuple(acc)

            on = cb == bi
            acc = tuple(jnp.where((sub == r) & on, 1.0, 0.0) for r in range(8))
            acc = list(lax.fori_loop(cb, bi, step, acc))
            for r in range(8):
                inv_s[i0 + r, pl.ds(c0, 8), :] = acc[r]
                for s in range(r + 1, 8):
                    acc[s] = acc[s] - low_s[i0 + s, pl.ds(i0 + r, 1), :] * acc[r]
            return 0

        lax.fori_loop(0, bi + 1, column, 0)
        return 0

    lax.fori_loop(0, BLOCK // 8, solve, 0)

    def from_lanes(i, _):
        t = inv_s[i] * colb_s[...]
        a = jnp.concatenate([t[:, :units], t[:, units:]], axis=0)
        gram_s[pl.ds(i, units, stride=BLOCK), :] = a.T
        return 0

    lax.fori_loop(0, BLOCK, from_lanes, 0)

    clane = lax.broadcasted_iota(jnp.int32, (BLOCK, lanes), 1)
    row64 = lax.broadcasted_iota(jnp.int32, (BLOCK, WIDE), 0)
    keep = row64 >= jnp.where(left, lane, lane - BLOCK)
    eye = ri == ci

    def unit(u, _):
        h = u // pairs
        p = u - h * pairs
        cols = pl.ds(pl.multiple_of(h * WIDE, WIDE), WIDE)
        toks = pl.ds(pl.multiple_of(p * WIDE, WIDE), WIDE)
        grow = row_s[0, pl.ds(u, 1), :]
        erow = row_s[1, pl.ds(u, 1), :]
        g0 = jnp.sum(jnp.where(clane == u, colg_s[...], 0.0), axis=1, keepdims=True)
        g1 = jnp.sum(jnp.where(clane == u + units, colg_s[...], 0.0), axis=1, keepdims=True)
        g0 = jnp.broadcast_to(g0, (BLOCK, WIDE))
        g1 = jnp.broadcast_to(g1, (BLOCK, WIDE))
        q = q_ref[toks, cols]
        kn = kn_s[h, toks, :]
        v = v_ref[toks, cols]
        qk = mxu_t(q, kn)
        decay = jnp.exp(jnp.where(keep, jnp.where(left, g0, g1) - grow, -1e30))
        score = jnp.where(left, qk[:BLOCK], qk[BLOCK:]) * decay
        zero = jnp.zeros_like(score)

        def diagonal(x):
            return jnp.concatenate([jnp.where(left, x, zero), jnp.where(left, zero, x)], axis=0)

        t1 = gram_s[pl.ds(pl.multiple_of(u * BLOCK, BLOCK), BLOCK), :]
        t2 = t1 * erow
        a_hi, a_lo = halves(diagonal(t1))
        b_hi, b_lo = halves(diagonal(t2))
        wv = mxu(jnp.concatenate([a_hi, a_lo], axis=1), jnp.concatenate([v, v], axis=0))
        wk = mxu(jnp.concatenate([b_hi, b_lo], axis=1), jnp.concatenate([kn, kn], axis=0))
        w = jnp.concatenate([wv, wk], axis=1)
        ys = mxu(diagonal(score).astype(bf16), w.astype(bf16))
        near_s[u] = ys[:, :WIDE]
        eg = jnp.exp(jnp.concatenate([g0, g1], axis=0))
        qt_s[u] = (eg * q.astype(f32) - ys[:, WIDE:]).astype(bf16)
        knt = kn.astype(f32).T.astype(bf16)
        kk = jnp.concatenate([knt, knt], axis=1)
        for half, g in enumerate((g0, g1)):
            end = g[BLOCK - 1:, :]
            tail = jnp.exp(end - g)
            part = w[half * BLOCK:(half + 1) * BLOCK] * jnp.concatenate([tail, tail], axis=1)
            hi, lo = halves(part)
            none = jnp.zeros_like(hi)
            stack = [hi, none, lo, none] if half == 0 else [none, hi, none, lo]
            y = mxu(kk, jnp.concatenate(stack, axis=0))
            s_s[2 * u + half] = y[:, :WIDE]
            m = jnp.where(eye, jnp.exp(end), 0.0) - y[:, WIDE:]
            m_hi, m_lo = halves(m)
            m_s[2 * u + half] = jnp.concatenate([m_hi, m_lo], axis=1)
        return 0

    lax.fori_loop(0, units, unit, 0)

    start = jnp.where(eye, 1.0, 0.0)
    for h in range(heads):
        p_s[h] = jnp.concatenate([jnp.zeros_like(start), start], axis=1)

    def scan(b, _):
        toks = pl.ds(pl.multiple_of(b * BLOCK, BLOCK), BLOCK)
        half = pl.ds(pl.multiple_of((b % 2) * BLOCK, BLOCK), BLOCK)
        for h in range(heads):
            u = h * pairs + b // 2
            at = h * blocks + b
            cols = pl.ds(h * WIDE, WIDE)
            p = p_s[h]
            p_hi, p_lo = halves(p)
            o = mxu(qt_s[u, half, :], p_hi)
            near_ref[toks, cols] = near_s[u, half, :] + o[:, :WIDE]
            rows_ref[toks, cols] = o[:, WIDE:].astype(bf16)
            m = m_s[at]
            n = mxu(
                jnp.concatenate([m, m[:, :WIDE]], axis=1),
                jnp.concatenate([p_hi, p_hi, p_lo], axis=0),
            )
            p_s[h] = n + jnp.concatenate([s_s[at], jnp.zeros_like(start)], axis=1)
        return 0

    lax.fori_loop(0, blocks, scan, 0)
    for h in range(heads):
        run_ref[h] = p_s[h].astype(bf16)


def local_call(q, k, v, ldt, wrt, group, heads):
    tokens = q.shape[0]
    units = heads * tokens // WIDE
    big = lambda: pl.BlockSpec((tokens, heads * WIDE), lambda i: (0, group))
    small = lambda: pl.BlockSpec((units, WIDE), lambda i: (group, 0))
    return pl.pallas_call(
        local_kernel,
        grid=(1,),
        in_specs=[big(), big(), big(), small(), small()],
        out_specs=[
            pl.BlockSpec((heads, WIDE, 2 * WIDE), lambda i: (0, 0, 0)),
            pl.BlockSpec((tokens, heads * WIDE), lambda i: (0, 0)),
            pl.BlockSpec((tokens, heads * WIDE), lambda i: (0, 0)),
        ],
        out_shape=[
            jax.ShapeDtypeStruct((heads, WIDE, 2 * WIDE), bf16),
            jax.ShapeDtypeStruct((tokens, heads * WIDE), f32),
            jax.ShapeDtypeStruct((tokens, heads * WIDE), bf16),
        ],
        scratch_shapes=[
            pltpu.VMEM((heads, tokens, WIDE), bf16),
            pltpu.VMEM((units * BLOCK, WIDE), f32),
            pltpu.VMEM((BLOCK, BLOCK, 2 * units), f32),
            pltpu.VMEM((BLOCK, BLOCK, 2 * units), f32),
            pltpu.VMEM((2, units, WIDE), f32),
            pltpu.VMEM((BLOCK, 2 * units), f32),
            pltpu.VMEM((BLOCK, 2 * units), f32),
            pltpu.VMEM((2 * units, WIDE, 2 * WIDE), bf16),
            pltpu.VMEM((2 * units, WIDE, WIDE), f32),
            pltpu.VMEM((units, WIDE, WIDE), bf16),
            pltpu.VMEM((units, WIDE, WIDE), f32),
            pltpu.VMEM((heads, WIDE, 2 * WIDE), f32),
        ],
        compiler_params=pltpu.CompilerParams(vmem_limit_bytes=60 * 1024 * 1024),
        name="local",
    )(q, k, v, ldt, wrt)


def rows_of(x):
    return x.T.reshape(-1, WIDE)


def stage_kernel(flag_ref, own_ref, other_ref, prefix_ref, run_ref, carry_ref, next_ref):
    heads = own_ref.shape[0]

    @pl.when(flag_ref[0] == 1)
    def _():
        for h in range(heads):
            own = own_ref[h]
            other = other_ref[h]
            both = mxu(jnp.concatenate([own[:, WIDE:], prefix_ref[h]], axis=0), other)
            run_ref[h, :, :WIDE] = (both[:WIDE, :WIDE] + own[:, :WIDE].astype(f32)).astype(bf16)
            run_ref[h, :, WIDE:] = both[:WIDE, WIDE:].astype(bf16)
            carry_ref[h] = both[WIDE:, :WIDE].astype(bf16)
            next_ref[h] = both[WIDE:, WIDE:].astype(bf16)

    @pl.when(flag_ref[0] == 0)
    def _():
        for h in range(heads):
            own = own_ref[h]
            other = other_ref[h]
            both = mxu(other[:, WIDE:], own)
            run_ref[h, :, :WIDE] = (both[:, :WIDE] + other[:, :WIDE].astype(f32)).astype(bf16)
            run_ref[h, :, WIDE:] = both[:, WIDE:].astype(bf16)
            carry_ref[h] = jnp.zeros((WIDE, WIDE), bf16)
            next_ref[h] = prefix_ref[h]


def stage_call(flag, own, other, prefix):
    heads = own.shape[0]
    square = jax.ShapeDtypeStruct((heads, WIDE, WIDE), bf16)
    vmem = pl.BlockSpec(memory_space=pltpu.VMEM)
    return pl.pallas_call(
        stage_kernel,
        in_specs=[pl.BlockSpec(memory_space=pltpu.SMEM), vmem, vmem, vmem],
        out_specs=[vmem, vmem, vmem],
        out_shape=[jax.ShapeDtypeStruct(own.shape, bf16), square, square],
        compiler_params=pltpu.CompilerParams(vmem_limit_bytes=40 * 1024 * 1024),
        name="stage",
    )(flag, own, other, prefix)


def finish_kernel(levels_ref, near_ref, rows_ref, weight_ref, *rest):
    *carry_refs, last_ref, prefix_ref, out_ref, weight_s = rest
    tokens = near_ref.shape[0]
    heads = near_ref.shape[1] // WIDE
    level = lax.rem(lax.broadcasted_iota(jnp.int32, (BLOCK, heads * LEVELS), 1), LEVELS)
    for b in range(tokens // BLOCK):
        part = slice(b * BLOCK, (b + 1) * BLOCK)
        weight_s[part, :] = jnp.where(level < levels_ref[b], weight_ref[part, :], 0.0)
    for h in range(heads):
        cols = slice(h * WIDE, (h + 1) * WIDE)
        parts = [ref[h] for ref in carry_refs]
        parts.append(mxu(prefix_ref[h], last_ref[h]).astype(bf16))
        far = mxu(rows_ref[:, cols], jnp.concatenate(parts, axis=1))
        total = near_ref[:, cols] * weight_s[:, h * LEVELS:h * LEVELS + 1]
        for i in range(len(parts)):
            at = h * LEVELS + 1 + i
            total = total + far[:, i * WIDE:(i + 1) * WIDE] * weight_s[:, at:at + 1]
        out_ref[:, cols] = total.astype(bf16)


def finish_call(levels, near, rows, weights, carries, last, prefix):
    vmem = pl.BlockSpec(memory_space=pltpu.VMEM)
    count = 3 + len(carries) + 2
    return pl.pallas_call(
        finish_kernel,
        in_specs=[pl.BlockSpec(memory_space=pltpu.SMEM)] + [vmem] * count,
        out_specs=vmem,
        out_shape=jax.ShapeDtypeStruct(near.shape, bf16),
        scratch_shapes=[pltpu.VMEM(weights.shape, f32)],
        compiler_params=pltpu.CompilerParams(vmem_limit_bytes=40 * 1024 * 1024),
        name="finish",
    )(levels, near, rows, weights, *carries, last, prefix)


def per_device(queries, key_rows, value_rows, log_decay, write_rate, level_weights, block_levels):
    heads = log_decay.shape[1]
    size = lax.axis_size("ctx")
    bits = size.bit_length() - 1
    position = lax.axis_index("ctx")
    run, near, rows = local_call(
        queries, key_rows, value_rows, rows_of(log_decay), rows_of(write_rate), 0, heads
    )
    prefix = jnp.broadcast_to(jnp.eye(WIDE, dtype=bf16), (heads, WIDE, WIDE))
    carries = []
    for bit in range(bits - 1):
        other = lax.ppermute(run, "ctx", [(i, i ^ 1 << bit) for i in range(size)])
        flag = (position >> bit & 1).astype(jnp.int32).reshape(1)
        run, carry, prefix = stage_call(flag, run, other, prefix)
        carries.append(carry)
    half = 1 << bits - 1
    last = lax.ppermute(run[..., :WIDE], "ctx", [(i, i + half) for i in range(half)])
    out = finish_call(block_levels, near, rows, level_weights, carries, last, prefix)
    return lax.all_to_all(out, "head", split_axis=0, concat_axis=1, tiled=True)


def solution(mesh):
    wide = P("ctx", "head")
    return jax.shard_map(
        per_device,
        mesh=mesh,
        in_specs=(wide, wide, wide, wide, wide, wide, P("ctx")),
        out_specs=P(("ctx", "head"), None),
        check_vma=False,
    )
```

time: 1020 us -> 196 us (0.19); the launches traced: 1010 us -> 195 us
  other arithmetic: 671 us -> 0.01 us
  matrix products: 113 us -> 0 us
  Pallas kernels: 0 us -> 76.9 us
  waiting for transfers between devices: 145 us -> 71.6 us
  local copies, waits for them, and re-layouts: 45 us -> 14.8 us
    another operation x4 -> x0, other arithmetic: 634 us -> none  [the longest x3 631 us: local_pass(): jax.scipy.linalg.solve_triangular(strict_part, right_side, lower=True, un...]
    dot_general x27 -> x0, matrix products: 102 us -> none  [the longest x8 28.3 us: advance(): jnp.einsum('hcd,hde->hce', wy_part, carry_state, precision=precise)]
    pallas_call x0 -> x4, Pallas kernels: none -> 76.9 us  [the longest x1 69.4 us: local_call(): pl.pallas_call(local_kernel, grid=(1,), in_specs=[big(), big(), big(), sm...]
    ppermute x3, waiting for transfers between devices: 145 us -> 71.6 us  [the longest x2 47.3 us: per_device(): other = lax.ppermute(run, 'ctx', [(i, i ^ 1 << bit) for i in range(size)])]
    reduce_sum x2 -> x0, other arithmetic: 11.4 us -> none  [the longest x1 8.06 us: finish(): total = jnp.sum(scaled[..., None] * terms, axis=2)]
    another operation x1 -> x0, matrix products: 11.1 us -> none  [local_pass(): jax.scipy.linalg.solve_triangular(strict_part, right_side, lower=True, un...]
  transfers between devices with their start and end apart: 3 -> 3, of which waited for: 3 -> 3; matrix products, arithmetic and copies ran while one was open for 4% -> 0% of each run, Pallas kernels for 0% -> 0%
where the time goes in v1:
time: 196 us; the launch traced here: 195 us
  Pallas kernels  76.9 us (39%)
  waiting for transfers between devices  71.6 us (37%)
  blocking collectives  28.3 us (14%)
  local copies, waits for them, and re-layouts  14.8 us (8%)
  starting transfers between devices  3.22 us (2%)
    pallas_call x1, Pallas kernels, local_call(): pl.pallas_call(local_kernel, grid=(1,), in_specs=[big(), big(), big(), sm...  69.4 us
    ppermute x2, waiting for transfers between devices, per_device(): other = lax.ppermute(run, 'ctx', [(i, i ^ 1 << bit) for i in range(size)])  47.3 us
    all_to_all x1, blocking collectives, per_device(): return lax.all_to_all(out, 'head', split_axis=0, concat_axis=1, tiled=True)  28.3 us
    ppermute x1, waiting for transfers between devices, per_device(): lax.ppermute(run[..., :WIDE], 'ctx', [(i, i + half) for i in range(half)])  24.3 us
    unnamed x27, local copies, waits for them, and re-layouts  9.44 us
    pallas_call x1, Pallas kernels, finish_call(): pl.pallas_call(finish_kernel, in_specs=[pl.BlockSpec(memory_space=pltpu.S...  5.13 us
  transfers between devices with their start and end apart: 3, of which 3 were waited for; matrix products, arithmetic and copies ran while one was open for 0% of the time, Pallas kernels for 0%

profile of v1, /device:TPU:24, one launch (start us, length us, event | category | flops | bytes accessed | tf_op | source)
XLA Modules:
  0.0 194.9 jit_solution(8216024013034996867)
XLA Ops:
  0.0 1.4 reshape.15.ld_ref
  1.4 1.4 reshape.16.wr_ref
  2.8 69.4 %local.1 = (bf16[16,128,256]{2,1,0:T(8,128)(2,1)}, f32[512,2048]{1,0:T(8,128)}, bf16[512,2048]{1,0:T(8,128)(2,1)}) custom-call(bf16[512,2048]{1,0:T(8,128)(2,1)} %q_ref.1, bf16[512,2048]{1,0:T(8,128)(2,1)} %k_ref.1, bf16[512,2048]{1,0:T(8,128)(2,1)} %v_ref.1, f32[64,128]{1,0:T(8,128)} %reshape.15.ld_ref, f32[64,128]{1,0:T(8,128)} %reshape.16.wr_ref), custom_call_target="tpu_custom_call" | custom-call | tf_op jit(solution)/shard_map/local/pallas_call | solution.py:212
  72.1 1.5 collective-permute-start
  73.6 23.6 %collective-permute-done.other_ref = bf16[16,128,256]{2,1,0:T(8,128)(2,1)S(1)} collective-permute-done((bf16[16,128,256]{2,1,0:T(8,128)(2,1)}, bf16[16,128,256]{2,1,0:T(8,128)(2,1)S(1)}, u32[]{:S(2)}, u32[]{:S(2)}) %collective-permute-start) | collective-permute-done | bytes 1048608 | tf_op jit(solution)/shard_map/ppermute | solution.py:334
  97.2 0.1 broadcast_in_dim.3.prefix_ref
  97.3 0.0 copy-start.2
  97.4 1.2 copy-done.2
  98.6 0.0 copy-start.12
  98.6 0.0 copy-start.11
  98.6 0.5 stage.2
  99.1 0.0 copy-start.3
  99.1 0.8 copy-done.3
  99.9 0.0 copy-start.5
  99.9 0.8 copy-done.5
  100.7 0.0 copy-start.1
  100.7 0.4 collective-permute-start.1
  101.2 23.7 %collective-permute-done.1.other_ref = bf16[16,128,256]{2,1,0:T(8,128)(2,1)} collective-permute-done((bf16[16,128,256]{2,1,0:T(8,128)(2,1)S(1)}, bf16[16,128,256]{2,1,0:T(8,128)(2,1)}, u32[]{:S(2)}, u32[]{:S(2)}) %collective-permute-start.1) | collective-permute-done | bytes 1048608 | tf_op jit(solution)/shard_map/ppermute | solution.py:334
  124.8 0.0 copy-start.4
  124.8 1.0 copy-done.4
  125.9 1.9 stage.3
  127.8 0.0 copy-start.7
  127.8 0.0 copy-start.9
  127.8 1.0 slice.3
  128.8 0.0 copy-done.7
  128.8 0.1 copy-done.9
  128.9 1.3 collective-permute-start.2
  130.2 0.0 copy-done.12
  130.2 0.1 copy.8.weight_ref
  130.4 24.3 %collective-permute-done.2.rest_2_ = bf16[16,128,128]{2,1,0:T(8,128)(2,1)S(1)} collective-permute-done((bf16[16,128,128]{2,1,0:T(8,128)(2,1)}, bf16[16,128,128]{2,1,0:T(8,128)(2,1)S(1)}, u32[]{:S(2)}, u32[]{:S(2)}) %collective-permute-start.2) | collective-permute-done | bytes 524320 | tf_op jit(solution)/shard_map/ppermute | solution.py:339
  154.7 0.0 copy-done.11
  154.7 0.0 copy-done.1
  154.7 0.0 copy-start
  154.7 2.2 %copy-done = f32[512,2048]{1,0:T(8,128)S(1)} copy-done((f32[512,2048]{1,0:T(8,128)S(1)}, f32[512,2048]{1,0:T(8,128)}, u32[]{:S(2)}) %copy-start) | copy-done | bytes 4194328
  156.9 0.0 copy-start.6
  156.9 1.0 copy-done.6
  157.9 0.0 copy-start.8
  157.9 1.0 copy-done.8
  159.0 0.0 copy-start.10
  159.0 1.0 copy-done.10
  160.0 5.1 %finish.1 = bf16[512,2048]{1,0:T(8,128)(2,1)S(1)} custom-call(s32[8]{0:T(128)S(1)} %copy-done.11, f32[512,2048]{1,0:T(8,128)S(1)} %copy-done, bf16[512,2048]{1,0:T(8,128)(2,1)S(1)} %copy-done.1, f32[512,80]{1,0:T(8,128)S(1)} %copy.8.weight_ref, bf16[16,128,128]{2,1,0:T(8,128)(2,1)S(1)} %copy-done.6, bf16[16,128,128]{2,1,0:T(8,128)(2,1)S(1)} %copy-done.8, ...), custom_call_target="tpu_custom_call" | custom-call | tf_op jit(solution)/shard_map/finish/pallas_call | solution.py:312
  165.2 28.3 %all_to_all.19 = bf16[4,128,2048]{2,1,0:T(8,128)(2,1)S(1)} all-to-all(bf16[4,128,2048]{2,1,0:T(8,128)(2,1)S(1)} %bitcast.8), channel_id=1, replica_groups=mesh['ctx'=8,'head'=4] {'head'}, dimensions={0} | all-to-all | bytes 4194304 | tf_op jit(solution)/shard_map/all_to_all | solution.py:341
  193.4 1.5 copy.10
  (1 shorter events, 0.0 us)
Async XLA Ops:
  72.1 25.1 %collective-permute-start = (bf16[16,128,256]{2,1,0:T(8,128)(2,1)}, bf16[16,128,256]{2,1,0:T(8,128)(2,1)S(1)}, u32[]{:S(2)}, u32[]{:S(2)}) collective-permute-start(bf16[16,128,256]{2,1,0:T(8,128)(2,1)} %get-tuple-element.16.own_ref), channel_id=1, source_target_pairs={{0,4},{4,0},{8,12},{12,8},{16,20},{20,16},{24,28},{28,24},{1,5},{5... | collective-permute-start | bytes 3145736 | tf_op jit(solution)/shard_map/ppermute | solution.py:334
  97.3 1.2 copy-start.2
  98.6 31.7 %copy-start.12 = (f32[512,80]{0,1:T(8,128)S(1)}, f32[512,80]{0,1:T(8,128)}, u32[]{:S(2)}) copy-start(f32[512,80]{0,1:T(8,128)} %param.12) | copy-start | bytes 491524
  98.6 56.1 %copy-start.11 = (s32[8]{0:T(128)S(1)}, s32[8]{0:T(128)}, u32[]{:S(2)}) copy-start(s32[8]{0:T(128)} %levels_ref.1) | copy-start | bytes 100
  99.1 0.8 copy-start.3
  99.9 0.8 copy-start.5
  100.7 54.0 %copy-start.1 = (bf16[512,2048]{1,0:T(8,128)(2,1)S(1)}, bf16[512,2048]{1,0:T(8,128)(2,1)}, u32[]{:S(2)}) copy-start(bf16[512,2048]{1,0:T(8,128)(2,1)} %get-tuple-element.15.rows_ref) | copy-start | bytes 6291460
  100.7 24.1 %collective-permute-start.1 = (bf16[16,128,256]{2,1,0:T(8,128)(2,1)S(1)}, bf16[16,128,256]{2,1,0:T(8,128)(2,1)}, u32[]{:S(2)}, u32[]{:S(2)}) collective-permute-start(bf16[16,128,256]{2,1,0:T(8,128)(2,1)S(1)} %get-tuple-element.18.own_ref), channel_id=1, source_target_pairs={{0,8},{4,12},{8,0},{12,4},{16,24},{20,28},{24,16},{28,20},{1,9},{5... | collective-permute-start | bytes 3145736 | tf_op jit(solution)/shard_map/ppermute | solution.py:334
  124.8 1.0 copy-start.4
  127.8 1.0 copy-start.7
  127.8 1.1 copy-start.9
  128.9 25.8 %collective-permute-start.2 = (bf16[16,128,128]{2,1,0:T(8,128)(2,1)}, bf16[16,128,128]{2,1,0:T(8,128)(2,1)S(1)}, u32[]{:S(2)}, u32[]{:S(2)}) collective-permute-start(bf16[16,128,128]{2,1,0:T(8,128)(2,1)} %slice.3), channel_id=1, source_target_pairs={{0,16},{4,20},{8,24},{12,28},{1,17},{5,21},{9,25},{13,29},{2,18},{... | collective-permute-start | bytes 1572872 | tf_op jit(solution)/shard_map/ppermute | solution.py:339
  154.7 2.2 %copy-start = (f32[512,2048]{1,0:T(8,128)S(1)}, f32[512,2048]{1,0:T(8,128)}, u32[]{:S(2)}) copy-start(f32[512,2048]{1,0:T(8,128)} %get-tuple-element.14.near_ref) | copy-start | bytes 12582916
  156.9 1.0 copy-start.6
  157.9 1.0 copy-start.8
  159.0 1.0 copy-start.10

commit v2 on v0

v2 whole, which is shorter than its diff:
```python
import jax
import jax.numpy as jnp
from jax import lax
from jax.sharding import PartitionSpec as P
from jax.experimental import pallas as pl
from jax.experimental.pallas import tpu as pltpu

BLOCK = 64
WIDE = 128
LEVELS = 5
SHARES = (8, 8)
f32 = jnp.float32
bf16 = jnp.bfloat16
MEG = 1024 * 1024
FINISH = 16
LOCAL = 62.25
GATHER = 8


def mxu(a, b):
    return lax.dot_general(a, b, (((1,), (0,)), ((), ())), preferred_element_type=f32)


def mxu_t(a, b):
    return lax.dot_general(a, b, (((1,), (1,)), ((), ())), preferred_element_type=f32)


def halves(x):
    hi = x.astype(bf16)
    return hi, (x - hi.astype(f32)).astype(bf16)


def together(live):
    while live:
        live = [g for g in live if next(g, g) is not g]


def repeat(count, body, unroll):
    while count % unroll:
        unroll -= 1

    def step(i, _):
        together([body(i * unroll + j) for j in range(unroll)])
        return 0

    lax.fori_loop(0, count // unroll, step, 0)


def split(heads, shares):
    counts = [heads * share // sum(shares) for share in shares]
    return [(sum(counts[:g]), n) for g, n in enumerate(counts)]


def aligned(index, size):
    return pl.ds(pl.multiple_of(index * size, size), size)


def left_half():
    return lax.broadcasted_iota(jnp.int32, (BLOCK, WIDE), 1) < BLOCK


def diagonal(x, left):
    zero = jnp.zeros_like(x)
    return jnp.concatenate([jnp.where(left, x, zero), jnp.where(left, zero, x)], axis=0)


def column(table, lane, at):
    picked = jnp.sum(jnp.where(lane == at, table, 0.0), axis=1, keepdims=True)
    return jnp.broadcast_to(picked, (BLOCK, WIDE))


def local_kernel(solve, span, heads, depth, levels_ref, *refs):
    first, count = span
    names = ["weight", "row", "col", "kn", "t", "q", "v"]
    if solve:
        names = ["weight", "ld", "wr", "k", "q", "v"]
    inputs, refs = dict(zip(names, refs)), refs[len(names):]
    run_ref, term_hbm, refs = refs[0], refs[1], refs[2:]
    if solve:
        row_s, colg_s, kn_hbm, t_hbm, refs = *refs[:4], refs[4:]
        ld_s, wr_s, k_s, low_s, inv_s, colb_s, key_sem, refs = *refs[:7], refs[7:]
    else:
        row_s, colg_s = inputs["row"], inputs["col"]
    (
        weight_s, q_s, v_s, kn_s, gram_s, scale_s, m_s, s_s, qt_s, near_s, p_s, term_s, copy_sem,
        keep_sem, step_sem,
    ) = refs
    tokens = q_s.shape[0]
    pairs = tokens // WIDE
    units = heads * pairs
    blocks = tokens // BLOCK
    lanes = 2 * units
    across = heads if solve else count
    mine = slice(first * WIDE, (first + count) * WIDE)

    loads = {
        "weight": (inputs["weight"], weight_s),
        "q": (inputs["q"].at[:, mine], q_s),
        "v": (inputs["v"].at[:, mine], v_s),
    }
    if solve:
        loads.update(ld=(inputs["ld"], ld_s), wr=(inputs["wr"], wr_s))
    else:
        loads["kn"] = (inputs["kn"].at[first:first + count], kn_s)
        for p in range(pairs):
            at = (p * heads + first) * BLOCK
            part = slice(p * count * BLOCK, (p + 1) * count * BLOCK)
            loads["t", p] = (inputs["t"].at[at:at + count * BLOCK], gram_s.at[part])
    loads = {
        name: pltpu.make_async_copy(x, y, copy_sem.at[i])
        for i, (name, (x, y)) in enumerate(loads.items())
    }
    if solve:
        quarter = k_s.shape[1] // 4

        def key_copy(i):
            part = aligned(i, quarter)
            return pltpu.make_async_copy(inputs["k"].at[:, part], k_s.at[:, part], key_sem.at[i])

        loads["ld"].start()
        loads["wr"].start()
        for i in range(4):
            key_copy(i).start()
    for name, c in loads.items():
        if name not in ("ld", "wr"):
            c.start()

    left = left_half()
    ri = lax.broadcasted_iota(jnp.int32, (WIDE, WIDE), 0)
    ci = lax.broadcasted_iota(jnp.int32, (WIDE, WIDE), 1)

    def inverses():
        tri = jnp.where((ri <= ci) & ((ri >= BLOCK) == (ci >= BLOCK)), 1.0, 0.0)
        def by_unit(x):
            return jnp.concatenate([x[:, p * WIDE:(p + 1) * WIDE] for p in range(pairs)], axis=0)

        loads["ld"].wait()
        loads["wr"].wait()
        grow = lax.dot_general(
            by_unit(ld_s[...]), tri, (((1,), (0,)), ((), ())),
            precision=lax.Precision.HIGHEST, preferred_element_type=f32,
        )
        row_s[...] = grow
        gcol = grow.T
        bcol = by_unit(wr_s[...]).T
        colg_s[...] = jnp.concatenate([gcol[:BLOCK], gcol[BLOCK:]], axis=1)
        colb_s[...] = jnp.concatenate([bcol[:BLOCK], bcol[BLOCK:]], axis=1)

        def keys(h):
            cols = aligned(h, WIDE)
            kf = k_s[:, cols].astype(f32)
            total = jnp.sum(kf * kf, axis=1, keepdims=True)
            yield
            kn = (kf * lax.rsqrt(total + 1e-6)).astype(bf16)
            kn_s[h] = kn
            grams = []
            for p in range(pairs):
                kp = kn[p * WIDE:(p + 1) * WIDE]
                grams.append(mxu_t(kp, kp))
            yield
            for p, g in enumerate(grams):
                gram_s[aligned(p * heads + h, BLOCK), :] = jnp.where(left, g[:BLOCK], g[BLOCK:])

        def key_group(i, _):
            key_copy(i).wait()
            together([keys(i * (heads // 4) + j) for j in range(heads // 4)])
            return 0

        lax.fori_loop(0, 4, key_group, 0)

        def to_lanes(i):
            a = gram_s[pl.ds(i, units, stride=BLOCK), :].T
            yield
            g = jnp.concatenate([a[:BLOCK], a[BLOCK:]], axis=1)
            gi = colg_s[pl.ds(i, 1), :]
            bi = colb_s[pl.ds(i, 1), :]
            e = jnp.exp(gi - colg_s[...])
            yield
            low_s[i] = g * (bi * e)
            inv_s[i] = jnp.zeros_like(g)

        repeat(BLOCK, to_lanes, 16)

        sub = lax.broadcasted_iota(jnp.int32, (8, lanes), 0)

        def solve(bi, _):
            i0 = bi * 8

            def columns(cb, _):
                c = aligned(cb, 8)

                def step(jb, acc):
                    acc = list(acc)
                    for jj in range(8):
                        j = jb * 8 + jj
                        t = inv_s[j, c, :]
                        for r in range(8):
                            acc[r] = acc[r] - low_s[i0 + r, pl.ds(j, 1), :] * t
                    return tuple(acc)

                on = cb == bi
                acc = tuple(jnp.where((sub == r) & on, 1.0, 0.0) for r in range(8))
                acc = list(lax.fori_loop(cb, bi, step, acc))
                for r in range(8):
                    inv_s[i0 + r, c, :] = acc[r]
                    for s in range(r + 1, 8):
                        acc[s] = acc[s] - low_s[i0 + s, pl.ds(i0 + r, 1), :] * acc[r]
                return 0

            lax.fori_loop(0, bi + 1, columns, 0)
            return 0

        lax.fori_loop(0, BLOCK // 8, solve, 0)

        def from_lanes(i):
            t = inv_s[i] * colb_s[...]
            a = jnp.concatenate([t[:, :units], t[:, units:]], axis=0).T
            yield
            gram_s[pl.ds(i, units, stride=BLOCK), :] = a

        repeat(BLOCK, from_lanes, 16)

    kept = []
    if solve:
        inverses()
        kept = [(kn_s, kn_hbm), (gram_s, t_hbm)]
        kept = [pltpu.make_async_copy(x, y, keep_sem.at[i]) for i, (x, y) in enumerate(kept)]
        for c in kept:
            c.start()
    for name, c in loads.items():
        if name not in ("ld", "wr", "weight"):
            c.wait()
    clane = lax.broadcasted_iota(jnp.int32, (BLOCK, lanes), 1)
    lane = lax.broadcasted_iota(jnp.int32, (BLOCK, WIDE), 1)
    row64 = lax.broadcasted_iota(jnp.int32, (BLOCK, WIDE), 0)
    keep = row64 >= jnp.where(left, lane, lane - BLOCK)
    eye = ri == ci

    def unit(i):
        p = i // count
        h = i - p * count
        u = p * heads + first + h
        grow = row_s[pl.ds(u, 1), :]
        gs = [column(colg_s[...], clane, u), column(colg_s[...], clane, u + units)]
        kn = kn_s[h, aligned(p, WIDE), :]
        v = v_s[aligned(p, WIDE), aligned(h, WIDE)]
        q = q_s[aligned(p, WIDE), aligned(h, WIDE)]
        qk = mxu_t(q, kn)
        t1 = gram_s[aligned(p * across + h, BLOCK), :]
        t2 = t1 * jnp.exp(grow)
        a_hi, a_lo = halves(diagonal(t1, left))
        b_hi, b_lo = halves(diagonal(t2, left))
        wv = mxu(jnp.concatenate([a_hi, a_lo], axis=1), jnp.concatenate([v, v], axis=0))
        wk = mxu(jnp.concatenate([b_hi, b_lo], axis=1), jnp.concatenate([kn, kn], axis=0))
        knt = kn.astype(f32).T.astype(bf16)
        decay = jnp.exp(jnp.where(keep, jnp.where(left, gs[0], gs[1]) - grow, -1e30))
        yield
        score = diagonal(jnp.where(left, qk[:BLOCK], qk[BLOCK:]) * decay, left).astype(bf16)
        w = jnp.concatenate([wv, wk], axis=1)
        kk = jnp.concatenate([knt, knt], axis=1)
        outs = []
        for half, g in enumerate(gs):
            end = g[BLOCK - 1:, :]
            tail = jnp.exp(end - g)
            part = w[half * BLOCK:(half + 1) * BLOCK] * jnp.concatenate([tail, tail], axis=1)
            hi, lo = halves(part)
            none = jnp.zeros_like(hi)
            stack = [hi, none, lo, none] if half == 0 else [none, hi, none, lo]
            outs.append((end, mxu(kk, jnp.concatenate(stack, axis=0))))
        ys = mxu(score, w.astype(bf16))
        yield
        for half, (end, y) in enumerate(outs):
            s_s[2 * p + half, h] = y[:, :WIDE]
            m = jnp.where(eye, jnp.exp(end), 0.0) - y[:, WIDE:]
            m_hi, m_lo = halves(m)
            m_s[2 * p + half, h] = jnp.concatenate([m_hi, m_lo], axis=1)
        near_s[i] = ys[:, :WIDE]
        eg = jnp.exp(jnp.concatenate(gs, axis=0))
        qt_s[i] = (eg * q.astype(f32) - ys[:, WIDE:]).astype(bf16)

    repeat(pairs * count, unit, 8)

    loads["weight"].wait()
    slots = weight_s.shape[0]
    level = lax.rem(lax.broadcasted_iota(jnp.int32, (BLOCK, slots), 1), LEVELS)
    weight = weight_s[...].T
    for b in range(blocks):
        toks = slice(b * BLOCK, (b + 1) * BLOCK)
        scale_s[toks, :] = jnp.where(level < levels_ref[b], weight[toks], 0.0)

    def term_copy(b):
        toks = aligned(b, BLOCK)
        return pltpu.make_async_copy(term_s.at[b], term_hbm.at[:, toks, :], step_sem.at[b])

    def write(b, h, near, rows):
        cols = pl.ds(h * WIDE, WIDE)
        scale = scale_s[aligned(b, BLOCK), :]
        for i in range(1 + depth):
            at = (first + h) * LEVELS + i
            term_s[b, i, :, cols] = ((rows if i else near) * scale[:, at:at + 1]).astype(bf16)

    for h in range(count):
        m = m_s[0, h]
        p_s[h, :, :WIDE] = s_s[0, h]
        p_s[h, :, WIDE:] = m[:, :WIDE].astype(f32) + m[:, WIDE:].astype(f32)
        write(0, h, near_s[h, :BLOCK, :], qt_s[h, :BLOCK, :].astype(f32))
    term_copy(0).start()

    def scan(b, _):
        half = aligned(b % 2, BLOCK)

        def advance(h):
            i = (b // 2) * count + h
            p_hi, p_lo = halves(p_s[h])
            m = m_s[b, h]
            n = mxu(
                jnp.concatenate([m, m[:, :WIDE]], axis=1),
                jnp.concatenate([p_hi, p_hi, p_lo], axis=0),
            )
            o = mxu(qt_s[i, half, :], p_hi)
            yield
            p_s[h, :, :WIDE] = n[:, :WIDE] + s_s[b, h]
            p_s[h, :, WIDE:] = n[:, WIDE:]
            write(b, h, near_s[i, half, :] + o[:, :WIDE], o[:, WIDE:])

        for h in range(0, count, 4):
            together([advance(h + j) for j in range(min(4, count - h))])
        term_copy(b).start()
        return 0

    lax.fori_loop(1, blocks, scan, 0)
    for h in range(count):
        run_ref[h] = p_s[h].astype(bf16)
    for c in kept:
        c.wait()
    for b in range(blocks):
        term_copy(b).wait()


def local_call(span, heads, depth, levels, weights, solved, inputs, q, v, after):
    tokens = q.shape[0]
    first, count = span
    pairs = tokens // WIDE
    units = heads * pairs
    blocks = tokens // BLOCK
    solve = solved is None
    smem = pl.BlockSpec(memory_space=pltpu.SMEM)
    vmem = pl.BlockSpec(memory_space=pltpu.VMEM)
    hbm = pl.BlockSpec(memory_space=pltpu.HBM)
    after, spaces = waits(after)
    out_specs = [vmem, hbm]
    out_shape = [
        jax.ShapeDtypeStruct((count, WIDE, 2 * WIDE), bf16),
        jax.ShapeDtypeStruct((1 + depth, tokens, count * WIDE), bf16),
    ]
    scratch = []
    if solve:
        operands = [weights, *inputs, q, v]
        in_specs = [hbm] * 6
        out_specs += [vmem, vmem, hbm, hbm]
        out_shape += [
            jax.ShapeDtypeStruct((units, WIDE), f32),
            jax.ShapeDtypeStruct((BLOCK, 2 * units), f32),
            jax.ShapeDtypeStruct((heads, tokens, WIDE), bf16),
            jax.ShapeDtypeStruct((units * BLOCK, WIDE), f32),
        ]
        scratch = [
            pltpu.VMEM(inputs[0].shape, f32),
            pltpu.VMEM(inputs[1].shape, f32),
            pltpu.VMEM(inputs[2].shape, bf16),
            pltpu.VMEM((BLOCK, BLOCK, 2 * units), f32),
            pltpu.VMEM((BLOCK, BLOCK, 2 * units), f32),
            pltpu.VMEM((BLOCK, 2 * units), f32),
            pltpu.SemaphoreType.DMA((4,)),
        ]
    else:
        operands = [weights, *solved, q, v]
        in_specs = [hbm, vmem, vmem, hbm, hbm, hbm, hbm]
    across = heads if solve else count

    def kernel(*refs):
        used = 1 + len(operands)
        local_kernel(solve, span, heads, depth, *refs[:used], *refs[used + len(after):])

    return pl.pallas_call(
        kernel,
        in_specs=[smem] + in_specs + spaces,
        out_specs=out_specs,
        out_shape=out_shape,
        scratch_shapes=scratch
        + [
            pltpu.VMEM(weights.shape, f32),
            pltpu.VMEM((tokens, count * WIDE), bf16),
            pltpu.VMEM((tokens, count * WIDE), bf16),
            pltpu.VMEM((across, tokens, WIDE), bf16),
            pltpu.VMEM((across * pairs * BLOCK, WIDE), f32),
            pltpu.VMEM((tokens, weights.shape[0]), f32),
            pltpu.VMEM((blocks, count, WIDE, 2 * WIDE), bf16),
            pltpu.VMEM((blocks, count, WIDE, WIDE), f32),
            pltpu.VMEM((pairs * count, WIDE, WIDE), bf16),
            pltpu.VMEM((pairs * count, WIDE, WIDE), f32),
            pltpu.VMEM((count, WIDE, 2 * WIDE), f32),
            pltpu.VMEM((blocks, 1 + depth, BLOCK, count * WIDE), bf16),
            pltpu.SemaphoreType.DMA((5 + pairs,)),
            pltpu.SemaphoreType.DMA((2,)),
            pltpu.SemaphoreType.DMA((blocks,)),
        ],
        compiler_params=pltpu.CompilerParams(vmem_limit_bytes=int(LOCAL * MEG)),
        name="local",
    )(levels, *operands, *after)


def waits(after):
    return [x for x, _ in after], [pl.BlockSpec(memory_space=space) for _, space in after]


def pair_kernel(flag_ref, own_ref, other_ref, *rest):
    s_ref, m_ref = rest[-2:]
    heads = own_ref.shape[0]
    upper = flag_ref[0] == 1

    def head(h):
        own = own_ref[h]
        other = other_ref[h]
        late = jnp.where(upper, own, other)
        early = jnp.where(upper, other, own)
        both = mxu(late[:, WIDE:], early)
        yield
        s_ref[h] = (both[:, :WIDE] + late[:, :WIDE].astype(f32)).astype(bf16)
        m_ref[h] = both[:, WIDE:].astype(bf16)

    together([head(h) for h in range(heads)])


def pair_call(flag, own, other, after):
    square = jax.ShapeDtypeStruct((own.shape[0], WIDE, WIDE), bf16)
    vmem = pl.BlockSpec(memory_space=pltpu.VMEM)
    after, spaces = waits(after)
    return pl.pallas_call(
        pair_kernel,
        in_specs=[pl.BlockSpec(memory_space=pltpu.SMEM), vmem, vmem]
        + spaces,
        out_specs=[vmem, vmem],
        out_shape=[square, square],
        compiler_params=pltpu.CompilerParams(vmem_limit_bytes=8 * MEG),
        name="pair",
    )(flag, own, other, *after)


def hop_kernel(m_ref, *refs):
    *entry_refs, out_ref = refs

    def head(h):
        entry = entry_refs[1][h]
        for ref in entry_refs[2:]:
            entry = (entry.astype(f32) + ref[h].astype(f32)).astype(bf16)
        o = mxu(m_ref[h], entry)
        yield
        if entry_refs[0] is not None:
            o = o + entry_refs[0][h].astype(f32)
        out_ref[h] = o.astype(bf16)

    together([head(h) for h in range(m_ref.shape[0])])


def hop_call(m, s, entries, after):
    vmem = pl.BlockSpec(memory_space=pltpu.VMEM)
    operands = ([] if s is None else [s]) + entries

    after, spaces = waits(after)

    def kernel(m_ref, *refs):
        used = refs[:len(operands)] + refs[-1:]
        hop_kernel(m_ref, *(used if s is not None else (None,) + used))

    return pl.pallas_call(
        kernel,
        in_specs=[vmem] * (1 + len(operands)) + spaces,
        out_specs=vmem,
        out_shape=jax.ShapeDtypeStruct(m.shape, bf16),
        compiler_params=pltpu.CompilerParams(vmem_limit_bytes=8 * MEG),
        name="hop",
    )(m, *operands, *after)


def finish_kernel(size, shape, here_ref, term_ref, other_ref, *refs):
    entries, at = [], 0
    for count in shape:
        entries.append(refs[at:at + count])
        at += count
    outs = refs[at:at + size]
    depth, tokens, width = term_ref.shape
    chunk = tokens // size
    heads = width // WIDE
    here = here_ref[0]
    position = here_ref[1]
    zero = jnp.zeros((WIDE, WIDE), bf16)
    odd = (position & 1) == 1
    pair = position >> 1
    carries = []
    for h in range(heads):
        came = []
        for m, options in enumerate(entries):
            entry = zero
            for j, ref in enumerate(options):
                mine = ((pair >> m) & 1 == 1) & ((pair & ((1 << m) - 1)) == j)
                entry = jnp.where(mine, ref[h], entry)
            came.append(entry)
        wide = jnp.concatenate(came, axis=1)
        ahead = mxu(other_ref[h, :, WIDE:], wide).astype(bf16)
        carries.append(jnp.concatenate(
            [jnp.where(odd, other_ref[h, :, :WIDE], zero)]
            + [
                jnp.where(odd, ahead[:, m * WIDE:(m + 1) * WIDE], x) for m, x in enumerate(came)
            ],
            axis=0,
        ))
    for d in range(size):
        toks = aligned(here ^ d, chunk)

        def head(h):
            part = slice(h * WIDE, (h + 1) * WIDE)
            far = jnp.concatenate([term_ref[i, toks, part] for i in range(1, depth)], axis=1)
            total = mxu(far, carries[h])
            yield
            outs[d][:, part] = (total + term_ref[0, toks, part].astype(f32)).astype(bf16)

        together([head(h) for h in range(heads)])


def finish_call(size, here, terms, other, entries, after):
    depth, tokens, width = terms.shape
    smem = pl.BlockSpec(memory_space=pltpu.SMEM)
    vmem = pl.BlockSpec(memory_space=pltpu.VMEM)
    shape = [len(e) for e in entries]
    flat = [x for e in entries for x in e]
    after, spaces = waits(after)

    def kernel(*refs):
        used = 3 + len(flat)
        finish_kernel(size, shape, *refs[:used], *refs[used + len(after):])

    return pl.pallas_call(
        kernel,
        in_specs=[smem] + [vmem] * (2 + len(flat)) + spaces,
        out_specs=[vmem] * size,
        out_shape=[jax.ShapeDtypeStruct((tokens // size, width), bf16)] * size,
        compiler_params=pltpu.CompilerParams(vmem_limit_bytes=FINISH * MEG),
        name="finish",
    )(here, terms, other, *flat, *after)


def gather_kernel(first, heads, size, place_ref, *refs):
    parts, (out_ref, sems) = refs[:size], refs[-2:]
    here = place_ref[0]
    copies = []
    for d, ref in enumerate(parts):
        col = pl.multiple_of(((here ^ d) * heads + first) * WIDE, WIDE)
        where = out_ref.at[:, pl.ds(col, ref.shape[1])]
        copies.append(pltpu.make_async_copy(ref, where, sems.at[d]))
        copies[-1].start()
    for c in copies:
        c.wait()


def gather_call(first, heads, place, parts, before, after):
    size = len(parts)
    vmem = pl.BlockSpec(memory_space=pltpu.VMEM)
    hbm = pl.BlockSpec(memory_space=pltpu.HBM)
    after, spaces = waits(after)
    kept = [] if before is None else [before]

    def kernel(*refs):
        gather_kernel(first, heads, size, *refs)

    return pl.pallas_call(
        kernel,
        in_specs=[pl.BlockSpec(memory_space=pltpu.SMEM)] + [vmem] * size + [hbm] * len(kept)
        + spaces,
        out_specs=hbm,
        out_shape=jax.ShapeDtypeStruct((parts[0].shape[0], heads * size * WIDE), bf16),
        input_output_aliases={1 + size: 0} if kept else {},
        scratch_shapes=[pltpu.SemaphoreType.DMA((size,))],
        compiler_params=pltpu.CompilerParams(vmem_limit_bytes=GATHER * MEG),
        name="gather",
    )(place, *parts, *kept, *after)


ORDER = ("l0", "l1", "p0", "h01", "p1", "h02", "h11", "f0", "h12", "f1", "g0", "g1")


def order(groups, steps):
    names = dict(l="local", p="pair", h="hop", f="finish", g="gather")
    if steps == 3:
        return [(names[x[0]], int(x[1]), int(x[2:] or 0)) for x in ORDER]
    out = [("local", g, 0) for g in range(groups)] + [("pair", g, 0) for g in range(groups)]
    out += [("hop", g, step) for step in range(1, steps) for g in range(groups)]
    out += [("finish", g, 0) for g in range(groups)]
    return out + [("gather", g, 0) for g in range(groups)]


def per_device(queries, key_rows, value_rows, log_decay, write_rate, level_weights, block_levels):
    size = lax.axis_size("ctx")
    bits = size.bit_length() - 1
    width = lax.axis_size("head")
    position = lax.axis_index("ctx").astype(jnp.int32)
    place = lax.axis_index("head").astype(jnp.int32)
    here = jnp.stack([place, position])
    flag = (position & 1).reshape(1)
    heads = log_decay.shape[1]
    groups = split(heads, SHARES)
    pairs = size // 2
    steps = [(m, j) for m in range(pairs.bit_length() - 1) for j in range(1 << m)]

    def swap(low, array):
        to = list(range(pairs))
        for p in low:
            to[p], to[p + 1] = p + 1, p
        return lax.ppermute(array, "ctx", [(i, 2 * to[i >> 1] + (i & 1)) for i in range(size)])

    runs, others, terms, states, solved = {}, {}, {}, {}, []
    entries = [[] for _ in groups]
    pieces = {}
    after = []

    def local(g):
        runs[g], terms[g], *kept = local_call(
            groups[g], heads, bits, block_levels, level_weights.T, solved[0] if solved else None,
            [log_decay.T, write_rate.T, key_rows], queries, value_rows, after,
        )
        if kept:
            solved.append(kept)
        others[g] = lax.ppermute(runs[g], "ctx", [(i, i ^ 1) for i in range(size)])
        return terms[g], pltpu.HBM

    def pair(g):
        states[g] = pair_call(flag, runs[g], others[g], after)
        return states[g][1], pltpu.VMEM

    def hop(g, step):
        m, j = steps[step]
        s, t = states[g]
        if j:
            sent = hop_call(t, None, [entries[g][m][j - 1]], after)
        elif m:
            sent = hop_call(t, s, [e[-1] for e in entries[g]], after)
        else:
            sent = s
        if j == 0:
            entries[g].append([])
        low = [p for p in range(pairs) if p % (2 << m) == (1 << m) + j - 1]
        entries[g][m].append(swap(low, sent))
        return sent, pltpu.VMEM

    def finish(g):
        outs = finish_call(width, here, terms[g], others[g], entries[g], after)
        for d in range(width):
            pairing = [(i, i ^ d) for i in range(width)]
            pieces[g, d] = outs[d] if d == 0 else lax.ppermute(outs[d], "head", pairing)
        return outs[0], pltpu.VMEM

    def gather(g, out):
        parts = [pieces[g, d] for d in range(width)]
        return gather_call(groups[g][0], heads, place.reshape(1), parts, out, after)

    out = None
    for name, g, step in order(len(groups), len(steps)):
        if name == "local":
            token = local(g)
        elif name == "pair":
            token = pair(g)
            hop(g, 0)
        elif name == "hop":
            token = hop(g, step)
        elif name == "finish":
            token = finish(g)
        else:
            out = gather(g, out)
            token = out, pltpu.HBM
        after = [token]
    return out


def solution(mesh):
    wide = P("ctx", "head")
    return jax.shard_map(
        per_device,
        mesh=mesh,
        in_specs=(wide, wide, wide, wide, wide, wide, P("ctx")),
        out_specs=P(("ctx", "head"), None),
        check_vma=False,
    )
```

time: 1020 us -> 99.7 us (0.10); the launches traced: 1010 us -> 99.4 us
  other arithmetic: 671 us -> 0.08 us
  waiting for transfers between devices: 145 us -> 31 us
  matrix products: 113 us -> 0 us
  Pallas kernels: 0 us -> 42.9 us
  local copies, waits for them, and re-layouts: 45 us -> 5.71 us
  blocking collectives: 28.9 us -> 0 us
  starting transfers between devices: 2.33 us -> 19.6 us
    another operation x4 -> x1, other arithmetic: 634 us -> 0.08 us  [per_device(): here = jnp.stack([place, position])]
    ppermute x3 -> x14, waiting for transfers between devices: 145 us -> 31 us  [the longest x6 15.6 us: finish(): pieces[g, d] = outs[d] if d == 0 else lax.ppermute(outs[d], 'head', pairing)]
    dot_general x27 -> x0, matrix products: 102 us -> none  [the longest x8 28.3 us: advance(): jnp.einsum('hcd,hde->hce', wy_part, carry_state, precision=precise)]
    pallas_call x0 -> x12, Pallas kernels: none -> 42.9 us  [the longest x2 36.9 us: local_call(): pl.pallas_call(kernel, in_specs=[smem] + in_specs + spaces, out_specs=out...]
    all_to_all x1 -> x0, blocking collectives: 28.9 us -> none  [per_device(): lax.all_to_all(outputs, 'head', split_axis=0, concat_axis=1, tiled=True)]
    ppermute x3 -> x14, starting transfers between devices: 2.33 us -> 19.6 us  [the longest x6 13.3 us: swap(): lax.ppermute(array, 'ctx', [(i, 2 * to[i >> 1] + (i & 1)) for i in range(...]
    reduce_sum x2 -> x0, other arithmetic: 11.4 us -> none  [the longest x1 8.06 us: finish(): total = jnp.sum(scaled[..., None] * terms, axis=2)]
    another operation x1 -> x0, matrix products: 11.1 us -> none  [local_pass(): jax.scipy.linalg.solve_triangular(strict_part, right_side, lower=True, un...]
  transfers between devices with their start and end apart: 3 -> 14, of which waited for: 3 -> 8; matrix products, arithmetic and copies ran while one was open for 4% -> 1% of each run, Pallas kernels for 0% -> 19%
where the time goes in v2:
time: 99.7 us; the launch traced here: 99.4 us
  Pallas kernels  42.9 us (43%)
  waiting for transfers between devices  31 us (31%)
  starting transfers between devices  19.6 us (20%)
  local copies, waits for them, and re-layouts  5.71 us (6%)
    pallas_call x2, Pallas kernels, local_call(): pl.pallas_call(kernel, in_specs=[smem] + in_specs + spaces, out_specs=out...  36.9 us
    ppermute x6, waiting for transfers between devices, finish(): pieces[g, d] = outs[d] if d == 0 else lax.ppermute(outs[d], 'head', pairing)  15.6 us
    ppermute x6, starting transfers between devices, swap(): lax.ppermute(array, 'ctx', [(i, 2 * to[i >> 1] + (i & 1)) for i in range(...  13.3 us
    ppermute x6, waiting for transfers between devices, swap(): lax.ppermute(array, 'ctx', [(i, 2 * to[i >> 1] + (i & 1)) for i in range(...  13.2 us
    unnamed x11, local copies, waits for them, and re-layouts  5.71 us
    ppermute x6, starting transfers between devices, finish(): pieces[g, d] = outs[d] if d == 0 else lax.ppermute(outs[d], 'head', pairing)  4.13 us
    pallas_call x2, Pallas kernels, finish_call(): pl.pallas_call(kernel, in_specs=[smem] + [vmem] * (2 + len(flat)) + space...  3.47 us
    ppermute x2, starting transfers between devices, local(): others[g] = lax.ppermute(runs[g], 'ctx', [(i, i ^ 1) for i in range(size)])  2.15 us
  transfers between devices with their start and end apart: 14, of which 8 were waited for; matrix products, arithmetic and copies ran while one was open for 1% of the time, Pallas kernels for 19%

profile of v2, /device:TPU:24, one launch (start us, length us, event | category | flops | bytes accessed | tf_op | source)
XLA Modules:
  0.0 99.4 jit_solution(14046794122160073039)
XLA Ops:
  0.0 22.9 %local.2 = (bf16[8,128,256]{2,1,0:T(8,128)(2,1)}, bf16[4,512,1024]{2,1,0:T(8,128)(2,1)}, f32[64,128]{1,0:T(8,128)}, f32[64,128]{1,0:T(8,128)}, bf16[16,512,128]{2,1,0:T(8,128)(2,1)}, /*index=5*/f32[4096,128]{1,0:T(8,128)}) custom-call(s32[8]{0:T(128)} %refs_0_.3, f32[80,512]{1,0:T(8,128)} %bitcast.6, f32[16,512]{1,0:T(8,128)} %bitcast.8, f32[16,512]{1,0:T(8,128)} %bitcast.9, ...), custom_call_target="tpu_custom_call" | custom-call | tf_op jit(solution)/shard_map/local/pallas_call | solution.py:385
  22.9 1.6 %collective-permute-start.1 = (bf16[8,128,256]{2,1,0:T(8,128)(2,1)}, bf16[8,128,256]{2,1,0:T(8,128)(2,1)S(1)}, u32[]{:S(2)}, u32[]{:S(2)}) collective-permute-start(bf16[8,128,256]{2,1,0:T(8,128)(2,1)} %get-tuple-element.32.own_ref), channel_id=1, source_target_pairs={{0,4},{4,0},{8,12},{12,8},{16,20},{20,16},{24,28},{28,24},{1,5},{5... | collective-permute-start | bytes 1572872 | tf_op jit(solution)/shard_map/ppermute | solution.py:633
  24.5 0.0 copy-start.4
  24.5 14.0 %local.3 = (bf16[8,128,256]{2,1,0:T(8,128)(2,1)}, bf16[4,512,1024]{2,1,0:T(8,128)(2,1)}) custom-call(s32[8]{0:T(128)} %refs_0_.3, f32[80,512]{1,0:T(8,128)} %bitcast.7, f32[64,128]{1,0:T(8,128)} %get-tuple-element.25.refs_2_, f32[64,128]{1,0:T(8,128)} %get-tuple-element.26.refs_3_, bf16[16,512,128]{2,1,0:T(8,128)(2,1)} %get-tuple-element.27.refs_4_, ...), custom_call_target="tpu_custom_call" | custom-call | tf_op jit(solution)/shard_map/local/pallas_call | solution.py:385
  38.4 0.6 collective-permute-start
  39.0 0.0 collective-permute-done.1.other_ref.refs_2_
  39.0 0.0 copy-done.4
  39.0 2.2 %copy-done = bf16[4,512,1024]{2,1,0:T(8,128)(2,1)S(1)} copy-done((bf16[4,512,1024]{2,1,0:T(8,128)(2,1)S(1)}, bf16[4,512,1024]{2,1,0:T(8,128)(2,1)}, u32[]{:S(2)}) %copy-start) | copy-done | bytes 4194328
  41.2 0.3 pair.2
  41.5 0.5 collective-permute-start.2
  42.0 7.1 %collective-permute-done.2.refs_1_.refs_3_ = bf16[8,128,128]{2,1,0:T(8,128)(2,1)S(1)} collective-permute-done((bf16[8,128,128]{2,1,0:T(8,128)(2,1)S(1)}, bf16[8,128,128]{2,1,0:T(8,128)(2,1)S(1)}, u32[]{:S(2)}, u32[]{:S(2)}) %collective-permute-start.2) | collective-permute-done | bytes 262176 | tf_op jit(solution)/shard_map/ppermute | solution.py:619
  49.1 0.2 hop.4.rest_0_
  49.3 0.7 collective-permute-start.4
  50.0 2.1 %collective-permute-done.other_ref.refs_2_ = bf16[8,128,256]{2,1,0:T(8,128)(2,1)S(1)} collective-permute-done((bf16[8,128,256]{2,1,0:T(8,128)(2,1)}, bf16[8,128,256]{2,1,0:T(8,128)(2,1)S(1)}, u32[]{:S(2)}, u32[]{:S(2)}) %collective-permute-start) | collective-permute-done | bytes 524320 | tf_op jit(solution)/shard_map/ppermute | solution.py:633
  52.1 0.0 copy-done.3
  52.1 0.3 pair.3
  52.4 0.5 collective-permute-start.3
  52.9 0.0 collective-permute-done.4.refs_0_.refs_4_
  52.9 0.2 hop.5.refs_2_
  53.2 7.2 %collective-permute-start.6 = (bf16[8,128,128]{2,1,0:T(8,128)(2,1)S(1)}, bf16[8,128,128]{2,1,0:T(8,128)(2,1)S(1)}, u32[]{:S(2)}, u32[]{:S(2)}) collective-permute-start(bf16[8,128,128]{2,1,0:T(8,128)(2,1)S(1)} %hop.5.refs_2_), channel_id=1, source_target_pairs={{0,0},{4,4},{8,8},{12,12},{16,24},{20,28},{24,16},{28,20},{1,1},{5... | collective-permute-start | bytes 786440 | tf_op jit(solution)/shard_map/ppermute | solution.py:619
  60.4 0.0 collective-permute-done.3.refs_1_.refs_3_
  60.4 0.2 hop.6.refs_6_
  60.6 0.7 collective-permute-start.5
  61.3 0.1 pad_add_fusion.refs_0_
  61.4 3.6 %collective-permute-done.6.refs_5_ = bf16[8,128,128]{2,1,0:T(8,128)(2,1)S(1)} collective-permute-done((bf16[8,128,128]{2,1,0:T(8,128)(2,1)S(1)}, bf16[8,128,128]{2,1,0:T(8,128)(2,1)S(1)}, u32[]{:S(2)}, u32[]{:S(2)}) %collective-permute-start.6) | collective-permute-done | bytes 262176 | tf_op jit(solution)/shard_map/ppermute | solution.py:619
  65.0 2.2 %copy-done.2 = bf16[4,512,1024]{2,1,0:T(8,128)(2,1)S(1)} copy-done((bf16[4,512,1024]{2,1,0:T(8,128)(2,1)S(1)}, bf16[4,512,1024]{2,1,0:T(8,128)(2,1)}, u32[]{:S(2)}) %copy-start.2) | copy-done | bytes 4194328
  67.1 1.7 %finish.2 = (bf16[128,1024]{1,0:T(8,128)(2,1)S(1)}, bf16[128,1024]{1,0:T(8,128)(2,1)S(1)}, bf16[128,1024]{1,0:T(8,128)(2,1)S(1)}, bf16[128,1024]{1,0:T(8,128)(2,1)S(1)}) custom-call(s32[2]{0:T(128)S(1)} %pad_add_fusion.refs_0_, bf16[4,512,1024]{2,1,0:T(8,128)(2,1)S(1)} %copy-done.2, bf16[8,128,256]{2,1,0:T(8,128)(2,1)S(1)} %collective-permute-done.1.other_ref.refs_2_, ...), custom_call_target="tpu_custom_call" | custom-call | tf_op jit(solution)/shard_map/finish/pallas_call | solution.py:543
  68.8 0.0 collective-permute-done.5.refs_0_.refs_4_
  68.8 0.2 hop.7.refs_6_
  69.1 3.7 %collective-permute-start.7 = (bf16[8,128,128]{2,1,0:T(8,128)(2,1)S(1)}, bf16[8,128,128]{2,1,0:T(8,128)(2,1)S(1)}, u32[]{:S(2)}, u32[]{:S(2)}) collective-permute-start(bf16[8,128,128]{2,1,0:T(8,128)(2,1)S(1)} %hop.7.refs_6_), channel_id=1, source_target_pairs={{0,0},{4,4},{8,8},{12,12},{16,24},{20,28},{24,16},{28,20},{1,1},{5... | collective-permute-start | bytes 786440 | tf_op jit(solution)/shard_map/ppermute | solution.py:619
  72.8 0.1 collective-permute-start.11
  72.9 1.6 %collective-permute-start.12 = (bf16[128,1024]{1,0:T(8,128)(2,1)S(1)}, bf16[128,1024]{1,0:T(8,128)(2,1)S(1)}, u32[]{:S(2)}, u32[]{:S(2)}) collective-permute-start(bf16[128,1024]{1,0:T(8,128)(2,1)S(1)} %get-tuple-element.43), channel_id=1, source_target_pairs={{0,2},{1,3},{2,0},{3,1},{4,6},{5,7},{6,4},{7,5},{8,10},{9,11},{10,... | collective-permute-start | bytes 786440 | tf_op jit(solution)/shard_map/ppermute | solution.py:659
  74.4 0.3 collective-permute-start.13
  74.7 2.6 %collective-permute-done.7.refs_5_ = bf16[8,128,128]{2,1,0:T(8,128)(2,1)S(1)} collective-permute-done((bf16[8,128,128]{2,1,0:T(8,128)(2,1)S(1)}, bf16[8,128,128]{2,1,0:T(8,128)(2,1)S(1)}, u32[]{:S(2)}, u32[]{:S(2)}) %collective-permute-start.7) | collective-permute-done | bytes 262176 | tf_op jit(solution)/shard_map/ppermute | solution.py:619
  77.3 0.0 copy-done.1
  77.3 1.8 %finish.3 = (bf16[128,1024]{1,0:T(8,128)(2,1)S(1)}, bf16[128,1024]{1,0:T(8,128)(2,1)S(1)}, bf16[128,1024]{1,0:T(8,128)(2,1)S(1)}, bf16[128,1024]{1,0:T(8,128)(2,1)S(1)}) custom-call(s32[2]{0:T(128)S(1)} %pad_add_fusion.refs_0_, bf16[4,512,1024]{2,1,0:T(8,128)(2,1)S(1)} %copy-done.1, bf16[8,128,256]{2,1,0:T(8,128)(2,1)S(1)} %collective-permute-done.other_ref.refs_2_, ...), custom_call_target="tpu_custom_call" | custom-call | tf_op jit(solution)/shard_map/finish/pallas_call | solution.py:543
  79.1 0.1 collective-permute-start.10
  79.2 1.6 %collective-permute-start.8 = (bf16[128,1024]{1,0:T(8,128)(2,1)S(1)}, bf16[128,1024]{1,0:T(8,128)(2,1)S(1)}, u32[]{:S(2)}, u32[]{:S(2)}) collective-permute-start(bf16[128,1024]{1,0:T(8,128)(2,1)S(1)} %get-tuple-element.39), channel_id=1, source_target_pairs={{0,1},{1,0},{2,3},{3,2},{4,5},{5,4},{6,7},{7,6},{8,9},{9,8},{10,11... | collective-permute-start | bytes 786440 | tf_op jit(solution)/shard_map/ppermute | solution.py:659
  80.8 0.0 collective-permute-done.11.refs_2_
  80.8 0.5 collective-permute-start.9
  81.3 0.7 collective-permute-done.12.refs_3_
  82.0 4.7 %collective-permute-done.13.refs_4_ = bf16[128,1024]{1,0:T(8,128)(2,1)S(1)} collective-permute-done((bf16[128,1024]{1,0:T(8,128)(2,1)S(1)}, bf16[128,1024]{1,0:T(8,128)(2,1)S(1)}, u32[]{:S(2)}, u32[]{:S(2)}) %collective-permute-start.13) | collective-permute-done | bytes 262176 | tf_op jit(solution)/shard_map/ppermute | solution.py:659
  86.7 0.1 gather.2.refs_6_
  86.9 1.3 %copy.9.refs_5_ = bf16[128,8192]{1,0:T(8,128)(2,1)} copy(bf16[128,8192]{1,0:T(8,128)(2,1)S(1)} %gather.2.refs_6_) | data formatting | bytes 4194304
  88.2 4.2 %collective-permute-done.10.refs_4_ = bf16[128,1024]{1,0:T(8,128)(2,1)S(1)} collective-permute-done((bf16[128,1024]{1,0:T(8,128)(2,1)S(1)}, bf16[128,1024]{1,0:T(8,128)(2,1)S(1)}, u32[]{:S(2)}, u32[]{:S(2)}) %collective-permute-start.10) | collective-permute-done | bytes 262176 | tf_op jit(solution)/shard_map/ppermute | solution.py:659
  92.4 0.0 collective-permute-done.8.refs_2_
  92.4 6.1 %collective-permute-done.9.refs_3_ = bf16[128,1024]{1,0:T(8,128)(2,1)S(1)} collective-permute-done((bf16[128,1024]{1,0:T(8,128)(2,1)S(1)}, bf16[128,1024]{1,0:T(8,128)(2,1)S(1)}, u32[]{:S(2)}, u32[]{:S(2)}) %collective-permute-start.9) | collective-permute-done | bytes 262176 | tf_op jit(solution)/shard_map/ppermute | solution.py:659
  98.4 1.0 gather.3
  (4 shorter events, 0.0 us)
Async XLA Ops:
  22.9 16.1 %collective-permute-start.1 = (bf16[8,128,256]{2,1,0:T(8,128)(2,1)}, bf16[8,128,256]{2,1,0:T(8,128)(2,1)S(1)}, u32[]{:S(2)}, u32[]{:S(2)}) collective-permute-start(bf16[8,128,256]{2,1,0:T(8,128)(2,1)} %get-tuple-element.32.own_ref), channel_id=1, source_target_pairs={{0,4},{4,0},{8,12},{12,8},{16,20},{20,16},{24,28},{28,24},{1,5},{5... | collective-permute-start | bytes 1572872 | tf_op jit(solution)/shard_map/ppermute | solution.py:633
  24.5 14.6 %copy-start.4 = (bf16[8,128,256]{2,1,0:T(8,128)(2,1)S(1)}, bf16[8,128,256]{2,1,0:T(8,128)(2,1)}, u32[]{:S(2)}) copy-start(bf16[8,128,256]{2,1,0:T(8,128)(2,1)} %get-tuple-element.32.own_ref) | copy-start | bytes 1572868
  38.4 13.7 %collective-permute-start = (bf16[8,128,256]{2,1,0:T(8,128)(2,1)}, bf16[8,128,256]{2,1,0:T(8,128)(2,1)S(1)}, u32[]{:S(2)}, u32[]{:S(2)}) collective-permute-start(bf16[8,128,256]{2,1,0:T(8,128)(2,1)} %get-tuple-element.31.own_ref), channel_id=1, source_target_pairs={{0,4},{4,0},{8,12},{12,8},{16,20},{20,16},{24,28},{28,24},{1,5},{5... | collective-permute-start | bytes 1572872 | tf_op jit(solution)/shard_map/ppermute | solution.py:633
  39.0 2.2 %copy-start = (bf16[4,512,1024]{2,1,0:T(8,128)(2,1)S(1)}, bf16[4,512,1024]{2,1,0:T(8,128)(2,1)}, u32[]{:S(2)}) copy-start(bf16[4,512,1024]{2,1,0:T(8,128)(2,1)} %get-tuple-element.30.rest_0_.refs_1_) | copy-start | bytes 12582916
  41.2 10.9 %copy-start.3 = (bf16[8,128,256]{2,1,0:T(8,128)(2,1)S(1)}, bf16[8,128,256]{2,1,0:T(8,128)(2,1)}, u32[]{:S(2)}) copy-start(bf16[8,128,256]{2,1,0:T(8,128)(2,1)} %get-tuple-element.31.own_ref) | copy-start | bytes 1572868
  41.5 7.6 %collective-permute-start.2 = (bf16[8,128,128]{2,1,0:T(8,128)(2,1)S(1)}, bf16[8,128,128]{2,1,0:T(8,128)(2,1)S(1)}, u32[]{:S(2)}, u32[]{:S(2)}) collective-permute-start(bf16[8,128,128]{2,1,0:T(8,128)(2,1)S(1)} %get-tuple-element.34.refs_0_), channel_id=1, source_target_pairs={{0,8},{4,12},{8,0},{12,4},{16,24},{20,28},{24,16},{28,20},{1,9},{5... | collective-permute-start | bytes 786440 | tf_op jit(solution)/shard_map/ppermute | solution.py:619
  49.3 3.6 %collective-permute-start.4 = (bf16[8,128,128]{2,1,0:T(8,128)(2,1)S(1)}, bf16[8,128,128]{2,1,0:T(8,128)(2,1)S(1)}, u32[]{:S(2)}, u32[]{:S(2)}) collective-permute-start(bf16[8,128,128]{2,1,0:T(8,128)(2,1)S(1)} %hop.4.rest_0_), channel_id=1, source_target_pairs={{0,0},{4,4},{8,16},{12,20},{16,8},{20,12},{24,24},{28,28},{1,1},{5... | collective-permute-start | bytes 786440 | tf_op jit(solution)/shard_map/ppermute | solution.py:619
  52.4 8.0 %collective-permute-start.3 = (bf16[8,128,128]{2,1,0:T(8,128)(2,1)S(1)}, bf16[8,128,128]{2,1,0:T(8,128)(2,1)S(1)}, u32[]{:S(2)}, u32[]{:S(2)}) collective-permute-start(bf16[8,128,128]{2,1,0:T(8,128)(2,1)S(1)} %get-tuple-element.35.refs_0_), channel_id=1, source_target_pairs={{0,8},{4,12},{8,0},{12,4},{16,24},{20,28},{24,16},{28,20},{1,9},{5... | collective-permute-start | bytes 786440 | tf_op jit(solution)/shard_map/ppermute | solution.py:619
  53.2 11.8 %collective-permute-start.6 = (bf16[8,128,128]{2,1,0:T(8,128)(2,1)S(1)}, bf16[8,128,128]{2,1,0:T(8,128)(2,1)S(1)}, u32[]{:S(2)}, u32[]{:S(2)}) collective-permute-start(bf16[8,128,128]{2,1,0:T(8,128)(2,1)S(1)} %hop.5.refs_2_), channel_id=1, source_target_pairs={{0,0},{4,4},{8,8},{12,12},{16,24},{20,28},{24,16},{28,20},{1,1},{5... | collective-permute-start | bytes 786440 | tf_op jit(solution)/shard_map/ppermute | solution.py:619
  60.6 8.2 %collective-permute-start.5 = (bf16[8,128,128]{2,1,0:T(8,128)(2,1)S(1)}, bf16[8,128,128]{2,1,0:T(8,128)(2,1)S(1)}, u32[]{:S(2)}, u32[]{:S(2)}) collective-permute-start(bf16[8,128,128]{2,1,0:T(8,128)(2,1)S(1)} %hop.6.refs_6_), channel_id=1, source_target_pairs={{0,0},{4,4},{8,16},{12,20},{16,8},{20,12},{24,24},{28,28},{1,1},{5... | collective-permute-start | bytes 786440 | tf_op jit(solution)/shard_map/ppermute | solution.py:619
  61.4 16.0 %copy-start.1 = (bf16[4,512,1024]{2,1,0:T(8,128)(2,1)S(1)}, bf16[4,512,1024]{2,1,0:T(8,128)(2,1)}, u32[]{:S(2)}) copy-start(bf16[4,512,1024]{2,1,0:T(8,128)(2,1)} %get-tuple-element.30.rest_0_.refs_1_) | copy-start | bytes 12582916
  64.9 2.2 %copy-start.2 = (bf16[4,512,1024]{2,1,0:T(8,128)(2,1)S(1)}, bf16[4,512,1024]{2,1,0:T(8,128)(2,1)}, u32[]{:S(2)}) copy-start(bf16[4,512,1024]{2,1,0:T(8,128)(2,1)} %get-tuple-element.29.refs_8_.refs_1_) | copy-start | bytes 12582916
  69.1 8.3 %collective-permute-start.7 = (bf16[8,128,128]{2,1,0:T(8,128)(2,1)S(1)}, bf16[8,128,128]{2,1,0:T(8,128)(2,1)S(1)}, u32[]{:S(2)}, u32[]{:S(2)}) collective-permute-start(bf16[8,128,128]{2,1,0:T(8,128)(2,1)S(1)} %hop.7.refs_6_), channel_id=1, source_target_pairs={{0,0},{4,4},{8,8},{12,12},{16,24},{20,28},{24,16},{28,20},{1,1},{5... | collective-permute-start | bytes 786440 | tf_op jit(solution)/shard_map/ppermute | solution.py:619
  72.8 8.1 %collective-permute-start.11 = (bf16[128,1024]{1,0:T(8,128)(2,1)S(1)}, bf16[128,1024]{1,0:T(8,128)(2,1)S(1)}, u32[]{:S(2)}, u32[]{:S(2)}) collective-permute-start(bf16[128,1024]{1,0:T(8,128)(2,1)S(1)} %get-tuple-element.42), channel_id=1, source_target_pairs={{0,1},{1,0},{2,3},{3,2},{4,5},{5,4},{6,7},{7,6},{8,9},{9,8},{10,11... | collective-permute-start | bytes 786440 | tf_op jit(solution)/shard_map/ppermute | solution.py:659
  72.9 9.2 %collective-permute-start.12 = (bf16[128,1024]{1,0:T(8,128)(2,1)S(1)}, bf16[128,1024]{1,0:T(8,128)(2,1)S(1)}, u32[]{:S(2)}, u32[]{:S(2)}) collective-permute-start(bf16[128,1024]{1,0:T(8,128)(2,1)S(1)} %get-tuple-element.43), channel_id=1, source_target_pairs={{0,2},{1,3},{2,0},{3,1},{4,6},{5,7},{6,4},{7,5},{8,10},{9,11},{10,... | collective-permute-start | bytes 786440 | tf_op jit(solution)/shard_map/ppermute | solution.py:659
  74.4 12.3 %collective-permute-start.13 = (bf16[128,1024]{1,0:T(8,128)(2,1)S(1)}, bf16[128,1024]{1,0:T(8,128)(2,1)S(1)}, u32[]{:S(2)}, u32[]{:S(2)}) collective-permute-start(bf16[128,1024]{1,0:T(8,128)(2,1)S(1)} %get-tuple-element.44), channel_id=1, source_target_pairs={{0,3},{1,2},{2,1},{3,0},{4,7},{5,6},{6,5},{7,4},{8,11},{9,10},{10,... | collective-permute-start | bytes 786440 | tf_op jit(solution)/shard_map/ppermute | solution.py:659
  79.1 13.2 %collective-permute-start.10 = (bf16[128,1024]{1,0:T(8,128)(2,1)S(1)}, bf16[128,1024]{1,0:T(8,128)(2,1)S(1)}, u32[]{:S(2)}, u32[]{:S(2)}) collective-permute-start(bf16[128,1024]{1,0:T(8,128)(2,1)S(1)} %get-tuple-element.41), channel_id=1, source_target_pairs={{0,3},{1,2},{2,1},{3,0},{4,7},{5,6},{6,5},{7,4},{8,11},{9,10},{10,... | collective-permute-start | bytes 786440 | tf_op jit(solution)/shard_map/ppermute | solution.py:659
  79.2 13.2 %collective-permute-start.8 = (bf16[128,1024]{1,0:T(8,128)(2,1)S(1)}, bf16[128,1024]{1,0:T(8,128)(2,1)S(1)}, u32[]{:S(2)}, u32[]{:S(2)}) collective-permute-start(bf16[128,1024]{1,0:T(8,128)(2,1)S(1)} %get-tuple-element.39), channel_id=1, source_target_pairs={{0,1},{1,0},{2,3},{3,2},{4,5},{5,4},{6,7},{7,6},{8,9},{9,8},{10,11... | collective-permute-start | bytes 786440 | tf_op jit(solution)/shard_map/ppermute | solution.py:659
  80.8 17.6 %collective-permute-start.9 = (bf16[128,1024]{1,0:T(8,128)(2,1)S(1)}, bf16[128,1024]{1,0:T(8,128)(2,1)S(1)}, u32[]{:S(2)}, u32[]{:S(2)}) collective-permute-start(bf16[128,1024]{1,0:T(8,128)(2,1)S(1)} %get-tuple-element.40), channel_id=1, source_target_pairs={{0,2},{1,3},{2,0},{3,1},{4,6},{5,7},{6,4},{7,5},{8,10},{9,11},{10,... | collective-permute-start | bytes 786440 | tf_op jit(solution)/shard_map/ppermute | solution.py:659

commit v3 on v2

--- a/solution.py
+++ b/solution.py
@@ -14,6 +14,8 @@
 MEG = 1024 * 1024
 FINISH = 16
 LOCAL = 62.25
+PARTS = 1
+SIDE = 4
 GATHER = 8
 
 
@@ -48,6 +50,7 @@
 
 def split(heads, shares):
     counts = [heads * share // sum(shares) for share in shares]
+    counts[-1] = heads - sum(counts[:-1])
     return [(sum(counts[:g]), n) for g, n in enumerate(counts)]
 
 
@@ -75,15 +78,16 @@
     if solve:
         names = ["weight", "ld", "wr", "k", "q", "v"]
     inputs, refs = dict(zip(names, refs)), refs[len(names):]
-    run_ref, term_hbm, refs = refs[0], refs[1], refs[2:]
+    run_ref, term_hbm, mark_ref, refs = *refs[:3], refs[3:]
+    mark_ref[...] = jnp.zeros_like(mark_ref)
     if solve:
         row_s, colg_s, kn_hbm, t_hbm, refs = *refs[:4], refs[4:]
         ld_s, wr_s, k_s, low_s, inv_s, colb_s, key_sem, refs = *refs[:7], refs[7:]
     else:
         row_s, colg_s = inputs["row"], inputs["col"]
     (
-        weight_s, q_s, v_s, kn_s, gram_s, scale_s, m_s, s_s, qt_s, near_s, p_s, term_s, copy_sem,
-        keep_sem, step_sem,
+        weight_s, q_s, v_s, kn_s, gram_s, scale_s, m_s, fall_s, s_s, qt_s, near_s, p_s, term_s, copy_sem,
+        pair_sem, keep_sem, step_sem,
     ) = refs
     tokens = q_s.shape[0]
     pairs = tokens // WIDE
@@ -93,19 +97,31 @@
     across = heads if solve else count
     mine = slice(first * WIDE, (first + count) * WIDE)
 
-    loads = {
-        "weight": (inputs["weight"], weight_s),
-        "q": (inputs["q"].at[:, mine], q_s),
-        "v": (inputs["v"].at[:, mine], v_s),
-    }
+    loads = {"weight": (inputs["weight"], weight_s)}
     if solve:
         loads.update(ld=(inputs["ld"], ld_s), wr=(inputs["wr"], wr_s))
-    else:
-        loads["kn"] = (inputs["kn"].at[first:first + count], kn_s)
-        for p in range(pairs):
-            at = (p * heads + first) * BLOCK
-            part = slice(p * count * BLOCK, (p + 1) * count * BLOCK)
-            loads["t", p] = (inputs["t"].at[at:at + count * BLOCK], gram_s.at[part])
+
+    def pair_copies(p):
+        toks = aligned(p, WIDE)
+        copies = [
+            (inputs["q"].at[toks, mine], q_s.at[toks, :]),
+            (inputs["v"].at[toks, mine], v_s.at[toks, :]),
+        ]
+        if not solve:
+            size = count * BLOCK
+            at = pl.ds(pl.multiple_of((p * heads + first) * BLOCK, BLOCK), size)
+            copies += [
+                (inputs["kn"].at[first:first + count, toks, :], kn_s.at[:, toks, :]),
+                (inputs["t"].at[at, :], gram_s.at[aligned(p, size), :]),
+            ]
+        return [
+            pltpu.make_async_copy(x, y, pair_sem.at[p, i]) for i, (x, y) in enumerate(copies)
+        ]
+
+    if solve:
+        for i, name in enumerate(("q", "v")):
+            loads[name] = (inputs[name].at[:, mine], (q_s, v_s)[i])
+
     loads = {
         name: pltpu.make_async_copy(x, y, copy_sem.at[i])
         for i, (name, (x, y)) in enumerate(loads.items())
@@ -121,6 +137,10 @@
         loads["wr"].start()
         for i in range(4):
             key_copy(i).start()
+    if not solve:
+        for p in range(pairs):
+            for c in pair_copies(p):
+                c.start()
     for name, c in loads.items():
         if name not in ("ld", "wr"):
             c.start()
@@ -227,18 +247,14 @@
         kept = [pltpu.make_async_copy(x, y, keep_sem.at[i]) for i, (x, y) in enumerate(kept)]
         for c in kept:
             c.start()
-    for name, c in loads.items():
-        if name not in ("ld", "wr", "weight"):
-            c.wait()
     clane = lax.broadcasted_iota(jnp.int32, (BLOCK, lanes), 1)
     lane = lax.broadcasted_iota(jnp.int32, (BLOCK, WIDE), 1)
     row64 = lax.broadcasted_iota(jnp.int32, (BLOCK, WIDE), 0)
     keep = row64 >= jnp.where(left, lane, lane - BLOCK)
     eye = ri == ci
 
-    def unit(i):
-        p = i // count
-        h = i - p * count
+    def unit(p, h):
+        i = p * count + h
         u = p * heads + first + h
         grow = row_s[pl.ds(u, 1), :]
         gs = [column(colg_s[...], clane, u), column(colg_s[...], clane, u + units)]
@@ -271,14 +287,24 @@
         yield
         for half, (end, y) in enumerate(outs):
             s_s[2 * p + half, h] = y[:, :WIDE]
-            m = jnp.where(eye, jnp.exp(end), 0.0) - y[:, WIDE:]
-            m_hi, m_lo = halves(m)
-            m_s[2 * p + half, h] = jnp.concatenate([m_hi, m_lo], axis=1)
+            m_s[2 * p + half, h] = y[:, WIDE:].astype(bf16)
+            fall_s[2 * p + half, pl.ds(h, 1), :] = jnp.exp(end)
         near_s[i] = ys[:, :WIDE]
         eg = jnp.exp(jnp.concatenate(gs, axis=0))
         qt_s[i] = (eg * q.astype(f32) - ys[:, WIDE:]).astype(bf16)
 
-    repeat(pairs * count, unit, 8)
+    if solve:
+        loads["q"].wait()
+        loads["v"].wait()
+
+    def pair_units(p, _):
+        if not solve:
+            for c in pair_copies(p):
+                c.wait()
+        repeat(count, lambda h: unit(p, h), 8)
+        return 0
+
+    lax.fori_loop(0, pairs, pair_units, 0)
 
     loads["weight"].wait()
     slots = weight_s.shape[0]
@@ -300,9 +326,8 @@
             term_s[b, i, :, cols] = ((rows if i else near) * scale[:, at:at + 1]).astype(bf16)
 
     for h in range(count):
-        m = m_s[0, h]
         p_s[h, :, :WIDE] = s_s[0, h]
-        p_s[h, :, WIDE:] = m[:, :WIDE].astype(f32) + m[:, WIDE:].astype(f32)
+        p_s[h, :, WIDE:] = jnp.where(eye, fall_s[0, h:h + 1, :], 0.0) - m_s[0, h].astype(f32)
         write(0, h, near_s[h, :BLOCK, :], qt_s[h, :BLOCK, :].astype(f32))
     term_copy(0).start()
 
@@ -311,20 +336,18 @@
 
         def advance(h):
             i = (b // 2) * count + h
-            p_hi, p_lo = halves(p_s[h])
-            m = m_s[b, h]
-            n = mxu(
-                jnp.concatenate([m, m[:, :WIDE]], axis=1),
-                jnp.concatenate([p_hi, p_hi, p_lo], axis=0),
+            both = mxu(
+                jnp.concatenate([m_s[b, h], qt_s[i, half, :]], axis=0), p_s[h].astype(bf16)
             )
-            o = mxu(qt_s[i, half, :], p_hi)
             yield
-            p_s[h, :, :WIDE] = n[:, :WIDE] + s_s[b, h]
-            p_s[h, :, WIDE:] = n[:, WIDE:]
+            fall = fall_s[b, h:h + 1, :]
+            n, o = both[:WIDE], both[WIDE:]
+            p_s[h, :, :WIDE] = fall * p_s[h, :, :WIDE] + s_s[b, h] - n[:, :WIDE]
+            p_s[h, :, WIDE:] = fall * p_s[h, :, WIDE:] - n[:, WIDE:]
             write(b, h, near_s[i, half, :] + o[:, :WIDE], o[:, WIDE:])
 
-        for h in range(0, count, 4):
-            together([advance(h + j) for j in range(min(4, count - h))])
+        for h in range(0, count, SIDE):
+            together([advance(h + j) for j in range(min(SIDE, count - h))])
         term_copy(b).start()
         return 0
 
@@ -348,10 +371,11 @@
     vmem = pl.BlockSpec(memory_space=pltpu.VMEM)
     hbm = pl.BlockSpec(memory_space=pltpu.HBM)
     after, spaces = waits(after)
-    out_specs = [vmem, hbm]
+    out_specs = [vmem, hbm, vmem]
     out_shape = [
         jax.ShapeDtypeStruct((count, WIDE, 2 * WIDE), bf16),
         jax.ShapeDtypeStruct((1 + depth, tokens, count * WIDE), bf16),
+        jax.ShapeDtypeStruct((8, WIDE), f32),
     ]
     scratch = []
     if solve:
@@ -395,13 +419,15 @@
             pltpu.VMEM((across, tokens, WIDE), bf16),
             pltpu.VMEM((across * pairs * BLOCK, WIDE), f32),
             pltpu.VMEM((tokens, weights.shape[0]), f32),
-            pltpu.VMEM((blocks, count, WIDE, 2 * WIDE), bf16),
+            pltpu.VMEM((blocks, count, WIDE, WIDE), bf16),
+            pltpu.VMEM((blocks, count, WIDE), f32),
             pltpu.VMEM((blocks, count, WIDE, WIDE), f32),
             pltpu.VMEM((pairs * count, WIDE, WIDE), bf16),
             pltpu.VMEM((pairs * count, WIDE, WIDE), f32),
             pltpu.VMEM((count, WIDE, 2 * WIDE), f32),
             pltpu.VMEM((blocks, 1 + depth, BLOCK, count * WIDE), bf16),
-            pltpu.SemaphoreType.DMA((5 + pairs,)),
+            pltpu.SemaphoreType.DMA((5,)),
+            pltpu.SemaphoreType.DMA((pairs, 4)),
             pltpu.SemaphoreType.DMA((2,)),
             pltpu.SemaphoreType.DMA((blocks,)),
         ],
@@ -483,7 +509,24 @@
     )(m, *operands, *after)
 
 
-def finish_kernel(size, shape, here_ref, term_ref, other_ref, *refs):
+def stage_kernel(from_ref, *refs):
+    refs[-1][...] = from_ref[...]
+
+
+def stage_call(terms, after):
+    vmem = pl.BlockSpec(memory_space=pltpu.VMEM)
+    after, spaces = waits(after)
+    return pl.pallas_call(
+        stage_kernel,
+        in_specs=[vmem] + spaces,
+        out_specs=vmem,
+        out_shape=jax.ShapeDtypeStruct(terms.shape, terms.dtype),
+        compiler_params=pltpu.CompilerParams(vmem_limit_bytes=16 * MEG),
+        name="stage",
+    )(terms, *after)
+
+
+def finish_kernel(span, size, shape, here_ref, term_ref, other_ref, *refs):
     entries, at = [], 0
     for count in shape:
         entries.append(refs[at:at + count])
@@ -491,14 +534,14 @@
     outs = refs[at:at + size]
     depth, tokens, width = term_ref.shape
     chunk = tokens // size
-    heads = width // WIDE
+    heads = range(span[0], sum(span))
     here = here_ref[0]
     position = here_ref[1]
     zero = jnp.zeros((WIDE, WIDE), bf16)
     odd = (position & 1) == 1
     pair = position >> 1
     carries = []
-    for h in range(heads):
+    for h in heads:
         came = []
         for m, options in enumerate(entries):
             entry = zero
@@ -521,14 +564,15 @@
         def head(h):
             part = slice(h * WIDE, (h + 1) * WIDE)
             far = jnp.concatenate([term_ref[i, toks, part] for i in range(1, depth)], axis=1)
-            total = mxu(far, carries[h])
+            total = mxu(far, carries[h - span[0]])
             yield
-            outs[d][:, part] = (total + term_ref[0, toks, part].astype(f32)).astype(bf16)
-
-        together([head(h) for h in range(heads)])
-
-
-def finish_call(size, here, terms, other, entries, after):
+            out = slice((h - span[0]) * WIDE, (h - span[0] + 1) * WIDE)
+            outs[d][:, out] = (total + term_ref[0, toks, part].astype(f32)).astype(bf16)
+
+        together([head(h) for h in heads])
+
+
+def finish_call(span, size, here, terms, other, entries, after):
     depth, tokens, width = terms.shape
     smem = pl.BlockSpec(memory_space=pltpu.SMEM)
     vmem = pl.BlockSpec(memory_space=pltpu.VMEM)
@@ -538,65 +582,71 @@
 
     def kernel(*refs):
         used = 3 + len(flat)
-        finish_kernel(size, shape, *refs[:used], *refs[used + len(after):])
+        finish_kernel(span, size, shape, *refs[:used], *refs[used + len(after):])
 
     return pl.pallas_call(
         kernel,
         in_specs=[smem] + [vmem] * (2 + len(flat)) + spaces,
         out_specs=[vmem] * size,
-        out_shape=[jax.ShapeDtypeStruct((tokens // size, width), bf16)] * size,
+        out_shape=[jax.ShapeDtypeStruct((tokens // size, span[1] * WIDE), bf16)] * size,
         compiler_params=pltpu.CompilerParams(vmem_limit_bytes=FINISH * MEG),
         name="finish",
     )(here, terms, other, *flat, *after)
 
 
-def gather_kernel(first, heads, size, place_ref, *refs):
-    parts, (out_ref, sems) = refs[:size], refs[-2:]
+def gather_kernel(first, heads, sources, place_ref, *refs):
+    parts, (out_ref, mark_ref, sems) = refs[:len(sources)], refs[-3:]
+    mark_ref[...] = jnp.zeros_like(mark_ref)
     here = place_ref[0]
     copies = []
-    for d, ref in enumerate(parts):
+    for i, (d, ref) in enumerate(zip(sources, parts)):
         col = pl.multiple_of(((here ^ d) * heads + first) * WIDE, WIDE)
         where = out_ref.at[:, pl.ds(col, ref.shape[1])]
-        copies.append(pltpu.make_async_copy(ref, where, sems.at[d]))
+        copies.append(pltpu.make_async_copy(ref, where, sems.at[i]))
         copies[-1].start()
     for c in copies:
         c.wait()
 
 
-def gather_call(first, heads, place, parts, before, after):
-    size = len(parts)
+def gather_call(first, heads, size, place, parts, before, after):
+    sources, parts = zip(*parts)
+    count = len(parts)
     vmem = pl.BlockSpec(memory_space=pltpu.VMEM)
     hbm = pl.BlockSpec(memory_space=pltpu.HBM)
     after, spaces = waits(after)
     kept = [] if before is None else [before]
 
     def kernel(*refs):
-        gather_kernel(first, heads, size, *refs)
+        gather_kernel(first, heads, sources, *refs)
 
     return pl.pallas_call(
         kernel,
-        in_specs=[pl.BlockSpec(memory_space=pltpu.SMEM)] + [vmem] * size + [hbm] * len(kept)
+        in_specs=[pl.BlockSpec(memory_space=pltpu.SMEM)] + [vmem] * count + [hbm] * len(kept)
         + spaces,
-        out_specs=hbm,
-        out_shape=jax.ShapeDtypeStruct((parts[0].shape[0], heads * size * WIDE), bf16),
-        input_output_aliases={1 + size: 0} if kept else {},
-        scratch_shapes=[pltpu.SemaphoreType.DMA((size,))],
+        out_specs=[hbm, vmem],
+        out_shape=[
+            jax.ShapeDtypeStruct((parts[0].shape[0], heads * size * WIDE), bf16),
+            jax.ShapeDtypeStruct((8, WIDE), f32),
+        ],
+        input_output_aliases={1 + count: 0} if kept else {},
+        scratch_shapes=[pltpu.SemaphoreType.DMA((count,))],
         compiler_params=pltpu.CompilerParams(vmem_limit_bytes=GATHER * MEG),
         name="gather",
     )(place, *parts, *kept, *after)
 
 
-ORDER = ("l0", "l1", "p0", "h01", "p1", "h02", "h11", "f0", "h12", "f1", "g0", "g1")
+ORDER = ("l0", "l1", "p0", "t0", "h01", "p1", "h02", "h11", "f00")
+ORDER += ("h12", "a00", "f10", "b00", "a10", "b10")
 
 
 def order(groups, steps):
-    names = dict(l="local", p="pair", h="hop", f="finish", g="gather")
+    names = dict(l="local", p="pair", t="stage", h="hop", f="finish", g="gather", a="some", b="rest")
     if steps == 3:
         return [(names[x[0]], int(x[1]), int(x[2:] or 0)) for x in ORDER]
     out = [("local", g, 0) for g in range(groups)] + [("pair", g, 0) for g in range(groups)]
     out += [("hop", g, step) for step in range(1, steps) for g in range(groups)]
-    out += [("finish", g, 0) for g in range(groups)]
-    return out + [("gather", g, 0) for g in range(groups)]
+    out += [("finish", g, i) for g in range(groups) for i in range(PARTS)]
+    return out + [("gather", g, i) for g in range(groups) for i in range(PARTS)]
 
 
 def per_device(queries, key_rows, value_rows, log_decay, write_rate, level_weights, block_levels):
@@ -624,14 +674,14 @@
     after = []
 
     def local(g):
-        runs[g], terms[g], *kept = local_call(
+        runs[g], terms[g], mark, *kept = local_call(
             groups[g], heads, bits, block_levels, level_weights.T, solved[0] if solved else None,
             [log_decay.T, write_rate.T, key_rows], queries, value_rows, after,
         )
         if kept:
             solved.append(kept)
         others[g] = lax.ppermute(runs[g], "ctx", [(i, i ^ 1) for i in range(size)])
-        return terms[g], pltpu.HBM
+        return mark, pltpu.VMEM
 
     def pair(g):
         states[g] = pair_call(flag, runs[g], others[g], after)
@@ -652,16 +702,26 @@
         entries[g][m].append(swap(low, sent))
         return sent, pltpu.VMEM
 
-    def finish(g):
-        outs = finish_call(width, here, terms[g], others[g], entries[g], after)
+    def stage(g):
+        terms[g] = stage_call(terms[g], after)
+        return terms[g], pltpu.VMEM
+
+    def span_of(g, part):
+        return split(groups[g][1], (1,) * PARTS)[part]
+
+    def finish(g, part):
+        outs = finish_call(
+            span_of(g, part), width, here, terms[g], others[g], entries[g], after
+        )
         for d in range(width):
             pairing = [(i, i ^ d) for i in range(width)]
-            pieces[g, d] = outs[d] if d == 0 else lax.ppermute(outs[d], "head", pairing)
+            pieces[g, part, d] = outs[d] if d == 0 else lax.ppermute(outs[d], "head", pairing)
         return outs[0], pltpu.VMEM
 
-    def gather(g, out):
-        parts = [pieces[g, d] for d in range(width)]
-        return gather_call(groups[g][0], heads, place.reshape(1), parts, out, after)
+    def gather(g, part, out, ds):
+        parts = [(d, pieces[g, part, d]) for d in ds]
+        first = groups[g][0] + span_of(g, part)[0]
+        return gather_call(first, heads, width, place.reshape(1), parts, out, after)
 
     out = None
     for name, g, step in order(len(groups), len(steps)):
@@ -670,13 +730,17 @@
         elif name == "pair":
             token = pair(g)
             hop(g, 0)
+        elif name == "stage":
+            token = stage(g)
         elif name == "hop":
             token = hop(g, step)
         elif name == "finish":
-            token = finish(g)
+            token = finish(g, step)
         else:
-            out = gather(g, out)
-            token = out, pltpu.HBM
+            cut = width - 1
+            ds = dict(some=range(cut), rest=range(cut, width)).get(name, range(width))
+            out, mark = gather(g, step, out, ds)
+            token = mark, pltpu.VMEM
         after = [token]
     return out
 

time: 99.7 us -> 95.2 us (0.955)
  starting transfers between devices: 19.6 us -> 16.2 us
    pallas_call x2, Pallas kernels: 36.9 us -> 33.3 us  [local_call(): pl.pallas_call(kernel, in_specs=[smem] + in_specs + spaces, out_specs=out...]
    ppermute x6, starting transfers between devices: 13.3 us -> 10.3 us  [swap(): lax.ppermute(array, 'ctx', [(i, 2 * to[i >> 1] + (i & 1)) for i in range(...]
    pallas_call x2 -> x4, Pallas kernels: 1.11 us -> 3.81 us  [gather_call(): pl.pallas_call(kernel, in_specs=[pl.BlockSpec(memory_space=pltpu.SMEM)] +...]
    ppermute x2, waiting for transfers between devices: 2.1 us -> 3.71 us  [local(): others[g] = lax.ppermute(runs[g], 'ctx', [(i, i ^ 1) for i in range(size)])]
    ppermute x6, waiting for transfers between devices: 13.2 us -> 11.7 us  [swap(): lax.ppermute(array, 'ctx', [(i, 2 * to[i >> 1] + (i & 1)) for i in range(...]
    unnamed x11 -> x14, local copies, waits for them, and re-layouts: 5.71 us -> 5.07 us
  transfers between devices with their start and end apart: 14 -> 14, of which waited for: 8 -> 9; matrix products, arithmetic and copies ran while one was open for 1% -> 0% of each run, Pallas kernels for 19% -> 21%
where the time goes in v3:
time: 95.2 us; the launch traced here: 94.5 us
  Pallas kernels  42.3 us (44%)
  waiting for transfers between devices  30.7 us (32%)
  starting transfers between devices  16.2 us (17%)
  local copies, waits for them, and re-layouts  5.07 us (5%)
    pallas_call x2, Pallas kernels, local_call(): pl.pallas_call(kernel, in_specs=[smem] + in_specs + spaces, out_specs=out...  33.3 us
    ppermute x6, waiting for transfers between devices, finish(): lax.ppermute(outs[d], 'head', pairing)  15.3 us
    ppermute x6, waiting for transfers between devices, swap(): lax.ppermute(array, 'ctx', [(i, 2 * to[i >> 1] + (i & 1)) for i in range(...  11.7 us
    ppermute x6, starting transfers between devices, swap(): lax.ppermute(array, 'ctx', [(i, 2 * to[i >> 1] + (i & 1)) for i in range(...  10.3 us
    unnamed x14, local copies, waits for them, and re-layouts  5.07 us
    pallas_call x4, Pallas kernels, gather_call(): pl.pallas_call(kernel, in_specs=[pl.BlockSpec(memory_space=pltpu.SMEM)] +...  3.81 us
    ppermute x2, waiting for transfers between devices, local(): others[g] = lax.ppermute(runs[g], 'ctx', [(i, i ^ 1) for i in range(size)])  3.71 us
    ppermute x6, starting transfers between devices, finish(): lax.ppermute(outs[d], 'head', pairing)  3.68 us
  transfers between devices with their start and end apart: 14, of which 9 were waited for; matrix products, arithmetic and copies ran while one was open for 0% of the time, Pallas kernels for 21%

profile of v3, /device:TPU:24, one launch (start us, length us, event | category | flops | bytes accessed | tf_op | source)
XLA Modules:
  0.0 94.5 jit_solution(241503055985241795)
XLA Ops:
  0.0 21.6 %local.2 = (bf16[8,128,256]{2,1,0:T(8,128)(2,1)}, bf16[4,512,1024]{2,1,0:T(8,128)(2,1)}, f32[8,128]{1,0:T(8,128)}, f32[64,128]{1,0:T(8,128)}, f32[64,128]{1,0:T(...) custom-call(s32[8]{0:T(128)} %refs_0_.3, f32[80,512]{1,0:T(8,128)} %bitcast.6, f32[16,512]{1,0:T(8,128)} %bitcast.8, ...), custom_call_target="tpu_custom_call" | custom-call | tf_op jit(solution)/shard_map/local/pallas_call | solution.py:409
  21.6 1.6 %collective-permute-start.1 = (bf16[8,128,256]{2,1,0:T(8,128)(2,1)}, bf16[8,128,256]{2,1,0:T(8,128)(2,1)S(1)}, u32[]{:S(2)}, u32[]{:S(2)}) collective-permute-start(bf16[8,128,256]{2,1,0:T(8,128)(2,1)} %get-tuple-element.41.own_ref), channel_id=1, source_target_pairs={{0,4},{4,0},{8,12},{12,8},{16,20},{20,16},{24,28},{28,24},{1,5},{5... | collective-permute-start | bytes 1572872 | tf_op jit(solution)/shard_map/ppermute | solution.py:683
  23.2 11.7 %local.3 = (bf16[8,128,256]{2,1,0:T(8,128)(2,1)}, bf16[4,512,1024]{2,1,0:T(8,128)(2,1)}, f32[8,128]{1,0:T(8,128)}) custom-call(s32[8]{0:T(128)} %refs_0_.3, f32[80,512]{1,0:T(8,128)} %bitcast.7, f32[64,128]{1,0:T(8,128)} %get-tuple-element.34.refs_2_, f32[64,128]{1,0:T(8,128)} %get-tuple-element.35.refs_3_, bf16[16,512,128]{2,1,0:T(8,128)(2,1)} %get-tuple-element.36.refs_4_, ...), custom_call_target="tpu_custom_call" | custom-call | tf_op jit(solution)/shard_map/local/pallas_call | solution.py:409
  34.9 0.6 collective-permute-start
  35.5 0.1 collective-permute-done.1.other_ref.refs_2_
  35.6 0.0 copy-done.5
  35.6 0.7 copy-done.6
  36.2 0.3 pair.2
  36.5 0.5 collective-permute-start.2
  37.1 2.2 %copy-done.3 = bf16[4,512,1024]{2,1,0:T(8,128)(2,1)S(1)} copy-done((bf16[4,512,1024]{2,1,0:T(8,128)(2,1)S(1)}, bf16[4,512,1024]{2,1,0:T(8,128)(2,1)}, u32[]{:S(2)}) %copy-start.3) | copy-done | bytes 4194328
  39.3 0.3 stage.1.refs_2_.refs_1_
  39.5 4.5 %collective-permute-done.2.refs_1_.refs_3_ = bf16[8,128,128]{2,1,0:T(8,128)(2,1)S(1)} collective-permute-done((bf16[8,128,128]{2,1,0:T(8,128)(2,1)S(1)}, bf16[8,128,128]{2,1,0:T(8,128)(2,1)S(1)}, u32[]{:S(2)}, u32[]{:S(2)}) %collective-permute-start.2) | collective-permute-done | bytes 262176 | tf_op jit(solution)/shard_map/ppermute | solution.py:669
  44.0 0.2 hop.4.rest_0_
  44.2 0.7 collective-permute-start.4
  44.9 3.6 %collective-permute-done.other_ref.refs_2_ = bf16[8,128,256]{2,1,0:T(8,128)(2,1)S(1)} collective-permute-done((bf16[8,128,256]{2,1,0:T(8,128)(2,1)}, bf16[8,128,256]{2,1,0:T(8,128)(2,1)S(1)}, u32[]{:S(2)}, u32[]{:S(2)}) %collective-permute-start) | collective-permute-done | bytes 524320 | tf_op jit(solution)/shard_map/ppermute | solution.py:683
  48.5 0.3 pair.3
  48.8 0.5 collective-permute-start.3
  49.4 0.0 collective-permute-done.4.refs_0_.refs_4_
  49.4 0.2 hop.5.refs_2_
  49.6 5.6 %collective-permute-start.6 = (bf16[8,128,128]{2,1,0:T(8,128)(2,1)S(1)}, bf16[8,128,128]{2,1,0:T(8,128)(2,1)S(1)}, u32[]{:S(2)}, u32[]{:S(2)}) collective-permute-start(bf16[8,128,128]{2,1,0:T(8,128)(2,1)S(1)} %hop.5.refs_2_), channel_id=1, source_target_pairs={{0,0},{4,4},{8,8},{12,12},{16,24},{20,28},{24,16},{28,20},{1,1},{5... | collective-permute-start | bytes 786440 | tf_op jit(solution)/shard_map/ppermute | solution.py:669
  55.2 3.0 %collective-permute-done.3.refs_1_.refs_3_ = bf16[8,128,128]{2,1,0:T(8,128)(2,1)S(1)} collective-permute-done((bf16[8,128,128]{2,1,0:T(8,128)(2,1)S(1)}, bf16[8,128,128]{2,1,0:T(8,128)(2,1)S(1)}, u32[]{:S(2)}, u32[]{:S(2)}) %collective-permute-start.3) | collective-permute-done | bytes 262176 | tf_op jit(solution)/shard_map/ppermute | solution.py:669
  58.1 0.2 hop.6.refs_6_
  58.4 0.7 collective-permute-start.5
  59.1 0.1 pad_add_fusion.refs_0_
  59.1 2.2 %collective-permute-done.6.refs_5_ = bf16[8,128,128]{2,1,0:T(8,128)(2,1)S(1)} collective-permute-done((bf16[8,128,128]{2,1,0:T(8,128)(2,1)S(1)}, bf16[8,128,128]{2,1,0:T(8,128)(2,1)S(1)}, u32[]{:S(2)}, u32[]{:S(2)}) %collective-permute-start.6) | collective-permute-done | bytes 262176 | tf_op jit(solution)/shard_map/ppermute | solution.py:669
  61.4 2.2 %copy-done.1 = bf16[4,512,1024]{2,1,0:T(8,128)(2,1)S(1)} copy-done((bf16[4,512,1024]{2,1,0:T(8,128)(2,1)S(1)}, bf16[4,512,1024]{2,1,0:T(8,128)(2,1)}, u32[]{:S(2)}) %copy-start.1) | copy-done | bytes 4194328
  63.6 1.7 %finish.2 = (bf16[128,1024]{1,0:T(8,128)(2,1)S(1)}, bf16[128,1024]{1,0:T(8,128)(2,1)S(1)}, bf16[128,1024]{1,0:T(8,128)(2,1)S(1)}, bf16[128,1024]{1,0:T(8,128)(2,1)S(1)}) custom-call(s32[2]{0:T(128)S(1)} %pad_add_fusion.refs_0_, bf16[4,512,1024]{2,1,0:T(8,128)(2,1)S(1)} %copy-done.1, bf16[8,128,256]{2,1,0:T(8,128)(2,1)S(1)} %collective-permute-done.1.other_ref.refs_2_, ...), custom_call_target="tpu_custom_call" | custom-call | tf_op jit(solution)/shard_map/finish/pallas_call | solution.py:587
  65.3 0.1 collective-permute-start.8
  65.3 1.6 %collective-permute-start.9 = (bf16[128,1024]{1,0:T(8,128)(2,1)S(1)}, bf16[128,1024]{1,0:T(8,128)(2,1)S(1)}, u32[]{:S(2)}, u32[]{:S(2)}) collective-permute-start(bf16[128,1024]{1,0:T(8,128)(2,1)S(1)} %get-tuple-element.50), channel_id=1, source_target_pairs={{0,2},{1,3},{2,0},{3,1},{4,6},{5,7},{6,4},{7,5},{8,10},{9,11},{10,... | collective-permute-start | bytes 786440 | tf_op jit(solution)/shard_map/ppermute | solution.py:718
  66.9 0.0 collective-permute-done.5.refs_0_.refs_4_
  66.9 0.2 hop.7.refs_4_
  67.2 2.4 %collective-permute-start.7 = (bf16[8,128,128]{2,1,0:T(8,128)(2,1)S(1)}, bf16[8,128,128]{2,1,0:T(8,128)(2,1)S(1)}, u32[]{:S(2)}, u32[]{:S(2)}) collective-permute-start(bf16[8,128,128]{2,1,0:T(8,128)(2,1)S(1)} %hop.7.refs_4_), channel_id=1, source_target_pairs={{0,0},{4,4},{8,8},{12,12},{16,24},{20,28},{24,16},{28,20},{1,1},{5... | collective-permute-start | bytes 786440 | tf_op jit(solution)/shard_map/ppermute | solution.py:669
  69.5 0.1 collective-permute-start.13
  69.6 0.0 collective-permute-done.8.refs_2_
  69.6 4.9 %collective-permute-done.9.refs_3_ = bf16[128,1024]{1,0:T(8,128)(2,1)S(1)} collective-permute-done((bf16[128,1024]{1,0:T(8,128)(2,1)S(1)}, bf16[128,1024]{1,0:T(8,128)(2,1)S(1)}, u32[]{:S(2)}, u32[]{:S(2)}) %collective-permute-start.9) | collective-permute-done | bytes 262176 | tf_op jit(solution)/shard_map/ppermute | solution.py:718
  74.5 0.9 gather.4
  75.4 2.0 %collective-permute-done.7.refs_5_ = bf16[8,128,128]{2,1,0:T(8,128)(2,1)S(1)} collective-permute-done((bf16[8,128,128]{2,1,0:T(8,128)(2,1)S(1)}, bf16[8,128,128]{2,1,0:T(8,128)(2,1)S(1)}, u32[]{:S(2)}, u32[]{:S(2)}) %collective-permute-start.7) | collective-permute-done | bytes 262176 | tf_op jit(solution)/shard_map/ppermute | solution.py:669
  77.4 1.8 %finish.3 = (bf16[128,1024]{1,0:T(8,128)(2,1)S(1)}, bf16[128,1024]{1,0:T(8,128)(2,1)S(1)}, bf16[128,1024]{1,0:T(8,128)(2,1)S(1)}, bf16[128,1024]{1,0:T(8,128)(2,1)S(1)}) custom-call(s32[2]{0:T(128)S(1)} %pad_add_fusion.refs_0_, bf16[4,512,1024]{2,1,0:T(8,128)(2,1)S(1)} %copy-done.2, bf16[8,128,256]{2,1,0:T(8,128)(2,1)S(1)} %collective-permute-done.other_ref.refs_2_, ...), custom_call_target="tpu_custom_call" | custom-call | tf_op jit(solution)/shard_map/finish/pallas_call | solution.py:587
  79.2 0.1 collective-permute-start.11
  79.3 0.6 collective-permute-start.12
  79.9 1.3 %collective-permute-start.10 = (bf16[128,1024]{1,0:T(8,128)(2,1)S(1)}, bf16[128,1024]{1,0:T(8,128)(2,1)S(1)}, u32[]{:S(2)}, u32[]{:S(2)}) collective-permute-start(bf16[128,1024]{1,0:T(8,128)(2,1)S(1)} %get-tuple-element.52), channel_id=1, source_target_pairs={{0,3},{1,2},{2,1},{3,0},{4,7},{5,6},{6,5},{7,4},{8,11},{9,10},{10,... | collective-permute-start | bytes 786440 | tf_op jit(solution)/shard_map/ppermute | solution.py:718
  81.2 0.0 collective-permute-done.13.refs_1_
  81.2 0.7 gather.5
  81.9 0.0 collective-permute-done.11.refs_2_
  81.9 6.6 %collective-permute-done.12.refs_3_ = bf16[128,1024]{1,0:T(8,128)(2,1)S(1)} collective-permute-done((bf16[128,1024]{1,0:T(8,128)(2,1)S(1)}, bf16[128,1024]{1,0:T(8,128)(2,1)S(1)}, u32[]{:S(2)}, u32[]{:S(2)}) %collective-permute-start.12) | collective-permute-done | bytes 262176 | tf_op jit(solution)/shard_map/ppermute | solution.py:718
  88.5 0.9 gather.6
  89.4 3.8 %collective-permute-done.10.refs_1_ = bf16[128,1024]{1,0:T(8,128)(2,1)S(1)} collective-permute-done((bf16[128,1024]{1,0:T(8,128)(2,1)S(1)}, bf16[128,1024]{1,0:T(8,128)(2,1)S(1)}, u32[]{:S(2)}, u32[]{:S(2)}) %collective-permute-start.10) | collective-permute-done | bytes 262176 | tf_op jit(solution)/shard_map/ppermute | solution.py:718
  93.2 1.3 %gather.7 = (bf16[128,8192]{1,0:T(8,128)(2,1)}, f32[8,128]{1,0:T(8,128)}) custom-call(s32[1]{0:T(128)} %bitcast.refs_0_, bf16[128,1024]{1,0:T(8,128)(2,1)S(1)} %collective-permute-done.10.refs_1_, bf16[128,8192]{1,0:T(8,128)(2,1)} %get-tuple-element.60.refs_2_, f32[8,128]{1,0:T(8,128)S(1)} %get-tuple-element.61.refs_3_), custom_call_target="tpu_custom_call", output_to_operand_aliasing={{0}: (2, {})} | custom-call | tf_op jit(solution)/shard_map/gather/pallas_call | solution.py:622
  (10 shorter events, 0.0 us)
Async XLA Ops:
  21.6 13.9 %collective-permute-start.1 = (bf16[8,128,256]{2,1,0:T(8,128)(2,1)}, bf16[8,128,256]{2,1,0:T(8,128)(2,1)S(1)}, u32[]{:S(2)}, u32[]{:S(2)}) collective-permute-start(bf16[8,128,256]{2,1,0:T(8,128)(2,1)} %get-tuple-element.41.own_ref), channel_id=1, source_target_pairs={{0,4},{4,0},{8,12},{12,8},{16,20},{20,16},{24,28},{28,24},{1,5},{5... | collective-permute-start | bytes 1572872 | tf_op jit(solution)/shard_map/ppermute | solution.py:683
  23.2 12.4 %copy-start.5 = (bf16[8,128,256]{2,1,0:T(8,128)(2,1)S(1)}, bf16[8,128,256]{2,1,0:T(8,128)(2,1)}, u32[]{:S(2)}) copy-start(bf16[8,128,256]{2,1,0:T(8,128)(2,1)} %get-tuple-element.41.own_ref) | copy-start | bytes 1572868
  34.9 13.7 %collective-permute-start = (bf16[8,128,256]{2,1,0:T(8,128)(2,1)}, bf16[8,128,256]{2,1,0:T(8,128)(2,1)S(1)}, u32[]{:S(2)}, u32[]{:S(2)}) collective-permute-start(bf16[8,128,256]{2,1,0:T(8,128)(2,1)} %get-tuple-element.40.own_ref), channel_id=1, source_target_pairs={{0,4},{4,0},{8,12},{12,8},{16,20},{20,16},{24,28},{28,24},{1,5},{5... | collective-permute-start | bytes 1572872 | tf_op jit(solution)/shard_map/ppermute | solution.py:683
  35.6 0.7 copy-start.6
  36.5 7.4 %collective-permute-start.2 = (bf16[8,128,128]{2,1,0:T(8,128)(2,1)S(1)}, bf16[8,128,128]{2,1,0:T(8,128)(2,1)S(1)}, u32[]{:S(2)}, u32[]{:S(2)}) collective-permute-start(bf16[8,128,128]{2,1,0:T(8,128)(2,1)S(1)} %get-tuple-element.44.refs_0_), channel_id=1, source_target_pairs={{0,8},{4,12},{8,0},{12,4},{16,24},{20,28},{24,16},{28,20},{1,9},{5... | collective-permute-start | bytes 786440 | tf_op jit(solution)/shard_map/ppermute | solution.py:669
  37.1 2.2 %copy-start.3 = (bf16[4,512,1024]{2,1,0:T(8,128)(2,1)S(1)}, bf16[4,512,1024]{2,1,0:T(8,128)(2,1)}, u32[]{:S(2)}) copy-start(bf16[4,512,1024]{2,1,0:T(8,128)(2,1)} %get-tuple-element.45.from_ref) | copy-start | bytes 12582916
  39.5 4.7 %copy-start = (bf16[4,512,1024]{2,1,0:T(8,128)(2,1)}, bf16[4,512,1024]{2,1,0:T(8,128)(2,1)S(1)}, u32[]{:S(2)}) copy-start(bf16[4,512,1024]{2,1,0:T(8,128)(2,1)S(1)} %stage.1.refs_2_.refs_1_) | copy-start | bytes 12582916
  39.5 9.0 %copy-start.4 = (bf16[8,128,256]{2,1,0:T(8,128)(2,1)S(1)}, bf16[8,128,256]{2,1,0:T(8,128)(2,1)}, u32[]{:S(2)}) copy-start(bf16[8,128,256]{2,1,0:T(8,128)(2,1)} %get-tuple-element.40.own_ref) | copy-start | bytes 1572868
  44.2 5.1 %collective-permute-start.4 = (bf16[8,128,128]{2,1,0:T(8,128)(2,1)S(1)}, bf16[8,128,128]{2,1,0:T(8,128)(2,1)S(1)}, u32[]{:S(2)}, u32[]{:S(2)}) collective-permute-start(bf16[8,128,128]{2,1,0:T(8,128)(2,1)S(1)} %hop.4.rest_0_), channel_id=1, source_target_pairs={{0,0},{4,4},{8,16},{12,20},{16,8},{20,12},{24,24},{28,28},{1,1},{5... | collective-permute-start | bytes 786440 | tf_op jit(solution)/shard_map/ppermute | solution.py:669
  48.8 9.3 %collective-permute-start.3 = (bf16[8,128,128]{2,1,0:T(8,128)(2,1)S(1)}, bf16[8,128,128]{2,1,0:T(8,128)(2,1)S(1)}, u32[]{:S(2)}, u32[]{:S(2)}) collective-permute-start(bf16[8,128,128]{2,1,0:T(8,128)(2,1)S(1)} %get-tuple-element.46.refs_0_), channel_id=1, source_target_pairs={{0,8},{4,12},{8,0},{12,4},{16,24},{20,28},{24,16},{28,20},{1,9},{5... | collective-permute-start | bytes 786440 | tf_op jit(solution)/shard_map/ppermute | solution.py:669
  49.6 11.8 %collective-permute-start.6 = (bf16[8,128,128]{2,1,0:T(8,128)(2,1)S(1)}, bf16[8,128,128]{2,1,0:T(8,128)(2,1)S(1)}, u32[]{:S(2)}, u32[]{:S(2)}) collective-permute-start(bf16[8,128,128]{2,1,0:T(8,128)(2,1)S(1)} %hop.5.refs_2_), channel_id=1, source_target_pairs={{0,0},{4,4},{8,8},{12,12},{16,24},{20,28},{24,16},{28,20},{1,1},{5... | collective-permute-start | bytes 786440 | tf_op jit(solution)/shard_map/ppermute | solution.py:669
  58.4 8.6 %collective-permute-start.5 = (bf16[8,128,128]{2,1,0:T(8,128)(2,1)S(1)}, bf16[8,128,128]{2,1,0:T(8,128)(2,1)S(1)}, u32[]{:S(2)}, u32[]{:S(2)}) collective-permute-start(bf16[8,128,128]{2,1,0:T(8,128)(2,1)S(1)} %hop.6.refs_6_), channel_id=1, source_target_pairs={{0,0},{4,4},{8,16},{12,20},{16,8},{20,12},{24,24},{28,28},{1,1},{5... | collective-permute-start | bytes 786440 | tf_op jit(solution)/shard_map/ppermute | solution.py:669
  61.4 2.2 %copy-start.1 = (bf16[4,512,1024]{2,1,0:T(8,128)(2,1)S(1)}, bf16[4,512,1024]{2,1,0:T(8,128)(2,1)}, u32[]{:S(2)}) copy-start(bf16[4,512,1024]{2,1,0:T(8,128)(2,1)} %copy-done) | copy-start | bytes 12582916
  63.5 13.9 %copy-start.2 = (bf16[4,512,1024]{2,1,0:T(8,128)(2,1)S(1)}, bf16[4,512,1024]{2,1,0:T(8,128)(2,1)}, u32[]{:S(2)}) copy-start(bf16[4,512,1024]{2,1,0:T(8,128)(2,1)} %get-tuple-element.39.refs_1_) | copy-start | bytes 12582916
  65.3 4.4 %collective-permute-start.8 = (bf16[128,1024]{1,0:T(8,128)(2,1)S(1)}, bf16[128,1024]{1,0:T(8,128)(2,1)S(1)}, u32[]{:S(2)}, u32[]{:S(2)}) collective-permute-start(bf16[128,1024]{1,0:T(8,128)(2,1)S(1)} %get-tuple-element.49), channel_id=1, source_target_pairs={{0,1},{1,0},{2,3},{3,2},{4,5},{5,4},{6,7},{7,6},{8,9},{9,8},{10,11... | collective-permute-start | bytes 786440 | tf_op jit(solution)/shard_map/ppermute | solution.py:718
  65.3 9.2 %collective-permute-start.9 = (bf16[128,1024]{1,0:T(8,128)(2,1)S(1)}, bf16[128,1024]{1,0:T(8,128)(2,1)S(1)}, u32[]{:S(2)}, u32[]{:S(2)}) collective-permute-start(bf16[128,1024]{1,0:T(8,128)(2,1)S(1)} %get-tuple-element.50), channel_id=1, source_target_pairs={{0,2},{1,3},{2,0},{3,1},{4,6},{5,7},{6,4},{7,5},{8,10},{9,11},{10,... | collective-permute-start | bytes 786440 | tf_op jit(solution)/shard_map/ppermute | solution.py:718
  67.2 10.3 %collective-permute-start.7 = (bf16[8,128,128]{2,1,0:T(8,128)(2,1)S(1)}, bf16[8,128,128]{2,1,0:T(8,128)(2,1)S(1)}, u32[]{:S(2)}, u32[]{:S(2)}) collective-permute-start(bf16[8,128,128]{2,1,0:T(8,128)(2,1)S(1)} %hop.7.refs_4_), channel_id=1, source_target_pairs={{0,0},{4,4},{8,8},{12,12},{16,24},{20,28},{24,16},{28,20},{1,1},{5... | collective-permute-start | bytes 786440 | tf_op jit(solution)/shard_map/ppermute | solution.py:669
  69.5 11.6 %collective-permute-start.13 = (bf16[128,1024]{1,0:T(8,128)(2,1)S(1)}, bf16[128,1024]{1,0:T(8,128)(2,1)S(1)}, u32[]{:S(2)}, u32[]{:S(2)}) collective-permute-start(bf16[128,1024]{1,0:T(8,128)(2,1)S(1)} %get-tuple-element.56), channel_id=1, source_target_pairs={{0,3},{1,2},{2,1},{3,0},{4,7},{5,6},{6,5},{7,4},{8,11},{9,10},{10,... | collective-permute-start | bytes 786440 | tf_op jit(solution)/shard_map/ppermute | solution.py:718
  79.2 2.7 %collective-permute-start.11 = (bf16[128,1024]{1,0:T(8,128)(2,1)S(1)}, bf16[128,1024]{1,0:T(8,128)(2,1)S(1)}, u32[]{:S(2)}, u32[]{:S(2)}) collective-permute-start(bf16[128,1024]{1,0:T(8,128)(2,1)S(1)} %get-tuple-element.54), channel_id=1, source_target_pairs={{0,1},{1,0},{2,3},{3,2},{4,5},{5,4},{6,7},{7,6},{8,9},{9,8},{10,11... | collective-permute-start | bytes 786440 | tf_op jit(solution)/shard_map/ppermute | solution.py:718
  79.3 9.2 %collective-permute-start.12 = (bf16[128,1024]{1,0:T(8,128)(2,1)S(1)}, bf16[128,1024]{1,0:T(8,128)(2,1)S(1)}, u32[]{:S(2)}, u32[]{:S(2)}) collective-permute-start(bf16[128,1024]{1,0:T(8,128)(2,1)S(1)} %get-tuple-element.55), channel_id=1, source_target_pairs={{0,2},{1,3},{2,0},{3,1},{4,6},{5,7},{6,4},{7,5},{8,10},{9,11},{10,... | collective-permute-start | bytes 786440 | tf_op jit(solution)/shard_map/ppermute | solution.py:718
  79.9 13.3 %collective-permute-start.10 = (bf16[128,1024]{1,0:T(8,128)(2,1)S(1)}, bf16[128,1024]{1,0:T(8,128)(2,1)S(1)}, u32[]{:S(2)}, u32[]{:S(2)}) collective-permute-start(bf16[128,1024]{1,0:T(8,128)(2,1)S(1)} %get-tuple-element.52), channel_id=1, source_target_pairs={{0,3},{1,2},{2,1},{3,0},{4,7},{5,6},{6,5},{7,4},{8,11},{9,10},{10,... | collective-permute-start | bytes 786440 | tf_op jit(solution)/shard_map/ppermute | solution.py:718

commit v4 on v3

--- a/solution.py
+++ b/solution.py
@@ -635,8 +635,8 @@
     )(place, *parts, *kept, *after)
 
 
-ORDER = ("l0", "l1", "p0", "t0", "h01", "p1", "h02", "h11", "f00")
-ORDER += ("h12", "a00", "f10", "b00", "a10", "b10")
+ORDER = ("l0", "l1", "p0", "h01", "p1", "h02", "h11", "t0", "f00")
+ORDER += ("h12", "t1", "a00", "f10", "b00", "a10", "b10")
 
 
 def order(groups, steps):

time: 95.2 us -> 93.7 us (0.984)
  local copies, waits for them, and re-layouts: 5.07 us -> 2.88 us
    unnamed x14 -> x10, local copies, waits for them, and re-layouts: 5.07 us -> 2.88 us
  transfers between devices with their start and end apart: 14 -> 14, of which waited for: 9 -> 8; matrix products, arithmetic and copies ran while one was open for 0% -> 0% of each run, Pallas kernels for 21% -> 21%
where the time goes in v4:
time: 93.7 us; the launch traced here: 92.6 us
  Pallas kernels  42.7 us (46%)
  waiting for transfers between devices  30 us (32%)
  starting transfers between devices  16.8 us (18%)
  local copies, waits for them, and re-layouts  2.88 us (3%)
    pallas_call x2, Pallas kernels, local_call(): pl.pallas_call(kernel, in_specs=[smem] + in_specs + spaces, out_specs=out...  33.3 us
    ppermute x6, waiting for transfers between devices, finish(): lax.ppermute(outs[d], 'head', pairing)  14.3 us
    ppermute x6, waiting for transfers between devices, swap(): lax.ppermute(array, 'ctx', [(i, 2 * to[i >> 1] + (i & 1)) for i in range(...  11.9 us
    ppermute x6, starting transfers between devices, swap(): lax.ppermute(array, 'ctx', [(i, 2 * to[i >> 1] + (i & 1)) for i in range(...  11 us
    pallas_call x4, Pallas kernels, gather_call(): pl.pallas_call(kernel, in_specs=[pl.BlockSpec(memory_space=pltpu.SMEM)] +...  3.81 us
    ppermute x2, waiting for transfers between devices, local(): others[g] = lax.ppermute(runs[g], 'ctx', [(i, i ^ 1) for i in range(size)])  3.7 us
    ppermute x6, starting transfers between devices, finish(): lax.ppermute(outs[d], 'head', pairing)  3.66 us
    pallas_call x2, Pallas kernels, finish_call(): pl.pallas_call(kernel, in_specs=[smem] + [vmem] * (2 + len(flat)) + space...  3.57 us
  transfers between devices with their start and end apart: 14, of which 8 were waited for; matrix products, arithmetic and copies ran while one was open for 0% of the time, Pallas kernels for 21%

profile of v4, /device:TPU:24, one launch (start us, length us, event | category | flops | bytes accessed | tf_op | source)
XLA Modules:
  0.0 92.6 jit_solution(13646802414154170439)
XLA Ops:
  0.0 21.6 %local.2 = (bf16[8,128,256]{2,1,0:T(8,128)(2,1)}, bf16[4,512,1024]{2,1,0:T(8,128)(2,1)}, f32[8,128]{1,0:T(8,128)}, f32[64,128]{1,0:T(8,128)}, f32[64,128]{1,0:T(...) custom-call(s32[8]{0:T(128)} %refs_0_.3, f32[80,512]{1,0:T(8,128)} %bitcast.6, f32[16,512]{1,0:T(8,128)} %bitcast.8, ...), custom_call_target="tpu_custom_call" | custom-call | tf_op jit(solution)/shard_map/local/pallas_call | solution.py:409
  21.6 1.6 %collective-permute-start.1 = (bf16[8,128,256]{2,1,0:T(8,128)(2,1)}, bf16[8,128,256]{2,1,0:T(8,128)(2,1)S(1)}, u32[]{:S(2)}, u32[]{:S(2)}) collective-permute-start(bf16[8,128,256]{2,1,0:T(8,128)(2,1)} %get-tuple-element.41.own_ref), channel_id=1, source_target_pairs={{0,4},{4,0},{8,12},{12,8},{16,20},{20,16},{24,28},{28,24},{1,5},{5... | collective-permute-start | bytes 1572872 | tf_op jit(solution)/shard_map/ppermute | solution.py:683
  23.2 11.7 %local.3 = (bf16[8,128,256]{2,1,0:T(8,128)(2,1)}, bf16[4,512,1024]{2,1,0:T(8,128)(2,1)}, f32[8,128]{1,0:T(8,128)}) custom-call(s32[8]{0:T(128)} %refs_0_.3, f32[80,512]{1,0:T(8,128)} %bitcast.7, f32[64,128]{1,0:T(8,128)} %get-tuple-element.34.refs_2_, f32[64,128]{1,0:T(8,128)} %get-tuple-element.35.refs_3_, bf16[16,512,128]{2,1,0:T(8,128)(2,1)} %get-tuple-element.36.refs_4_, ...), custom_call_target="tpu_custom_call" | custom-call | tf_op jit(solution)/shard_map/local/pallas_call | solution.py:409
  34.9 0.6 collective-permute-start
  35.5 0.1 collective-permute-done.1.other_ref.refs_2_
  35.6 0.7 copy-done.4
  36.3 0.3 pair.2
  36.6 0.5 collective-permute-start.2
  37.1 6.9 %collective-permute-done.2.refs_1_.refs_3_ = bf16[8,128,128]{2,1,0:T(8,128)(2,1)S(1)} collective-permute-done((bf16[8,128,128]{2,1,0:T(8,128)(2,1)S(1)}, bf16[8,128,128]{2,1,0:T(8,128)(2,1)S(1)}, u32[]{:S(2)}, u32[]{:S(2)}) %collective-permute-start.2) | collective-permute-done | bytes 262176 | tf_op jit(solution)/shard_map/ppermute | solution.py:669
  44.0 0.2 hop.4.rest_0_
  44.2 0.7 collective-permute-start.4
  44.9 3.6 %collective-permute-done.other_ref.refs_2_ = bf16[8,128,256]{2,1,0:T(8,128)(2,1)S(1)} collective-permute-done((bf16[8,128,256]{2,1,0:T(8,128)(2,1)}, bf16[8,128,256]{2,1,0:T(8,128)(2,1)S(1)}, u32[]{:S(2)}, u32[]{:S(2)}) %collective-permute-start) | collective-permute-done | bytes 524320 | tf_op jit(solution)/shard_map/ppermute | solution.py:683
  48.5 0.0 copy-done.2
  48.5 0.3 pair.3
  48.8 0.5 collective-permute-start.3
  49.4 0.0 collective-permute-done.4.refs_0_.refs_4_
  49.4 0.2 hop.5.refs_2_
  49.6 5.6 %collective-permute-start.6 = (bf16[8,128,128]{2,1,0:T(8,128)(2,1)S(1)}, bf16[8,128,128]{2,1,0:T(8,128)(2,1)S(1)}, u32[]{:S(2)}, u32[]{:S(2)}) collective-permute-start(bf16[8,128,128]{2,1,0:T(8,128)(2,1)S(1)} %hop.5.refs_2_), channel_id=1, source_target_pairs={{0,0},{4,4},{8,8},{12,12},{16,24},{20,28},{24,16},{28,20},{1,1},{5... | collective-permute-start | bytes 786440 | tf_op jit(solution)/shard_map/ppermute | solution.py:669
  55.2 2.9 %collective-permute-done.3.refs_1_.refs_3_ = bf16[8,128,128]{2,1,0:T(8,128)(2,1)S(1)} collective-permute-done((bf16[8,128,128]{2,1,0:T(8,128)(2,1)S(1)}, bf16[8,128,128]{2,1,0:T(8,128)(2,1)S(1)}, u32[]{:S(2)}, u32[]{:S(2)}) %collective-permute-start.3) | collective-permute-done | bytes 262176 | tf_op jit(solution)/shard_map/ppermute | solution.py:669
  58.2 0.2 hop.6.refs_0_
  58.4 0.7 collective-permute-start.5
  59.1 0.1 pad_add_fusion.refs_0_
  59.1 2.2 %copy-done.1 = bf16[4,512,1024]{2,1,0:T(8,128)(2,1)S(1)} copy-done((bf16[4,512,1024]{2,1,0:T(8,128)(2,1)S(1)}, bf16[4,512,1024]{2,1,0:T(8,128)(2,1)}, u32[]{:S(2)}) %copy-start.1) | copy-done | bytes 4194328
  61.3 0.3 stage.2.refs_1_.refs_6_
  61.6 0.0 collective-permute-done.6.refs_5_
  61.6 1.8 %finish.2 = (bf16[128,1024]{1,0:T(8,128)(2,1)S(1)}, bf16[128,1024]{1,0:T(8,128)(2,1)S(1)}, bf16[128,1024]{1,0:T(8,128)(2,1)S(1)}, bf16[128,1024]{1,0:T(8,128)(2,1)S(1)}) custom-call(s32[2]{0:T(128)S(1)} %pad_add_fusion.refs_0_, bf16[4,512,1024]{2,1,0:T(8,128)(2,1)S(1)} %stage.2.refs_1_.refs_6_, ...), custom_call_target="tpu_custom_call" | custom-call | tf_op jit(solution)/shard_map/finish/pallas_call | solution.py:587
  63.4 0.1 collective-permute-start.8
  63.5 1.6 %collective-permute-start.9 = (bf16[128,1024]{1,0:T(8,128)(2,1)S(1)}, bf16[128,1024]{1,0:T(8,128)(2,1)S(1)}, u32[]{:S(2)}, u32[]{:S(2)}) collective-permute-start(bf16[128,1024]{1,0:T(8,128)(2,1)S(1)} %get-tuple-element.50), channel_id=1, source_target_pairs={{0,2},{1,3},{2,0},{3,1},{4,6},{5,7},{6,4},{7,5},{8,10},{9,11},{10,... | collective-permute-start | bytes 786440 | tf_op jit(solution)/shard_map/ppermute | solution.py:718
  65.1 0.0 collective-permute-done.5.refs_0_.refs_4_
  65.1 0.2 hop.7.refs_0_
  65.3 3.0 %collective-permute-start.7 = (bf16[8,128,128]{2,1,0:T(8,128)(2,1)S(1)}, bf16[8,128,128]{2,1,0:T(8,128)(2,1)S(1)}, u32[]{:S(2)}, u32[]{:S(2)}) collective-permute-start(bf16[8,128,128]{2,1,0:T(8,128)(2,1)S(1)} %hop.7.refs_0_), channel_id=1, source_target_pairs={{0,0},{4,4},{8,8},{12,12},{16,24},{20,28},{24,16},{28,20},{1,1},{5... | collective-permute-start | bytes 786440 | tf_op jit(solution)/shard_map/ppermute | solution.py:669
  68.3 0.3 stage.3.refs_4_.refs_1_
  68.6 0.1 collective-permute-start.13
  68.7 0.0 collective-permute-done.8.refs_2_
  68.7 4.0 %collective-permute-done.9.refs_3_ = bf16[128,1024]{1,0:T(8,128)(2,1)S(1)} collective-permute-done((bf16[128,1024]{1,0:T(8,128)(2,1)S(1)}, bf16[128,1024]{1,0:T(8,128)(2,1)S(1)}, u32[]{:S(2)}, u32[]{:S(2)}) %collective-permute-start.9) | collective-permute-done | bytes 262176 | tf_op jit(solution)/shard_map/ppermute | solution.py:718
  72.7 0.9 gather.4
  73.6 2.0 %collective-permute-done.7.refs_5_ = bf16[8,128,128]{2,1,0:T(8,128)(2,1)S(1)} collective-permute-done((bf16[8,128,128]{2,1,0:T(8,128)(2,1)S(1)}, bf16[8,128,128]{2,1,0:T(8,128)(2,1)S(1)}, u32[]{:S(2)}, u32[]{:S(2)}) %collective-permute-start.7) | collective-permute-done | bytes 262176 | tf_op jit(solution)/shard_map/ppermute | solution.py:669
  75.6 1.8 %finish.3 = (bf16[128,1024]{1,0:T(8,128)(2,1)S(1)}, bf16[128,1024]{1,0:T(8,128)(2,1)S(1)}, bf16[128,1024]{1,0:T(8,128)(2,1)S(1)}, bf16[128,1024]{1,0:T(8,128)(2,1)S(1)}) custom-call(s32[2]{0:T(128)S(1)} %pad_add_fusion.refs_0_, bf16[4,512,1024]{2,1,0:T(8,128)(2,1)S(1)} %stage.3.refs_4_.refs_1_, ...), custom_call_target="tpu_custom_call" | custom-call | tf_op jit(solution)/shard_map/finish/pallas_call | solution.py:587
  77.4 0.1 collective-permute-start.11
  77.5 0.6 collective-permute-start.12
  78.0 1.3 %collective-permute-start.10 = (bf16[128,1024]{1,0:T(8,128)(2,1)S(1)}, bf16[128,1024]{1,0:T(8,128)(2,1)S(1)}, u32[]{:S(2)}, u32[]{:S(2)}) collective-permute-start(bf16[128,1024]{1,0:T(8,128)(2,1)S(1)} %get-tuple-element.52), channel_id=1, source_target_pairs={{0,3},{1,2},{2,1},{3,0},{4,7},{5,6},{6,5},{7,4},{8,11},{9,10},{10,... | collective-permute-start | bytes 786440 | tf_op jit(solution)/shard_map/ppermute | solution.py:718
  79.3 0.0 collective-permute-done.13.refs_1_
  79.3 0.7 gather.5
  80.0 0.0 collective-permute-done.11.refs_2_
  80.0 6.6 %collective-permute-done.12.refs_3_ = bf16[128,1024]{1,0:T(8,128)(2,1)S(1)} collective-permute-done((bf16[128,1024]{1,0:T(8,128)(2,1)S(1)}, bf16[128,1024]{1,0:T(8,128)(2,1)S(1)}, u32[]{:S(2)}, u32[]{:S(2)}) %collective-permute-start.12) | collective-permute-done | bytes 262176 | tf_op jit(solution)/shard_map/ppermute | solution.py:718
  86.6 0.9 gather.6
  87.5 3.8 %collective-permute-done.10.refs_1_ = bf16[128,1024]{1,0:T(8,128)(2,1)S(1)} collective-permute-done((bf16[128,1024]{1,0:T(8,128)(2,1)S(1)}, bf16[128,1024]{1,0:T(8,128)(2,1)S(1)}, u32[]{:S(2)}, u32[]{:S(2)}) %collective-permute-start.10) | collective-permute-done | bytes 262176 | tf_op jit(solution)/shard_map/ppermute | solution.py:718
  91.3 1.3 %gather.7 = (bf16[128,8192]{1,0:T(8,128)(2,1)}, f32[8,128]{1,0:T(8,128)}) custom-call(s32[1]{0:T(128)} %bitcast.refs_0_, bf16[128,1024]{1,0:T(8,128)(2,1)S(1)} %collective-permute-done.10.refs_1_, bf16[128,8192]{1,0:T(8,128)(2,1)} %get-tuple-element.60.refs_2_, f32[8,128]{1,0:T(8,128)S(1)} %get-tuple-element.61.refs_3_), custom_call_target="tpu_custom_call", output_to_operand_aliasing={{0}: (2, {})} | custom-call | tf_op jit(solution)/shard_map/gather/pallas_call | solution.py:622
  (7 shorter events, 0.0 us)
Async XLA Ops:
  21.6 13.9 %collective-permute-start.1 = (bf16[8,128,256]{2,1,0:T(8,128)(2,1)}, bf16[8,128,256]{2,1,0:T(8,128)(2,1)S(1)}, u32[]{:S(2)}, u32[]{:S(2)}) collective-permute-start(bf16[8,128,256]{2,1,0:T(8,128)(2,1)} %get-tuple-element.41.own_ref), channel_id=1, source_target_pairs={{0,4},{4,0},{8,12},{12,8},{16,20},{20,16},{24,28},{28,24},{1,5},{5... | collective-permute-start | bytes 1572872 | tf_op jit(solution)/shard_map/ppermute | solution.py:683
  23.2 12.4 %copy-start.3 = (bf16[8,128,256]{2,1,0:T(8,128)(2,1)S(1)}, bf16[8,128,256]{2,1,0:T(8,128)(2,1)}, u32[]{:S(2)}) copy-start(bf16[8,128,256]{2,1,0:T(8,128)(2,1)} %get-tuple-element.41.own_ref) | copy-start | bytes 1572868
  34.9 13.7 %copy-start.2 = (bf16[8,128,256]{2,1,0:T(8,128)(2,1)S(1)}, bf16[8,128,256]{2,1,0:T(8,128)(2,1)}, u32[]{:S(2)}) copy-start(bf16[8,128,256]{2,1,0:T(8,128)(2,1)} %get-tuple-element.40.own_ref) | copy-start | bytes 1572868
  34.9 13.7 %collective-permute-start = (bf16[8,128,256]{2,1,0:T(8,128)(2,1)}, bf16[8,128,256]{2,1,0:T(8,128)(2,1)S(1)}, u32[]{:S(2)}, u32[]{:S(2)}) collective-permute-start(bf16[8,128,256]{2,1,0:T(8,128)(2,1)} %get-tuple-element.40.own_ref), channel_id=1, source_target_pairs={{0,4},{4,0},{8,12},{12,8},{16,20},{20,16},{24,28},{28,24},{1,5},{5... | collective-permute-start | bytes 1572872 | tf_op jit(solution)/shard_map/ppermute | solution.py:683
  35.6 0.7 copy-start.4
  36.6 7.5 %collective-permute-start.2 = (bf16[8,128,128]{2,1,0:T(8,128)(2,1)S(1)}, bf16[8,128,128]{2,1,0:T(8,128)(2,1)S(1)}, u32[]{:S(2)}, u32[]{:S(2)}) collective-permute-start(bf16[8,128,128]{2,1,0:T(8,128)(2,1)S(1)} %get-tuple-element.44.refs_0_), channel_id=1, source_target_pairs={{0,8},{4,12},{8,0},{12,4},{16,24},{20,28},{24,16},{28,20},{1,9},{5... | collective-permute-start | bytes 786440 | tf_op jit(solution)/shard_map/ppermute | solution.py:669
  44.2 5.1 %collective-permute-start.4 = (bf16[8,128,128]{2,1,0:T(8,128)(2,1)S(1)}, bf16[8,128,128]{2,1,0:T(8,128)(2,1)S(1)}, u32[]{:S(2)}, u32[]{:S(2)}) collective-permute-start(bf16[8,128,128]{2,1,0:T(8,128)(2,1)S(1)} %hop.4.rest_0_), channel_id=1, source_target_pairs={{0,0},{4,4},{8,16},{12,20},{16,8},{20,12},{24,24},{28,28},{1,1},{5... | collective-permute-start | bytes 786440 | tf_op jit(solution)/shard_map/ppermute | solution.py:669
  48.8 9.3 %collective-permute-start.3 = (bf16[8,128,128]{2,1,0:T(8,128)(2,1)S(1)}, bf16[8,128,128]{2,1,0:T(8,128)(2,1)S(1)}, u32[]{:S(2)}, u32[]{:S(2)}) collective-permute-start(bf16[8,128,128]{2,1,0:T(8,128)(2,1)S(1)} %get-tuple-element.46.refs_0_), channel_id=1, source_target_pairs={{0,8},{4,12},{8,0},{12,4},{16,24},{20,28},{24,16},{28,20},{1,9},{5... | collective-permute-start | bytes 786440 | tf_op jit(solution)/shard_map/ppermute | solution.py:669
  49.6 12.0 %collective-permute-start.6 = (bf16[8,128,128]{2,1,0:T(8,128)(2,1)S(1)}, bf16[8,128,128]{2,1,0:T(8,128)(2,1)S(1)}, u32[]{:S(2)}, u32[]{:S(2)}) collective-permute-start(bf16[8,128,128]{2,1,0:T(8,128)(2,1)S(1)} %hop.5.refs_2_), channel_id=1, source_target_pairs={{0,0},{4,4},{8,8},{12,12},{16,24},{20,28},{24,16},{28,20},{1,1},{5... | collective-permute-start | bytes 786440 | tf_op jit(solution)/shard_map/ppermute | solution.py:669
  58.4 6.7 %collective-permute-start.5 = (bf16[8,128,128]{2,1,0:T(8,128)(2,1)S(1)}, bf16[8,128,128]{2,1,0:T(8,128)(2,1)S(1)}, u32[]{:S(2)}, u32[]{:S(2)}) collective-permute-start(bf16[8,128,128]{2,1,0:T(8,128)(2,1)S(1)} %hop.6.refs_0_), channel_id=1, source_target_pairs={{0,0},{4,4},{8,16},{12,20},{16,8},{20,12},{24,24},{28,28},{1,1},{5... | collective-permute-start | bytes 786440 | tf_op jit(solution)/shard_map/ppermute | solution.py:669
  59.1 2.2 %copy-start.1 = (bf16[4,512,1024]{2,1,0:T(8,128)(2,1)S(1)}, bf16[4,512,1024]{2,1,0:T(8,128)(2,1)}, u32[]{:S(2)}) copy-start(bf16[4,512,1024]{2,1,0:T(8,128)(2,1)} %get-tuple-element.47.from_ref) | copy-start | bytes 12582916
  61.6 6.7 %copy-start = (bf16[4,512,1024]{2,1,0:T(8,128)(2,1)S(1)}, bf16[4,512,1024]{2,1,0:T(8,128)(2,1)}, u32[]{:S(2)}) copy-start(bf16[4,512,1024]{2,1,0:T(8,128)(2,1)} %get-tuple-element.39.from_ref) | copy-start | bytes 12582916
  63.4 5.3 %collective-permute-start.8 = (bf16[128,1024]{1,0:T(8,128)(2,1)S(1)}, bf16[128,1024]{1,0:T(8,128)(2,1)S(1)}, u32[]{:S(2)}, u32[]{:S(2)}) collective-permute-start(bf16[128,1024]{1,0:T(8,128)(2,1)S(1)} %get-tuple-element.49), channel_id=1, source_target_pairs={{0,1},{1,0},{2,3},{3,2},{4,5},{5,4},{6,7},{7,6},{8,9},{9,8},{10,11... | collective-permute-start | bytes 786440 | tf_op jit(solution)/shard_map/ppermute | solution.py:718
  63.5 9.2 %collective-permute-start.9 = (bf16[128,1024]{1,0:T(8,128)(2,1)S(1)}, bf16[128,1024]{1,0:T(8,128)(2,1)S(1)}, u32[]{:S(2)}, u32[]{:S(2)}) collective-permute-start(bf16[128,1024]{1,0:T(8,128)(2,1)S(1)} %get-tuple-element.50), channel_id=1, source_target_pairs={{0,2},{1,3},{2,0},{3,1},{4,6},{5,7},{6,4},{7,5},{8,10},{9,11},{10,... | collective-permute-start | bytes 786440 | tf_op jit(solution)/shard_map/ppermute | solution.py:718
  65.3 10.3 %collective-permute-start.7 = (bf16[8,128,128]{2,1,0:T(8,128)(2,1)S(1)}, bf16[8,128,128]{2,1,0:T(8,128)(2,1)S(1)}, u32[]{:S(2)}, u32[]{:S(2)}) collective-permute-start(bf16[8,128,128]{2,1,0:T(8,128)(2,1)S(1)} %hop.7.refs_0_), channel_id=1, source_target_pairs={{0,0},{4,4},{8,8},{12,12},{16,24},{20,28},{24,16},{28,20},{1,1},{5... | collective-permute-start | bytes 786440 | tf_op jit(solution)/shard_map/ppermute | solution.py:669
  68.6 10.7 %collective-permute-start.13 = (bf16[128,1024]{1,0:T(8,128)(2,1)S(1)}, bf16[128,1024]{1,0:T(8,128)(2,1)S(1)}, u32[]{:S(2)}, u32[]{:S(2)}) collective-permute-start(bf16[128,1024]{1,0:T(8,128)(2,1)S(1)} %get-tuple-element.56), channel_id=1, source_target_pairs={{0,3},{1,2},{2,1},{3,0},{4,7},{5,6},{6,5},{7,4},{8,11},{9,10},{10,... | collective-permute-start | bytes 786440 | tf_op jit(solution)/shard_map/ppermute | solution.py:718
  77.4 2.7 %collective-permute-start.11 = (bf16[128,1024]{1,0:T(8,128)(2,1)S(1)}, bf16[128,1024]{1,0:T(8,128)(2,1)S(1)}, u32[]{:S(2)}, u32[]{:S(2)}) collective-permute-start(bf16[128,1024]{1,0:T(8,128)(2,1)S(1)} %get-tuple-element.54), channel_id=1, source_target_pairs={{0,1},{1,0},{2,3},{3,2},{4,5},{5,4},{6,7},{7,6},{8,9},{9,8},{10,11... | collective-permute-start | bytes 786440 | tf_op jit(solution)/shard_map/ppermute | solution.py:718
  77.5 9.2 %collective-permute-start.12 = (bf16[128,1024]{1,0:T(8,128)(2,1)S(1)}, bf16[128,1024]{1,0:T(8,128)(2,1)S(1)}, u32[]{:S(2)}, u32[]{:S(2)}) collective-permute-start(bf16[128,1024]{1,0:T(8,128)(2,1)S(1)} %get-tuple-element.55), channel_id=1, source_target_pairs={{0,2},{1,3},{2,0},{3,1},{4,6},{5,7},{6,4},{7,5},{8,10},{9,11},{10,... | collective-permute-start | bytes 786440 | tf_op jit(solution)/shard_map/ppermute | solution.py:718
  78.0 13.3 %collective-permute-start.10 = (bf16[128,1024]{1,0:T(8,128)(2,1)S(1)}, bf16[128,1024]{1,0:T(8,128)(2,1)S(1)}, u32[]{:S(2)}, u32[]{:S(2)}) collective-permute-start(bf16[128,1024]{1,0:T(8,128)(2,1)S(1)} %get-tuple-element.52), channel_id=1, source_target_pairs={{0,3},{1,2},{2,1},{3,0},{4,7},{5,6},{6,5},{7,4},{8,11},{9,10},{10,... | collective-permute-start | bytes 786440 | tf_op jit(solution)/shard_map/ppermute | solution.py:718

commit v5 on v4

--- a/solution.py
+++ b/solution.py
@@ -199,7 +199,7 @@
             low_s[i] = g * (bi * e)
             inv_s[i] = jnp.zeros_like(g)
 
-        repeat(BLOCK, to_lanes, 16)
+        repeat(BLOCK, to_lanes, 32)
 
         sub = lax.broadcasted_iota(jnp.int32, (8, lanes), 0)
 
@@ -238,12 +238,12 @@
             yield
             gram_s[pl.ds(i, units, stride=BLOCK), :] = a
 
-        repeat(BLOCK, from_lanes, 16)
+        repeat(BLOCK, from_lanes, 32)
 
     kept = []
     if solve:
         inverses()
-        kept = [(kn_s, kn_hbm), (gram_s, t_hbm)]
+        kept = [(kn_s, kn_hbm), (gram_s.at[:units * BLOCK], t_hbm)]
         kept = [pltpu.make_async_copy(x, y, keep_sem.at[i]) for i, (x, y) in enumerate(kept)]
         for c in kept:
             c.start()
@@ -417,7 +417,7 @@
             pltpu.VMEM((tokens, count * WIDE), bf16),
             pltpu.VMEM((tokens, count * WIDE), bf16),
             pltpu.VMEM((across, tokens, WIDE), bf16),
-            pltpu.VMEM((across * pairs * BLOCK, WIDE), f32),
+            pltpu.VMEM((across * pairs * BLOCK + (BLOCK if solve else 0), WIDE), f32),
             pltpu.VMEM((tokens, weights.shape[0]), f32),
             pltpu.VMEM((blocks, count, WIDE, WIDE), bf16),
             pltpu.VMEM((blocks, count, WIDE), f32),

time: 93.7 us -> 93.3 us (level)
  no operation moved by 1% of the time
where the time goes in v5:
time: 93.3 us; the launch traced here: 92.2 us
  Pallas kernels  42.3 us (45%)
  waiting for transfers between devices  30 us (32%)
  starting transfers between devices  16.8 us (18%)
  local copies, waits for them, and re-layouts  2.88 us (3%)
    pallas_call x2, Pallas kernels, local_call(): pl.pallas_call(kernel, in_specs=[smem] + in_specs + spaces, out_specs=out...  32.9 us
    ppermute x6, waiting for transfers between devices, finish(): lax.ppermute(outs[d], 'head', pairing)  14.3 us
    ppermute x6, waiting for transfers between devices, swap(): lax.ppermute(array, 'ctx', [(i, 2 * to[i >> 1] + (i & 1)) for i in range(...  11.9 us
    ppermute x6, starting transfers between devices, swap(): lax.ppermute(array, 'ctx', [(i, 2 * to[i >> 1] + (i & 1)) for i in range(...  11 us
    pallas_call x4, Pallas kernels, gather_call(): pl.pallas_call(kernel, in_specs=[pl.BlockSpec(memory_space=pltpu.SMEM)] +...  3.81 us
    ppermute x2, waiting for transfers between devices, local(): others[g] = lax.ppermute(runs[g], 'ctx', [(i, i ^ 1) for i in range(size)])  3.7 us
    ppermute x6, starting transfers between devices, finish(): lax.ppermute(outs[d], 'head', pairing)  3.66 us
    pallas_call x2, Pallas kernels, finish_call(): pl.pallas_call(kernel, in_specs=[smem] + [vmem] * (2 + len(flat)) + space...  3.57 us
  transfers between devices with their start and end apart: 14, of which 8 were waited for; matrix products, arithmetic and copies ran while one was open for 0% of the time, Pallas kernels for 21%

profile of v5, /device:TPU:24, one launch (start us, length us, event | category | flops | bytes accessed | tf_op | source)
XLA Modules:
  0.0 92.2 jit_solution(6989525122823137196)
XLA Ops:
  0.0 21.2 %local.2 = (bf16[8,128,256]{2,1,0:T(8,128)(2,1)}, bf16[4,512,1024]{2,1,0:T(8,128)(2,1)}, f32[8,128]{1,0:T(8,128)}, f32[64,128]{1,0:T(8,128)}, f32[64,128]{1,0:T(...) custom-call(s32[8]{0:T(128)} %refs_0_.3, f32[80,512]{1,0:T(8,128)} %bitcast.6, f32[16,512]{1,0:T(8,128)} %bitcast.8, ...), custom_call_target="tpu_custom_call" | custom-call | tf_op jit(solution)/shard_map/local/pallas_call | solution.py:409
  21.2 1.6 %collective-permute-start.1 = (bf16[8,128,256]{2,1,0:T(8,128)(2,1)}, bf16[8,128,256]{2,1,0:T(8,128)(2,1)S(1)}, u32[]{:S(2)}, u32[]{:S(2)}) collective-permute-start(bf16[8,128,256]{2,1,0:T(8,128)(2,1)} %get-tuple-element.41.own_ref), channel_id=1, source_target_pairs={{0,4},{4,0},{8,12},{12,8},{16,20},{20,16},{24,28},{28,24},{1,5},{5... | collective-permute-start | bytes 1572872 | tf_op jit(solution)/shard_map/ppermute | solution.py:683
  22.8 11.7 %local.3 = (bf16[8,128,256]{2,1,0:T(8,128)(2,1)}, bf16[4,512,1024]{2,1,0:T(8,128)(2,1)}, f32[8,128]{1,0:T(8,128)}) custom-call(s32[8]{0:T(128)} %refs_0_.3, f32[80,512]{1,0:T(8,128)} %bitcast.7, f32[64,128]{1,0:T(8,128)} %get-tuple-element.34.refs_2_, f32[64,128]{1,0:T(8,128)} %get-tuple-element.35.refs_3_, bf16[16,512,128]{2,1,0:T(8,128)(2,1)} %get-tuple-element.36.refs_4_, ...), custom_call_target="tpu_custom_call" | custom-call | tf_op jit(solution)/shard_map/local/pallas_call | solution.py:409
  34.5 0.6 collective-permute-start
  35.1 0.1 collective-permute-done.1.other_ref.refs_2_
  35.2 0.0 copy-done.3
  35.2 0.7 copy-done.4
  35.9 0.3 pair.2
  36.2 0.5 collective-permute-start.2
  36.7 6.9 %collective-permute-done.2.refs_1_.refs_3_ = bf16[8,128,128]{2,1,0:T(8,128)(2,1)S(1)} collective-permute-done((bf16[8,128,128]{2,1,0:T(8,128)(2,1)S(1)}, bf16[8,128,128]{2,1,0:T(8,128)(2,1)S(1)}, u32[]{:S(2)}, u32[]{:S(2)}) %collective-permute-start.2) | collective-permute-done | bytes 262176 | tf_op jit(solution)/shard_map/ppermute | solution.py:669
  43.6 0.2 hop.4.rest_0_
  43.8 0.7 collective-permute-start.4
  44.5 3.6 %collective-permute-done.other_ref.refs_2_ = bf16[8,128,256]{2,1,0:T(8,128)(2,1)S(1)} collective-permute-done((bf16[8,128,256]{2,1,0:T(8,128)(2,1)}, bf16[8,128,256]{2,1,0:T(8,128)(2,1)S(1)}, u32[]{:S(2)}, u32[]{:S(2)}) %collective-permute-start) | collective-permute-done | bytes 524320 | tf_op jit(solution)/shard_map/ppermute | solution.py:683
  48.1 0.3 pair.3
  48.4 0.5 collective-permute-start.3
  49.0 0.0 collective-permute-done.4.refs_0_.refs_4_
  49.0 0.2 hop.5.refs_2_
  49.2 5.6 %collective-permute-start.6 = (bf16[8,128,128]{2,1,0:T(8,128)(2,1)S(1)}, bf16[8,128,128]{2,1,0:T(8,128)(2,1)S(1)}, u32[]{:S(2)}, u32[]{:S(2)}) collective-permute-start(bf16[8,128,128]{2,1,0:T(8,128)(2,1)S(1)} %hop.5.refs_2_), channel_id=1, source_target_pairs={{0,0},{4,4},{8,8},{12,12},{16,24},{20,28},{24,16},{28,20},{1,1},{5... | collective-permute-start | bytes 786440 | tf_op jit(solution)/shard_map/ppermute | solution.py:669
  54.8 2.9 %collective-permute-done.3.refs_1_.refs_3_ = bf16[8,128,128]{2,1,0:T(8,128)(2,1)S(1)} collective-permute-done((bf16[8,128,128]{2,1,0:T(8,128)(2,1)S(1)}, bf16[8,128,128]{2,1,0:T(8,128)(2,1)S(1)}, u32[]{:S(2)}, u32[]{:S(2)}) %collective-permute-start.3) | collective-permute-done | bytes 262176 | tf_op jit(solution)/shard_map/ppermute | solution.py:669
  57.7 0.2 hop.6.refs_0_
  58.0 0.7 collective-permute-start.5
  58.7 0.1 pad_add_fusion.refs_0_
  58.7 2.2 %copy-done.1 = bf16[4,512,1024]{2,1,0:T(8,128)(2,1)S(1)} copy-done((bf16[4,512,1024]{2,1,0:T(8,128)(2,1)S(1)}, bf16[4,512,1024]{2,1,0:T(8,128)(2,1)}, u32[]{:S(2)}) %copy-start.1) | copy-done | bytes 4194328
  60.9 0.3 stage.2.refs_1_.refs_6_
  61.2 0.0 collective-permute-done.6.refs_5_
  61.2 1.8 %finish.2 = (bf16[128,1024]{1,0:T(8,128)(2,1)S(1)}, bf16[128,1024]{1,0:T(8,128)(2,1)S(1)}, bf16[128,1024]{1,0:T(8,128)(2,1)S(1)}, bf16[128,1024]{1,0:T(8,128)(2,1)S(1)}) custom-call(s32[2]{0:T(128)S(1)} %pad_add_fusion.refs_0_, bf16[4,512,1024]{2,1,0:T(8,128)(2,1)S(1)} %stage.2.refs_1_.refs_6_, ...), custom_call_target="tpu_custom_call" | custom-call | tf_op jit(solution)/shard_map/finish/pallas_call | solution.py:587
  63.0 0.1 collective-permute-start.8
  63.1 1.6 %collective-permute-start.9 = (bf16[128,1024]{1,0:T(8,128)(2,1)S(1)}, bf16[128,1024]{1,0:T(8,128)(2,1)S(1)}, u32[]{:S(2)}, u32[]{:S(2)}) collective-permute-start(bf16[128,1024]{1,0:T(8,128)(2,1)S(1)} %get-tuple-element.50), channel_id=1, source_target_pairs={{0,2},{1,3},{2,0},{3,1},{4,6},{5,7},{6,4},{7,5},{8,10},{9,11},{10,... | collective-permute-start | bytes 786440 | tf_op jit(solution)/shard_map/ppermute | solution.py:718
  64.7 0.0 collective-permute-done.5.refs_0_.refs_4_
  64.7 0.2 hop.7.refs_0_
  64.9 3.0 %collective-permute-start.7 = (bf16[8,128,128]{2,1,0:T(8,128)(2,1)S(1)}, bf16[8,128,128]{2,1,0:T(8,128)(2,1)S(1)}, u32[]{:S(2)}, u32[]{:S(2)}) collective-permute-start(bf16[8,128,128]{2,1,0:T(8,128)(2,1)S(1)} %hop.7.refs_0_), channel_id=1, source_target_pairs={{0,0},{4,4},{8,8},{12,12},{16,24},{20,28},{24,16},{28,20},{1,1},{5... | collective-permute-start | bytes 786440 | tf_op jit(solution)/shard_map/ppermute | solution.py:669
  67.9 0.3 stage.3.refs_4_.refs_1_
  68.2 0.1 collective-permute-start.13
  68.3 0.0 collective-permute-done.8.refs_2_
  68.3 4.0 %collective-permute-done.9.refs_3_ = bf16[128,1024]{1,0:T(8,128)(2,1)S(1)} collective-permute-done((bf16[128,1024]{1,0:T(8,128)(2,1)S(1)}, bf16[128,1024]{1,0:T(8,128)(2,1)S(1)}, u32[]{:S(2)}, u32[]{:S(2)}) %collective-permute-start.9) | collective-permute-done | bytes 262176 | tf_op jit(solution)/shard_map/ppermute | solution.py:718
  72.3 0.9 gather.4
  73.2 2.0 %collective-permute-done.7.refs_5_ = bf16[8,128,128]{2,1,0:T(8,128)(2,1)S(1)} collective-permute-done((bf16[8,128,128]{2,1,0:T(8,128)(2,1)S(1)}, bf16[8,128,128]{2,1,0:T(8,128)(2,1)S(1)}, u32[]{:S(2)}, u32[]{:S(2)}) %collective-permute-start.7) | collective-permute-done | bytes 262176 | tf_op jit(solution)/shard_map/ppermute | solution.py:669
  75.2 1.8 %finish.3 = (bf16[128,1024]{1,0:T(8,128)(2,1)S(1)}, bf16[128,1024]{1,0:T(8,128)(2,1)S(1)}, bf16[128,1024]{1,0:T(8,128)(2,1)S(1)}, bf16[128,1024]{1,0:T(8,128)(2,1)S(1)}) custom-call(s32[2]{0:T(128)S(1)} %pad_add_fusion.refs_0_, bf16[4,512,1024]{2,1,0:T(8,128)(2,1)S(1)} %stage.3.refs_4_.refs_1_, ...), custom_call_target="tpu_custom_call" | custom-call | tf_op jit(solution)/shard_map/finish/pallas_call | solution.py:587
  77.0 0.1 collective-permute-start.11
  77.0 0.6 collective-permute-start.12
  77.6 1.3 %collective-permute-start.10 = (bf16[128,1024]{1,0:T(8,128)(2,1)S(1)}, bf16[128,1024]{1,0:T(8,128)(2,1)S(1)}, u32[]{:S(2)}, u32[]{:S(2)}) collective-permute-start(bf16[128,1024]{1,0:T(8,128)(2,1)S(1)} %get-tuple-element.52), channel_id=1, source_target_pairs={{0,3},{1,2},{2,1},{3,0},{4,7},{5,6},{6,5},{7,4},{8,11},{9,10},{10,... | collective-permute-start | bytes 786440 | tf_op jit(solution)/shard_map/ppermute | solution.py:718
  78.9 0.0 collective-permute-done.13.refs_1_
  78.9 0.7 gather.5
  79.6 0.0 collective-permute-done.11.refs_2_
  79.6 6.6 %collective-permute-done.12.refs_3_ = bf16[128,1024]{1,0:T(8,128)(2,1)S(1)} collective-permute-done((bf16[128,1024]{1,0:T(8,128)(2,1)S(1)}, bf16[128,1024]{1,0:T(8,128)(2,1)S(1)}, u32[]{:S(2)}, u32[]{:S(2)}) %collective-permute-start.12) | collective-permute-done | bytes 262176 | tf_op jit(solution)/shard_map/ppermute | solution.py:718
  86.2 0.9 gather.6
  87.1 3.8 %collective-permute-done.10.refs_1_ = bf16[128,1024]{1,0:T(8,128)(2,1)S(1)} collective-permute-done((bf16[128,1024]{1,0:T(8,128)(2,1)S(1)}, bf16[128,1024]{1,0:T(8,128)(2,1)S(1)}, u32[]{:S(2)}, u32[]{:S(2)}) %collective-permute-start.10) | collective-permute-done | bytes 262176 | tf_op jit(solution)/shard_map/ppermute | solution.py:718
  90.9 1.3 %gather.7 = (bf16[128,8192]{1,0:T(8,128)(2,1)}, f32[8,128]{1,0:T(8,128)}) custom-call(s32[1]{0:T(128)} %bitcast.refs_0_, bf16[128,1024]{1,0:T(8,128)(2,1)S(1)} %collective-permute-done.10.refs_1_, bf16[128,8192]{1,0:T(8,128)(2,1)} %get-tuple-element.60.refs_2_, f32[8,128]{1,0:T(8,128)S(1)} %get-tuple-element.61.refs_3_), custom_call_target="tpu_custom_call", output_to_operand_aliasing={{0}: (2, {})} | custom-call | tf_op jit(solution)/shard_map/gather/pallas_call | solution.py:622
  (7 shorter events, 0.0 us)
Async XLA Ops:
  21.2 13.9 %collective-permute-start.1 = (bf16[8,128,256]{2,1,0:T(8,128)(2,1)}, bf16[8,128,256]{2,1,0:T(8,128)(2,1)S(1)}, u32[]{:S(2)}, u32[]{:S(2)}) collective-permute-start(bf16[8,128,256]{2,1,0:T(8,128)(2,1)} %get-tuple-element.41.own_ref), channel_id=1, source_target_pairs={{0,4},{4,0},{8,12},{12,8},{16,20},{20,16},{24,28},{28,24},{1,5},{5... | collective-permute-start | bytes 1572872 | tf_op jit(solution)/shard_map/ppermute | solution.py:683
  22.8 12.4 %copy-start.3 = (bf16[8,128,256]{2,1,0:T(8,128)(2,1)S(1)}, bf16[8,128,256]{2,1,0:T(8,128)(2,1)}, u32[]{:S(2)}) copy-start(bf16[8,128,256]{2,1,0:T(8,128)(2,1)} %get-tuple-element.41.own_ref) | copy-start | bytes 1572868
  34.5 13.7 %copy-start.2 = (bf16[8,128,256]{2,1,0:T(8,128)(2,1)S(1)}, bf16[8,128,256]{2,1,0:T(8,128)(2,1)}, u32[]{:S(2)}) copy-start(bf16[8,128,256]{2,1,0:T(8,128)(2,1)} %get-tuple-element.40.own_ref) | copy-start | bytes 1572868
  34.5 13.7 %collective-permute-start = (bf16[8,128,256]{2,1,0:T(8,128)(2,1)}, bf16[8,128,256]{2,1,0:T(8,128)(2,1)S(1)}, u32[]{:S(2)}, u32[]{:S(2)}) collective-permute-start(bf16[8,128,256]{2,1,0:T(8,128)(2,1)} %get-tuple-element.40.own_ref), channel_id=1, source_target_pairs={{0,4},{4,0},{8,12},{12,8},{16,20},{20,16},{24,28},{28,24},{1,5},{5... | collective-permute-start | bytes 1572872 | tf_op jit(solution)/shard_map/ppermute | solution.py:683
  35.2 0.7 copy-start.4
  36.2 7.5 %collective-permute-start.2 = (bf16[8,128,128]{2,1,0:T(8,128)(2,1)S(1)}, bf16[8,128,128]{2,1,0:T(8,128)(2,1)S(1)}, u32[]{:S(2)}, u32[]{:S(2)}) collective-permute-start(bf16[8,128,128]{2,1,0:T(8,128)(2,1)S(1)} %get-tuple-element.44.refs_0_), channel_id=1, source_target_pairs={{0,8},{4,12},{8,0},{12,4},{16,24},{20,28},{24,16},{28,20},{1,9},{5... | collective-permute-start | bytes 786440 | tf_op jit(solution)/shard_map/ppermute | solution.py:669
  43.8 5.1 %collective-permute-start.4 = (bf16[8,128,128]{2,1,0:T(8,128)(2,1)S(1)}, bf16[8,128,128]{2,1,0:T(8,128)(2,1)S(1)}, u32[]{:S(2)}, u32[]{:S(2)}) collective-permute-start(bf16[8,128,128]{2,1,0:T(8,128)(2,1)S(1)} %hop.4.rest_0_), channel_id=1, source_target_pairs={{0,0},{4,4},{8,16},{12,20},{16,8},{20,12},{24,24},{28,28},{1,1},{5... | collective-permute-start | bytes 786440 | tf_op jit(solution)/shard_map/ppermute | solution.py:669
  48.4 9.3 %collective-permute-start.3 = (bf16[8,128,128]{2,1,0:T(8,128)(2,1)S(1)}, bf16[8,128,128]{2,1,0:T(8,128)(2,1)S(1)}, u32[]{:S(2)}, u32[]{:S(2)}) collective-permute-start(bf16[8,128,128]{2,1,0:T(8,128)(2,1)S(1)} %get-tuple-element.46.refs_0_), channel_id=1, source_target_pairs={{0,8},{4,12},{8,0},{12,4},{16,24},{20,28},{24,16},{28,20},{1,9},{5... | collective-permute-start | bytes 786440 | tf_op jit(solution)/shard_map/ppermute | solution.py:669
  49.2 12.0 %collective-permute-start.6 = (bf16[8,128,128]{2,1,0:T(8,128)(2,1)S(1)}, bf16[8,128,128]{2,1,0:T(8,128)(2,1)S(1)}, u32[]{:S(2)}, u32[]{:S(2)}) collective-permute-start(bf16[8,128,128]{2,1,0:T(8,128)(2,1)S(1)} %hop.5.refs_2_), channel_id=1, source_target_pairs={{0,0},{4,4},{8,8},{12,12},{16,24},{20,28},{24,16},{28,20},{1,1},{5... | collective-permute-start | bytes 786440 | tf_op jit(solution)/shard_map/ppermute | solution.py:669
  58.0 6.7 %collective-permute-start.5 = (bf16[8,128,128]{2,1,0:T(8,128)(2,1)S(1)}, bf16[8,128,128]{2,1,0:T(8,128)(2,1)S(1)}, u32[]{:S(2)}, u32[]{:S(2)}) collective-permute-start(bf16[8,128,128]{2,1,0:T(8,128)(2,1)S(1)} %hop.6.refs_0_), channel_id=1, source_target_pairs={{0,0},{4,4},{8,16},{12,20},{16,8},{20,12},{24,24},{28,28},{1,1},{5... | collective-permute-start | bytes 786440 | tf_op jit(solution)/shard_map/ppermute | solution.py:669
  58.7 2.2 %copy-start.1 = (bf16[4,512,1024]{2,1,0:T(8,128)(2,1)S(1)}, bf16[4,512,1024]{2,1,0:T(8,128)(2,1)}, u32[]{:S(2)}) copy-start(bf16[4,512,1024]{2,1,0:T(8,128)(2,1)} %get-tuple-element.47.from_ref) | copy-start | bytes 12582916
  61.2 6.7 %copy-start = (bf16[4,512,1024]{2,1,0:T(8,128)(2,1)S(1)}, bf16[4,512,1024]{2,1,0:T(8,128)(2,1)}, u32[]{:S(2)}) copy-start(bf16[4,512,1024]{2,1,0:T(8,128)(2,1)} %get-tuple-element.39.from_ref) | copy-start | bytes 12582916
  63.0 5.3 %collective-permute-start.8 = (bf16[128,1024]{1,0:T(8,128)(2,1)S(1)}, bf16[128,1024]{1,0:T(8,128)(2,1)S(1)}, u32[]{:S(2)}, u32[]{:S(2)}) collective-permute-start(bf16[128,1024]{1,0:T(8,128)(2,1)S(1)} %get-tuple-element.49), channel_id=1, source_target_pairs={{0,1},{1,0},{2,3},{3,2},{4,5},{5,4},{6,7},{7,6},{8,9},{9,8},{10,11... | collective-permute-start | bytes 786440 | tf_op jit(solution)/shard_map/ppermute | solution.py:718
  63.1 9.2 %collective-permute-start.9 = (bf16[128,1024]{1,0:T(8,128)(2,1)S(1)}, bf16[128,1024]{1,0:T(8,128)(2,1)S(1)}, u32[]{:S(2)}, u32[]{:S(2)}) collective-permute-start(bf16[128,1024]{1,0:T(8,128)(2,1)S(1)} %get-tuple-element.50), channel_id=1, source_target_pairs={{0,2},{1,3},{2,0},{3,1},{4,6},{5,7},{6,4},{7,5},{8,10},{9,11},{10,... | collective-permute-start | bytes 786440 | tf_op jit(solution)/shard_map/ppermute | solution.py:718
  64.9 10.3 %collective-permute-start.7 = (bf16[8,128,128]{2,1,0:T(8,128)(2,1)S(1)}, bf16[8,128,128]{2,1,0:T(8,128)(2,1)S(1)}, u32[]{:S(2)}, u32[]{:S(2)}) collective-permute-start(bf16[8,128,128]{2,1,0:T(8,128)(2,1)S(1)} %hop.7.refs_0_), channel_id=1, source_target_pairs={{0,0},{4,4},{8,8},{12,12},{16,24},{20,28},{24,16},{28,20},{1,1},{5... | collective-permute-start | bytes 786440 | tf_op jit(solution)/shard_map/ppermute | solution.py:669
  68.2 10.7 %collective-permute-start.13 = (bf16[128,1024]{1,0:T(8,128)(2,1)S(1)}, bf16[128,1024]{1,0:T(8,128)(2,1)S(1)}, u32[]{:S(2)}, u32[]{:S(2)}) collective-permute-start(bf16[128,1024]{1,0:T(8,128)(2,1)S(1)} %get-tuple-element.56), channel_id=1, source_target_pairs={{0,3},{1,2},{2,1},{3,0},{4,7},{5,6},{6,5},{7,4},{8,11},{9,10},{10,... | collective-permute-start | bytes 786440 | tf_op jit(solution)/shard_map/ppermute | solution.py:718
  77.0 2.7 %collective-permute-start.11 = (bf16[128,1024]{1,0:T(8,128)(2,1)S(1)}, bf16[128,1024]{1,0:T(8,128)(2,1)S(1)}, u32[]{:S(2)}, u32[]{:S(2)}) collective-permute-start(bf16[128,1024]{1,0:T(8,128)(2,1)S(1)} %get-tuple-element.54), channel_id=1, source_target_pairs={{0,1},{1,0},{2,3},{3,2},{4,5},{5,4},{6,7},{7,6},{8,9},{9,8},{10,11... | collective-permute-start | bytes 786440 | tf_op jit(solution)/shard_map/ppermute | solution.py:718
  77.0 9.2 %collective-permute-start.12 = (bf16[128,1024]{1,0:T(8,128)(2,1)S(1)}, bf16[128,1024]{1,0:T(8,128)(2,1)S(1)}, u32[]{:S(2)}, u32[]{:S(2)}) collective-permute-start(bf16[128,1024]{1,0:T(8,128)(2,1)S(1)} %get-tuple-element.55), channel_id=1, source_target_pairs={{0,2},{1,3},{2,0},{3,1},{4,6},{5,7},{6,4},{7,5},{8,10},{9,11},{10,... | collective-permute-start | bytes 786440 | tf_op jit(solution)/shard_map/ppermute | solution.py:718
  77.6 13.3 %collective-permute-start.10 = (bf16[128,1024]{1,0:T(8,128)(2,1)S(1)}, bf16[128,1024]{1,0:T(8,128)(2,1)S(1)}, u32[]{:S(2)}, u32[]{:S(2)}) collective-permute-start(bf16[128,1024]{1,0:T(8,128)(2,1)S(1)} %get-tuple-element.52), channel_id=1, source_target_pairs={{0,3},{1,2},{2,1},{3,0},{4,7},{5,6},{6,5},{7,4},{8,11},{9,10},{10,... | collective-permute-start | bytes 786440 | tf_op jit(solution)/shard_map/ppermute | solution.py:718

commit v6 on v5

--- a/solution.py
+++ b/solution.py
@@ -86,7 +86,7 @@
     else:
         row_s, colg_s = inputs["row"], inputs["col"]
     (
-        weight_s, q_s, v_s, kn_s, gram_s, scale_s, m_s, fall_s, s_s, qt_s, near_s, p_s, term_s, copy_sem,
+        weight_s, q_s, v_s, kn_s, gram_s, scale_s, m_s, fall_s, s_s, qt_s, near_s, p_s, term_s, run_s, copy_sem,
         pair_sem, keep_sem, step_sem,
     ) = refs
     tokens = q_s.shape[0]
@@ -353,11 +353,14 @@
 
     lax.fori_loop(1, blocks, scan, 0)
     for h in range(count):
-        run_ref[h] = p_s[h].astype(bf16)
+        run_s[h] = p_s[h].astype(bf16)
+    run_copy = pltpu.make_async_copy(run_s, run_ref, keep_sem.at[2])
+    run_copy.start()
     for c in kept:
         c.wait()
     for b in range(blocks):
         term_copy(b).wait()
+    run_copy.wait()
 
 
 def local_call(span, heads, depth, levels, weights, solved, inputs, q, v, after):
@@ -371,7 +374,7 @@
     vmem = pl.BlockSpec(memory_space=pltpu.VMEM)
     hbm = pl.BlockSpec(memory_space=pltpu.HBM)
     after, spaces = waits(after)
-    out_specs = [vmem, hbm, vmem]
+    out_specs = [hbm, hbm, vmem]
     out_shape = [
         jax.ShapeDtypeStruct((count, WIDE, 2 * WIDE), bf16),
         jax.ShapeDtypeStruct((1 + depth, tokens, count * WIDE), bf16),
@@ -426,9 +429,10 @@
             pltpu.VMEM((pairs * count, WIDE, WIDE), f32),
             pltpu.VMEM((count, WIDE, 2 * WIDE), f32),
             pltpu.VMEM((blocks, 1 + depth, BLOCK, count * WIDE), bf16),
+            pltpu.VMEM((count, WIDE, 2 * WIDE), bf16),
             pltpu.SemaphoreType.DMA((5,)),
             pltpu.SemaphoreType.DMA((pairs, 4)),
-            pltpu.SemaphoreType.DMA((2,)),
+            pltpu.SemaphoreType.DMA((3,)),
             pltpu.SemaphoreType.DMA((blocks,)),
         ],
         compiler_params=pltpu.CompilerParams(vmem_limit_bytes=int(LOCAL * MEG)),

time: 93.3 us -> 93.2 us (level)
  no operation moved by 1% of the time
where the time goes in v6:
time: 93.2 us; the launch traced here: 92.1 us
  Pallas kernels  42.2 us (45%)
  waiting for transfers between devices  30 us (32%)
  starting transfers between devices  16.8 us (18%)
  local copies, waits for them, and re-layouts  2.88 us (3%)
    pallas_call x2, Pallas kernels, local_call(): pl.pallas_call(kernel, in_specs=[smem] + in_specs + spaces, out_specs=out...  32.8 us
    ppermute x6, waiting for transfers between devices, finish(): lax.ppermute(outs[d], 'head', pairing)  14.3 us
    ppermute x6, waiting for transfers between devices, swap(): lax.ppermute(array, 'ctx', [(i, 2 * to[i >> 1] + (i & 1)) for i in range(...  11.9 us
    ppermute x6, starting transfers between devices, swap(): lax.ppermute(array, 'ctx', [(i, 2 * to[i >> 1] + (i & 1)) for i in range(...  10.9 us
    pallas_call x4, Pallas kernels, gather_call(): pl.pallas_call(kernel, in_specs=[pl.BlockSpec(memory_space=pltpu.SMEM)] +...  3.81 us
    ppermute x2, waiting for transfers between devices, local(): others[g] = lax.ppermute(runs[g], 'ctx', [(i, i ^ 1) for i in range(size)])  3.76 us
    ppermute x6, starting transfers between devices, finish(): lax.ppermute(outs[d], 'head', pairing)  3.67 us
    pallas_call x2, Pallas kernels, finish_call(): pl.pallas_call(kernel, in_specs=[smem] + [vmem] * (2 + len(flat)) + space...  3.56 us
  transfers between devices with their start and end apart: 14, of which 8 were waited for; matrix products, arithmetic and copies ran while one was open for 0% of the time, Pallas kernels for 21%

profile of v6, /device:TPU:24, one launch (start us, length us, event | category | flops | bytes accessed | tf_op | source)
XLA Modules:
  0.0 92.1 jit_solution(15954860995018454238)
XLA Ops:
  0.0 21.2 %local.2 = (bf16[8,128,256]{2,1,0:T(8,128)(2,1)}, bf16[4,512,1024]{2,1,0:T(8,128)(2,1)}, f32[8,128]{1,0:T(8,128)}, f32[64,128]{1,0:T(8,128)}, f32[64,128]{1,0:T(...) custom-call(s32[8]{0:T(128)} %refs_0_.3, f32[80,512]{1,0:T(8,128)} %bitcast.6, f32[16,512]{1,0:T(8,128)} %bitcast.8, ...), custom_call_target="tpu_custom_call" | custom-call | tf_op jit(solution)/shard_map/local/pallas_call | solution.py:412
  21.2 1.6 %collective-permute-start.1 = (bf16[8,128,256]{2,1,0:T(8,128)(2,1)}, bf16[8,128,256]{2,1,0:T(8,128)(2,1)S(1)}, u32[]{:S(2)}, u32[]{:S(2)}) collective-permute-start(bf16[8,128,256]{2,1,0:T(8,128)(2,1)} %get-tuple-element.41.own_ref), channel_id=1, source_target_pairs={{0,4},{4,0},{8,12},{12,8},{16,20},{20,16},{24,28},{28,24},{1,5},{5... | collective-permute-start | bytes 1572872 | tf_op jit(solution)/shard_map/ppermute | solution.py:687
  22.7 11.6 %local.3 = (bf16[8,128,256]{2,1,0:T(8,128)(2,1)}, bf16[4,512,1024]{2,1,0:T(8,128)(2,1)}, f32[8,128]{1,0:T(8,128)}) custom-call(s32[8]{0:T(128)} %refs_0_.3, f32[80,512]{1,0:T(8,128)} %bitcast.7, f32[64,128]{1,0:T(8,128)} %get-tuple-element.34.refs_2_, f32[64,128]{1,0:T(8,128)} %get-tuple-element.35.refs_3_, bf16[16,512,128]{2,1,0:T(8,128)(2,1)} %get-tuple-element.36.refs_4_, ...), custom_call_target="tpu_custom_call" | custom-call | tf_op jit(solution)/shard_map/local/pallas_call | solution.py:412
  34.4 0.6 collective-permute-start
  35.0 0.2 collective-permute-done.1.other_ref.refs_2_
  35.1 0.0 copy-done.3
  35.1 0.7 copy-done.4
  35.8 0.3 pair.2
  36.1 0.5 collective-permute-start.2
  36.6 6.9 %collective-permute-done.2.refs_1_.refs_3_ = bf16[8,128,128]{2,1,0:T(8,128)(2,1)S(1)} collective-permute-done((bf16[8,128,128]{2,1,0:T(8,128)(2,1)S(1)}, bf16[8,128,128]{2,1,0:T(8,128)(2,1)S(1)}, u32[]{:S(2)}, u32[]{:S(2)}) %collective-permute-start.2) | collective-permute-done | bytes 262176 | tf_op jit(solution)/shard_map/ppermute | solution.py:673
  43.5 0.2 hop.4.rest_0_
  43.7 0.7 collective-permute-start.4
  44.4 3.6 %collective-permute-done.other_ref.refs_2_ = bf16[8,128,256]{2,1,0:T(8,128)(2,1)S(1)} collective-permute-done((bf16[8,128,256]{2,1,0:T(8,128)(2,1)}, bf16[8,128,256]{2,1,0:T(8,128)(2,1)S(1)}, u32[]{:S(2)}, u32[]{:S(2)}) %collective-permute-start) | collective-permute-done | bytes 524320 | tf_op jit(solution)/shard_map/ppermute | solution.py:687
  48.0 0.3 pair.3
  48.3 0.5 collective-permute-start.3
  48.9 0.0 collective-permute-done.4.refs_0_.refs_4_
  48.9 0.2 hop.5.refs_2_
  49.1 5.5 %collective-permute-start.6 = (bf16[8,128,128]{2,1,0:T(8,128)(2,1)S(1)}, bf16[8,128,128]{2,1,0:T(8,128)(2,1)S(1)}, u32[]{:S(2)}, u32[]{:S(2)}) collective-permute-start(bf16[8,128,128]{2,1,0:T(8,128)(2,1)S(1)} %hop.5.refs_2_), channel_id=1, source_target_pairs={{0,0},{4,4},{8,8},{12,12},{16,24},{20,28},{24,16},{28,20},{1,1},{5... | collective-permute-start | bytes 786440 | tf_op jit(solution)/shard_map/ppermute | solution.py:673
  54.6 3.0 %collective-permute-done.3.refs_1_.refs_3_ = bf16[8,128,128]{2,1,0:T(8,128)(2,1)S(1)} collective-permute-done((bf16[8,128,128]{2,1,0:T(8,128)(2,1)S(1)}, bf16[8,128,128]{2,1,0:T(8,128)(2,1)S(1)}, u32[]{:S(2)}, u32[]{:S(2)}) %collective-permute-start.3) | collective-permute-done | bytes 262176 | tf_op jit(solution)/shard_map/ppermute | solution.py:673
  57.6 0.2 hop.6.refs_0_
  57.9 0.7 collective-permute-start.5
  58.6 0.1 pad_add_fusion.refs_0_
  58.6 2.2 %copy-done.1 = bf16[4,512,1024]{2,1,0:T(8,128)(2,1)S(1)} copy-done((bf16[4,512,1024]{2,1,0:T(8,128)(2,1)S(1)}, bf16[4,512,1024]{2,1,0:T(8,128)(2,1)}, u32[]{:S(2)}) %copy-start.1) | copy-done | bytes 4194328
  60.8 0.3 stage.2.refs_1_.refs_6_
  61.1 0.0 collective-permute-done.6.refs_5_
  61.1 1.8 %finish.2 = (bf16[128,1024]{1,0:T(8,128)(2,1)S(1)}, bf16[128,1024]{1,0:T(8,128)(2,1)S(1)}, bf16[128,1024]{1,0:T(8,128)(2,1)S(1)}, bf16[128,1024]{1,0:T(8,128)(2,1)S(1)}) custom-call(s32[2]{0:T(128)S(1)} %pad_add_fusion.refs_0_, bf16[4,512,1024]{2,1,0:T(8,128)(2,1)S(1)} %stage.2.refs_1_.refs_6_, ...), custom_call_target="tpu_custom_call" | custom-call | tf_op jit(solution)/shard_map/finish/pallas_call | solution.py:591
  62.9 0.1 collective-permute-start.8
  63.0 1.6 %collective-permute-start.9 = (bf16[128,1024]{1,0:T(8,128)(2,1)S(1)}, bf16[128,1024]{1,0:T(8,128)(2,1)S(1)}, u32[]{:S(2)}, u32[]{:S(2)}) collective-permute-start(bf16[128,1024]{1,0:T(8,128)(2,1)S(1)} %get-tuple-element.50), channel_id=1, source_target_pairs={{0,2},{1,3},{2,0},{3,1},{4,6},{5,7},{6,4},{7,5},{8,10},{9,11},{10,... | collective-permute-start | bytes 786440 | tf_op jit(solution)/shard_map/ppermute | solution.py:722
  64.6 0.0 collective-permute-done.5.refs_0_.refs_4_
  64.6 0.2 hop.7.refs_0_
  64.8 3.0 %collective-permute-start.7 = (bf16[8,128,128]{2,1,0:T(8,128)(2,1)S(1)}, bf16[8,128,128]{2,1,0:T(8,128)(2,1)S(1)}, u32[]{:S(2)}, u32[]{:S(2)}) collective-permute-start(bf16[8,128,128]{2,1,0:T(8,128)(2,1)S(1)} %hop.7.refs_0_), channel_id=1, source_target_pairs={{0,0},{4,4},{8,8},{12,12},{16,24},{20,28},{24,16},{28,20},{1,1},{5... | collective-permute-start | bytes 786440 | tf_op jit(solution)/shard_map/ppermute | solution.py:673
  67.8 0.3 stage.3.refs_4_.refs_1_
  68.1 0.1 collective-permute-start.13
  68.2 0.0 collective-permute-done.8.refs_2_
  68.2 4.0 %collective-permute-done.9.refs_3_ = bf16[128,1024]{1,0:T(8,128)(2,1)S(1)} collective-permute-done((bf16[128,1024]{1,0:T(8,128)(2,1)S(1)}, bf16[128,1024]{1,0:T(8,128)(2,1)S(1)}, u32[]{:S(2)}, u32[]{:S(2)}) %collective-permute-start.9) | collective-permute-done | bytes 262176 | tf_op jit(solution)/shard_map/ppermute | solution.py:722
  72.2 0.9 gather.4
  73.1 2.0 %collective-permute-done.7.refs_5_ = bf16[8,128,128]{2,1,0:T(8,128)(2,1)S(1)} collective-permute-done((bf16[8,128,128]{2,1,0:T(8,128)(2,1)S(1)}, bf16[8,128,128]{2,1,0:T(8,128)(2,1)S(1)}, u32[]{:S(2)}, u32[]{:S(2)}) %collective-permute-start.7) | collective-permute-done | bytes 262176 | tf_op jit(solution)/shard_map/ppermute | solution.py:673
  75.1 1.8 %finish.3 = (bf16[128,1024]{1,0:T(8,128)(2,1)S(1)}, bf16[128,1024]{1,0:T(8,128)(2,1)S(1)}, bf16[128,1024]{1,0:T(8,128)(2,1)S(1)}, bf16[128,1024]{1,0:T(8,128)(2,1)S(1)}) custom-call(s32[2]{0:T(128)S(1)} %pad_add_fusion.refs_0_, bf16[4,512,1024]{2,1,0:T(8,128)(2,1)S(1)} %stage.3.refs_4_.refs_1_, ...), custom_call_target="tpu_custom_call" | custom-call | tf_op jit(solution)/shard_map/finish/pallas_call | solution.py:591
  76.9 0.1 collective-permute-start.11
  76.9 0.6 collective-permute-start.12
  77.5 1.3 %collective-permute-start.10 = (bf16[128,1024]{1,0:T(8,128)(2,1)S(1)}, bf16[128,1024]{1,0:T(8,128)(2,1)S(1)}, u32[]{:S(2)}, u32[]{:S(2)}) collective-permute-start(bf16[128,1024]{1,0:T(8,128)(2,1)S(1)} %get-tuple-element.52), channel_id=1, source_target_pairs={{0,3},{1,2},{2,1},{3,0},{4,7},{5,6},{6,5},{7,4},{8,11},{9,10},{10,... | collective-permute-start | bytes 786440 | tf_op jit(solution)/shard_map/ppermute | solution.py:722
  78.8 0.0 collective-permute-done.13.refs_1_
  78.8 0.7 gather.5
  79.5 0.0 collective-permute-done.11.refs_2_
  79.5 6.6 %collective-permute-done.12.refs_3_ = bf16[128,1024]{1,0:T(8,128)(2,1)S(1)} collective-permute-done((bf16[128,1024]{1,0:T(8,128)(2,1)S(1)}, bf16[128,1024]{1,0:T(8,128)(2,1)S(1)}, u32[]{:S(2)}, u32[]{:S(2)}) %collective-permute-start.12) | collective-permute-done | bytes 262176 | tf_op jit(solution)/shard_map/ppermute | solution.py:722
  86.1 0.9 gather.6
  87.0 3.8 %collective-permute-done.10.refs_1_ = bf16[128,1024]{1,0:T(8,128)(2,1)S(1)} collective-permute-done((bf16[128,1024]{1,0:T(8,128)(2,1)S(1)}, bf16[128,1024]{1,0:T(8,128)(2,1)S(1)}, u32[]{:S(2)}, u32[]{:S(2)}) %collective-permute-start.10) | collective-permute-done | bytes 262176 | tf_op jit(solution)/shard_map/ppermute | solution.py:722
  90.8 1.3 %gather.7 = (bf16[128,8192]{1,0:T(8,128)(2,1)}, f32[8,128]{1,0:T(8,128)}) custom-call(s32[1]{0:T(128)} %bitcast.refs_0_, bf16[128,1024]{1,0:T(8,128)(2,1)S(1)} %collective-permute-done.10.refs_1_, bf16[128,8192]{1,0:T(8,128)(2,1)} %get-tuple-element.60.refs_2_, f32[8,128]{1,0:T(8,128)S(1)} %get-tuple-element.61.refs_3_), custom_call_target="tpu_custom_call", output_to_operand_aliasing={{0}: (2, {})} | custom-call | tf_op jit(solution)/shard_map/gather/pallas_call | solution.py:626
  (7 shorter events, 0.0 us)
Async XLA Ops:
  21.2 13.9 %collective-permute-start.1 = (bf16[8,128,256]{2,1,0:T(8,128)(2,1)}, bf16[8,128,256]{2,1,0:T(8,128)(2,1)S(1)}, u32[]{:S(2)}, u32[]{:S(2)}) collective-permute-start(bf16[8,128,256]{2,1,0:T(8,128)(2,1)} %get-tuple-element.41.own_ref), channel_id=1, source_target_pairs={{0,4},{4,0},{8,12},{12,8},{16,20},{20,16},{24,28},{28,24},{1,5},{5... | collective-permute-start | bytes 1572872 | tf_op jit(solution)/shard_map/ppermute | solution.py:687
  22.7 12.4 %copy-start.3 = (bf16[8,128,256]{2,1,0:T(8,128)(2,1)S(1)}, bf16[8,128,256]{2,1,0:T(8,128)(2,1)}, u32[]{:S(2)}) copy-start(bf16[8,128,256]{2,1,0:T(8,128)(2,1)} %get-tuple-element.41.own_ref) | copy-start | bytes 1572868
  34.4 13.7 %copy-start.2 = (bf16[8,128,256]{2,1,0:T(8,128)(2,1)S(1)}, bf16[8,128,256]{2,1,0:T(8,128)(2,1)}, u32[]{:S(2)}) copy-start(bf16[8,128,256]{2,1,0:T(8,128)(2,1)} %get-tuple-element.40.own_ref) | copy-start | bytes 1572868
  34.4 13.7 %collective-permute-start = (bf16[8,128,256]{2,1,0:T(8,128)(2,1)}, bf16[8,128,256]{2,1,0:T(8,128)(2,1)S(1)}, u32[]{:S(2)}, u32[]{:S(2)}) collective-permute-start(bf16[8,128,256]{2,1,0:T(8,128)(2,1)} %get-tuple-element.40.own_ref), channel_id=1, source_target_pairs={{0,4},{4,0},{8,12},{12,8},{16,20},{20,16},{24,28},{28,24},{1,5},{5... | collective-permute-start | bytes 1572872 | tf_op jit(solution)/shard_map/ppermute | solution.py:687
  35.1 0.7 copy-start.4
  36.1 7.4 %collective-permute-start.2 = (bf16[8,128,128]{2,1,0:T(8,128)(2,1)S(1)}, bf16[8,128,128]{2,1,0:T(8,128)(2,1)S(1)}, u32[]{:S(2)}, u32[]{:S(2)}) collective-permute-start(bf16[8,128,128]{2,1,0:T(8,128)(2,1)S(1)} %get-tuple-element.44.refs_0_), channel_id=1, source_target_pairs={{0,8},{4,12},{8,0},{12,4},{16,24},{20,28},{24,16},{28,20},{1,9},{5... | collective-permute-start | bytes 786440 | tf_op jit(solution)/shard_map/ppermute | solution.py:673
  43.7 5.1 %collective-permute-start.4 = (bf16[8,128,128]{2,1,0:T(8,128)(2,1)S(1)}, bf16[8,128,128]{2,1,0:T(8,128)(2,1)S(1)}, u32[]{:S(2)}, u32[]{:S(2)}) collective-permute-start(bf16[8,128,128]{2,1,0:T(8,128)(2,1)S(1)} %hop.4.rest_0_), channel_id=1, source_target_pairs={{0,0},{4,4},{8,16},{12,20},{16,8},{20,12},{24,24},{28,28},{1,1},{5... | collective-permute-start | bytes 786440 | tf_op jit(solution)/shard_map/ppermute | solution.py:673
  48.3 9.3 %collective-permute-start.3 = (bf16[8,128,128]{2,1,0:T(8,128)(2,1)S(1)}, bf16[8,128,128]{2,1,0:T(8,128)(2,1)S(1)}, u32[]{:S(2)}, u32[]{:S(2)}) collective-permute-start(bf16[8,128,128]{2,1,0:T(8,128)(2,1)S(1)} %get-tuple-element.46.refs_0_), channel_id=1, source_target_pairs={{0,8},{4,12},{8,0},{12,4},{16,24},{20,28},{24,16},{28,20},{1,9},{5... | collective-permute-start | bytes 786440 | tf_op jit(solution)/shard_map/ppermute | solution.py:673
  49.1 12.0 %collective-permute-start.6 = (bf16[8,128,128]{2,1,0:T(8,128)(2,1)S(1)}, bf16[8,128,128]{2,1,0:T(8,128)(2,1)S(1)}, u32[]{:S(2)}, u32[]{:S(2)}) collective-permute-start(bf16[8,128,128]{2,1,0:T(8,128)(2,1)S(1)} %hop.5.refs_2_), channel_id=1, source_target_pairs={{0,0},{4,4},{8,8},{12,12},{16,24},{20,28},{24,16},{28,20},{1,1},{5... | collective-permute-start | bytes 786440 | tf_op jit(solution)/shard_map/ppermute | solution.py:673
  57.9 6.7 %collective-permute-start.5 = (bf16[8,128,128]{2,1,0:T(8,128)(2,1)S(1)}, bf16[8,128,128]{2,1,0:T(8,128)(2,1)S(1)}, u32[]{:S(2)}, u32[]{:S(2)}) collective-permute-start(bf16[8,128,128]{2,1,0:T(8,128)(2,1)S(1)} %hop.6.refs_0_), channel_id=1, source_target_pairs={{0,0},{4,4},{8,16},{12,20},{16,8},{20,12},{24,24},{28,28},{1,1},{5... | collective-permute-start | bytes 786440 | tf_op jit(solution)/shard_map/ppermute | solution.py:673
  58.6 2.2 %copy-start.1 = (bf16[4,512,1024]{2,1,0:T(8,128)(2,1)S(1)}, bf16[4,512,1024]{2,1,0:T(8,128)(2,1)}, u32[]{:S(2)}) copy-start(bf16[4,512,1024]{2,1,0:T(8,128)(2,1)} %get-tuple-element.47.from_ref) | copy-start | bytes 12582916
  61.1 6.7 %copy-start = (bf16[4,512,1024]{2,1,0:T(8,128)(2,1)S(1)}, bf16[4,512,1024]{2,1,0:T(8,128)(2,1)}, u32[]{:S(2)}) copy-start(bf16[4,512,1024]{2,1,0:T(8,128)(2,1)} %get-tuple-element.39.from_ref) | copy-start | bytes 12582916
  62.9 5.3 %collective-permute-start.8 = (bf16[128,1024]{1,0:T(8,128)(2,1)S(1)}, bf16[128,1024]{1,0:T(8,128)(2,1)S(1)}, u32[]{:S(2)}, u32[]{:S(2)}) collective-permute-start(bf16[128,1024]{1,0:T(8,128)(2,1)S(1)} %get-tuple-element.49), channel_id=1, source_target_pairs={{0,1},{1,0},{2,3},{3,2},{4,5},{5,4},{6,7},{7,6},{8,9},{9,8},{10,11... | collective-permute-start | bytes 786440 | tf_op jit(solution)/shard_map/ppermute | solution.py:722
  63.0 9.2 %collective-permute-start.9 = (bf16[128,1024]{1,0:T(8,128)(2,1)S(1)}, bf16[128,1024]{1,0:T(8,128)(2,1)S(1)}, u32[]{:S(2)}, u32[]{:S(2)}) collective-permute-start(bf16[128,1024]{1,0:T(8,128)(2,1)S(1)} %get-tuple-element.50), channel_id=1, source_target_pairs={{0,2},{1,3},{2,0},{3,1},{4,6},{5,7},{6,4},{7,5},{8,10},{9,11},{10,... | collective-permute-start | bytes 786440 | tf_op jit(solution)/shard_map/ppermute | solution.py:722
  64.8 10.3 %collective-permute-start.7 = (bf16[8,128,128]{2,1,0:T(8,128)(2,1)S(1)}, bf16[8,128,128]{2,1,0:T(8,128)(2,1)S(1)}, u32[]{:S(2)}, u32[]{:S(2)}) collective-permute-start(bf16[8,128,128]{2,1,0:T(8,128)(2,1)S(1)} %hop.7.refs_0_), channel_id=1, source_target_pairs={{0,0},{4,4},{8,8},{12,12},{16,24},{20,28},{24,16},{28,20},{1,1},{5... | collective-permute-start | bytes 786440 | tf_op jit(solution)/shard_map/ppermute | solution.py:673
  68.1 10.7 %collective-permute-start.13 = (bf16[128,1024]{1,0:T(8,128)(2,1)S(1)}, bf16[128,1024]{1,0:T(8,128)(2,1)S(1)}, u32[]{:S(2)}, u32[]{:S(2)}) collective-permute-start(bf16[128,1024]{1,0:T(8,128)(2,1)S(1)} %get-tuple-element.56), channel_id=1, source_target_pairs={{0,3},{1,2},{2,1},{3,0},{4,7},{5,6},{6,5},{7,4},{8,11},{9,10},{10,... | collective-permute-start | bytes 786440 | tf_op jit(solution)/shard_map/ppermute | solution.py:722
  76.9 2.7 %collective-permute-start.11 = (bf16[128,1024]{1,0:T(8,128)(2,1)S(1)}, bf16[128,1024]{1,0:T(8,128)(2,1)S(1)}, u32[]{:S(2)}, u32[]{:S(2)}) collective-permute-start(bf16[128,1024]{1,0:T(8,128)(2,1)S(1)} %get-tuple-element.54), channel_id=1, source_target_pairs={{0,1},{1,0},{2,3},{3,2},{4,5},{5,4},{6,7},{7,6},{8,9},{9,8},{10,11... | collective-permute-start | bytes 786440 | tf_op jit(solution)/shard_map/ppermute | solution.py:722
  76.9 9.2 %collective-permute-start.12 = (bf16[128,1024]{1,0:T(8,128)(2,1)S(1)}, bf16[128,1024]{1,0:T(8,128)(2,1)S(1)}, u32[]{:S(2)}, u32[]{:S(2)}) collective-permute-start(bf16[128,1024]{1,0:T(8,128)(2,1)S(1)} %get-tuple-element.55), channel_id=1, source_target_pairs={{0,2},{1,3},{2,0},{3,1},{4,6},{5,7},{6,4},{7,5},{8,10},{9,11},{10,... | collective-permute-start | bytes 786440 | tf_op jit(solution)/shard_map/ppermute | solution.py:722
  77.5 13.3 %collective-permute-start.10 = (bf16[128,1024]{1,0:T(8,128)(2,1)S(1)}, bf16[128,1024]{1,0:T(8,128)(2,1)S(1)}, u32[]{:S(2)}, u32[]{:S(2)}) collective-permute-start(bf16[128,1024]{1,0:T(8,128)(2,1)S(1)} %get-tuple-element.52), channel_id=1, source_target_pairs={{0,3},{1,2},{2,1},{3,0},{4,7},{5,6},{6,5},{7,4},{8,11},{9,10},{10,... | collective-permute-start | bytes 786440 | tf_op jit(solution)/shard_map/ppermute | solution.py:722
